TPU v7x, 32 devices: a whole 2x2x4 slice. The times are simulated.
32 devices in a mesh: ctx: 16 (over z, y, core), ch: 2 (over x).
Axes of the slice: x: 2, y: 2, z: 4, core: 2. Of those that a mesh axis runs over, the one named last changes fastest.
Arguments:
- cotangent: bfloat16 [2048, 4096], P('ctx', 'ch'), may hold values from -6 to 6
- out_weight: bfloat16 [4096, 4096], P('ch', 'ctx'), may hold values from -0.09375 to 0.09375
- gate_value: float32 [2048, 4096], P('ctx', 'ch'), may hold values from -6 to 6
- conv_output: float32 [2048, 4096], P('ctx', 'ch'), may hold values from -6 to 6
- conv_input: float32 [2048, 4096], P('ctx', 'ch'), may hold values from -6 to 6
- filters: float32 [256, 2048], P('ch'), may hold values from -1 to 1
Outputs:
- input_grad: float32 [2048, 4096], P('ctx', 'ch')
- gate_grad: float32 [2048, 4096], P('ctx', 'ch')
- filter_grad: float32 [256, 2048], P('ch', 'ctx')
All inputs are finite; a program needn't handle non-finite values.
Results may differ from a plain program's by a relative error of at most 0.0003.
Values may be sent and summed in bfloat16 or wider, within the bound.
No kernel may reach another device: no remote copies, remote signals or barrier semaphores. Data moves between devices by JAX's collectives and lax.ppermute only.
A program may use at most 128 MiB of HBM per device.

v0:
```python
import math

import jax
import jax.numpy as jnp
from jax import lax
from jax.sharding import PartitionSpec as P

exact_mode = lax.Precision.HIGHEST


def spectral_tables(tok_rows):
    length = 2 * tok_rows
    frequency = jnp.arange(length, dtype=jnp.int32)
    angles = (frequency[:, None] * frequency[None, :] % length).astype(jnp.float32) * (
        2.0 * math.pi / length
    )
    cosine = jnp.cos(angles)
    sine_part = jnp.sin(angles)
    forward = jnp.concatenate([cosine, -sine_part], axis=0)
    inverse = jnp.concatenate([cosine, -sine_part], axis=1) / length
    return (forward, inverse)


def spectrum_step(
    spectra, shard_block, offset, forward_rows, filter_spectra, input_spectrum, groups
):
    running, lag_spectra = spectra
    freq_count = forward_rows.shape[0] // 2
    channels = shard_block.shape[1]
    per_group = channels // groups
    block_spectrum = jnp.dot(forward_rows, shard_block, precision=exact_mode)
    filter_block = lax.dynamic_index_in_dim(filter_spectra, offset, 0, keepdims=False)
    block_real = block_spectrum[:freq_count].reshape(freq_count, groups, per_group)
    block_imag = block_spectrum[freq_count:].reshape(freq_count, groups, per_group)
    filter_real = filter_block[:freq_count][:, :, None]
    filter_imag = filter_block[freq_count:][:, :, None]
    input_real = input_spectrum[:freq_count].reshape(freq_count, groups, per_group)
    input_imag = input_spectrum[freq_count:].reshape(freq_count, groups, per_group)
    prod_real = block_real * filter_real + block_imag * filter_imag
    prod_imag = block_imag * filter_real - block_real * filter_imag
    running = running + jnp.concatenate([prod_real, prod_imag], axis=0).reshape(
        2 * freq_count, channels
    )
    cross_real = jnp.sum(block_real * input_real + block_imag * input_imag, axis=2)
    cross_imag = jnp.sum(block_imag * input_real - block_real * input_imag, axis=2)
    cross_spectrum = jnp.concatenate([cross_real, cross_imag], axis=0)
    lag_spectra = lax.dynamic_update_index_in_dim(lag_spectra, cross_spectrum, offset, 0)
    return (running, lag_spectra)


def body(cotangent, out_weight, gate_value, conv_output, conv_input, filters):
    tok_rows, channels = gate_value.shape
    groups, lag_count = filters.shape
    ahead_blocks = lag_count // tok_rows
    spectrum_len = 2 * tok_rows
    full_cotangent = lax.all_gather(cotangent, "ch", axis=1, tiled=True)
    grad_out = lax.dot_general(
        full_cotangent,
        lax.all_gather(out_weight, "ctx", axis=1, tiled=True),
        (((1,), (1,)), ((), ())),
        preferred_element_type=jnp.float32,
    )
    gate_grad = grad_out * conv_output
    seq_grad = grad_out * gate_value
    forward_full, inverse_full = spectral_tables(tok_rows)
    forward_rows = forward_full[:, :tok_rows]
    blocks = filters.reshape(groups, ahead_blocks, tok_rows)
    border = jnp.zeros((groups, 1, tok_rows), jnp.float32)
    padded = jnp.concatenate([border, blocks, border], axis=1)
    segments = jnp.concatenate([padded[:, 1:], padded[:, :-1]], axis=2)
    filter_spectra = jnp.einsum("gdn,fn->dfg", segments, forward_full, precision=exact_mode)
    input_spectrum = jnp.dot(forward_rows, conv_input, precision=exact_mode)

    def absorb(spectra, shard_block, offset):
        return spectrum_step(
            spectra, shard_block, offset, forward_rows, filter_spectra, input_spectrum, groups
        )

    spectra = (
        jnp.zeros((2 * spectrum_len, channels), jnp.float32),
        jnp.zeros((ahead_blocks + 1, 2 * spectrum_len, groups), jnp.float32),
    )
    own_index = lax.axis_index("ctx")
    inner_state = spectra
    piece_rows = lax.all_gather(seq_grad, "ctx", axis=0, tiled=True)
    shard_count = piece_rows.shape[0] // tok_rows
    shards = piece_rows.reshape(shard_count, tok_rows, channels)

    def absorb_one(carried, element):
        shard_block, number = element
        offset = number - own_index
        inside = (offset >= 0) & (offset <= ahead_blocks)
        clipped = jnp.clip(offset, 0, ahead_blocks)
        return (
            lax.cond(
                inside,
                lambda current: absorb(current, shard_block, clipped),
                lambda current: current,
                carried,
            ),
            None,
        )

    inner_state, unused = lax.scan(
        absorb_one, inner_state, (shards, jnp.arange(shard_count, dtype=jnp.int32))
    )
    spectra = inner_state
    running, lag_spectra = spectra
    input_grad = jnp.dot(inverse_full[:tok_rows], running, precision=exact_mode)
    lag_terms = jnp.einsum("mf,dfg->dmg", inverse_full, lag_spectra, precision=exact_mode)
    joined = lag_terms[:ahead_blocks, :tok_rows] + lag_terms[1:, tok_rows:]
    tokens = tok_rows * lax.axis_size("ctx")
    per_group = channels // groups
    partial_sums = joined.transpose(2, 0, 1).reshape(groups, lag_count) * (
        1.0 / math.sqrt(per_group * tokens)
    )
    filter_grad = lax.psum_scatter(partial_sums, "ctx", scatter_dimension=1, tiled=True)
    return (input_grad, gate_grad, filter_grad)


def solution(mesh):
    return jax.shard_map(
        body,
        mesh=mesh,
        in_specs=(
            P("ctx", "ch"),
            P("ch", "ctx"),
            P("ctx", "ch"),
            P("ctx", "ch"),
            P("ctx", "ch"),
            P("ch", None),
        ),
        out_specs=(P("ctx", "ch"), P("ctx", "ch"), P("ch", "ctx")),
        check_vma=False,
    )
```

profile of v0, /device:TPU:0, one launch (start us, length us, event | category | flops | bytes accessed | tf_op | source)
XLA Modules:
  0.0 614.1 jit_solution(14471508110479238447)
XLA Ops:
  8.7 24.9 %all-gather.4.cloned.1.call-done = bf16[128,4096]{1,0:T(8,128)(2,1)} async-done(((bf16[128,2048]{1,0:T(8,128)(2,1)}), bf16[128,4096]{1,0:T(8,128)(2,1)}) %all-gather.4.cloned.1.call-update) | async-done | bytes 1048592 | tf_op jit(solution)/shard_map/all_gather | solution.py:56
  33.6 132.5 %all-gather.6.cloned.1.call-done = bf16[2048,4096]{1,0:T(8,128)(2,1)} async-done(((bf16[2048,256]{1,0:T(8,128)(2,1)}), bf16[2048,4096]{1,0:T(8,128)(2,1)}) %all-gather.6.cloned.1.call-update) | async-done | bytes 16777232 | tf_op jit(solution)/shard_map/all_gather | solution.py:59
  166.1 13.6 %fusion.31 = (f32[128,2048]{1,0:T(8,128)}, f32[128,2048]{1,0:T(8,128)}) fusion(f32[128,2048]{1,0:T(8,128)} %param.13, f32[128,2048]{1,0:T(8,128)} %param.12, bf16[128,4096]{1,0:T(8,128)(2,1)} %all-gather.4.cloned.1.call-done, bf16[2048,4096]{1,0:T(8,128)(2,1)} %all-gather.6.cloned.1.call-done), kind=kOutput, calls=%fused_computation.56 | convolution fusion | flops 2148007936 | bytes 22020096 | tf_op jit(solution)/shard_map/dot_general | solution.py:57
  181.5 5.8 fusion.10
  187.3 6.0 copy.23
  193.3 5.1 fusion.32
  198.4 106.5 %all-gather.8.cloned.1.call-done = f32[2048,2048]{1,0:T(8,128)} async-done(((f32[128,2048]{1,0:T(8,128)}), f32[2048,2048]{1,0:T(8,128)}) %all-gather.8.cloned.1.call-update) | async-done | bytes 16777232 | tf_op jit(solution)/shard_map/all_gather | solution.py:85
  305.0 2.5 broadcast_in_dim.16
  307.5 2.7 broadcast_in_dim.17
  310.2 234.0 %while.12 = (s32[]{:T(128)}, f32[512,2048]{0,1:T(8,128)}, f32[17,512,128]{1,2,0:T(8,128)}, s32[16]{0:T(128)S(1)}, s32[]{:T(128)}, /*index=5*/f32[16,128,2048]{2,...) while((s32[]{:T(128)}, f32[512,2048]{0,1:T(8,128)}, ...), condition=%wide.region_5.6_spmd, body=%wide.region_0.5_spmd.sunk | while | flops 1620049920 | bytes 86770584 | solution.py:104
  311.4 13.3 %conditional.2 = ((f32[512,2048]{0,1:T(8,128)}, f32[17,512,128]{1,2,0:T(8,128)})) conditional(s32[]{:T(128)} %convert_element_type.21, (f32[512,2048]{0,1:T(8,128)}, f32[17,512,128]{1,2,0:T(8,128)}) %tuple.45, (f32[16,128,2048]{2,1,0:T(8,128)}, s32[]{:T(128)}, f32[512,128]{1,0:T(8,128)S(1)}, s32[]{:T(128)}, f32[17,512,128]{1,2,0:T(8,128)}, ...), branch_computations={%region_1.1_spmd, %region_2.4_spmd} | conditional | flops 1620049920 | bytes 86770328 | solution.py:95
  312.6 4.9 convolution_bitcast_fusion
  319.2 1.7 copy-done.2
  322.1 2.0 copy-done.3
  326.0 13.4 %conditional.2 = ((f32[512,2048]{0,1:T(8,128)}, f32[17,512,128]{1,2,0:T(8,128)})) conditional(s32[]{:T(128)} %convert_element_type.21, (f32[512,2048]{0,1:T(8,128)}, f32[17,512,128]{1,2,0:T(8,128)}) %tuple.45, (f32[16,128,2048]{2,1,0:T(8,128)}, s32[]{:T(128)}, f32[512,128]{1,0:T(8,128)S(1)}, s32[]{:T(128)}, f32[17,512,128]{1,2,0:T(8,128)}, ...), branch_computations={%region_1.1_spmd, %region_2.4_spmd} | conditional | flops 1620049920 | bytes 86770328 | solution.py:95
  327.2 4.9 convolution_bitcast_fusion
  333.9 1.7 copy-done.2
  336.7 2.0 copy-done.3
  340.6 13.4 %conditional.2 = ((f32[512,2048]{0,1:T(8,128)}, f32[17,512,128]{1,2,0:T(8,128)})) conditional(s32[]{:T(128)} %convert_element_type.21, (f32[512,2048]{0,1:T(8,128)}, f32[17,512,128]{1,2,0:T(8,128)}) %tuple.45, (f32[16,128,2048]{2,1,0:T(8,128)}, s32[]{:T(128)}, f32[512,128]{1,0:T(8,128)S(1)}, s32[]{:T(128)}, f32[17,512,128]{1,2,0:T(8,128)}, ...), branch_computations={%region_1.1_spmd, %region_2.4_spmd} | conditional | flops 1620049920 | bytes 86770328 | solution.py:95
  341.8 4.9 convolution_bitcast_fusion
  351.3 2.0 copy-done.3
  355.3 13.4 %conditional.2 = ((f32[512,2048]{0,1:T(8,128)}, f32[17,512,128]{1,2,0:T(8,128)})) conditional(s32[]{:T(128)} %convert_element_type.21, (f32[512,2048]{0,1:T(8,128)}, f32[17,512,128]{1,2,0:T(8,128)}) %tuple.45, (f32[16,128,2048]{2,1,0:T(8,128)}, s32[]{:T(128)}, f32[512,128]{1,0:T(8,128)S(1)}, s32[]{:T(128)}, f32[17,512,128]{1,2,0:T(8,128)}, ...), branch_computations={%region_1.1_spmd, %region_2.4_spmd} | conditional | flops 1620049920 | bytes 86770328 | solution.py:95
  356.4 4.9 convolution_bitcast_fusion
  365.9 2.0 copy-done.3
  369.9 13.4 %conditional.2 = ((f32[512,2048]{0,1:T(8,128)}, f32[17,512,128]{1,2,0:T(8,128)})) conditional(s32[]{:T(128)} %convert_element_type.21, (f32[512,2048]{0,1:T(8,128)}, f32[17,512,128]{1,2,0:T(8,128)}) %tuple.45, (f32[16,128,2048]{2,1,0:T(8,128)}, s32[]{:T(128)}, f32[512,128]{1,0:T(8,128)S(1)}, s32[]{:T(128)}, f32[17,512,128]{1,2,0:T(8,128)}, ...), branch_computations={%region_1.1_spmd, %region_2.4_spmd} | conditional | flops 1620049920 | bytes 86770328 | solution.py:95
  371.1 4.9 convolution_bitcast_fusion
  380.6 2.0 copy-done.3
  384.5 13.4 %conditional.2 = ((f32[512,2048]{0,1:T(8,128)}, f32[17,512,128]{1,2,0:T(8,128)})) conditional(s32[]{:T(128)} %convert_element_type.21, (f32[512,2048]{0,1:T(8,128)}, f32[17,512,128]{1,2,0:T(8,128)}) %tuple.45, (f32[16,128,2048]{2,1,0:T(8,128)}, s32[]{:T(128)}, f32[512,128]{1,0:T(8,128)S(1)}, s32[]{:T(128)}, f32[17,512,128]{1,2,0:T(8,128)}, ...), branch_computations={%region_1.1_spmd, %region_2.4_spmd} | conditional | flops 1620049920 | bytes 86770328 | solution.py:95
  385.7 4.9 convolution_bitcast_fusion
  395.2 2.0 copy-done.3
  399.2 13.4 %conditional.2 = ((f32[512,2048]{0,1:T(8,128)}, f32[17,512,128]{1,2,0:T(8,128)})) conditional(s32[]{:T(128)} %convert_element_type.21, (f32[512,2048]{0,1:T(8,128)}, f32[17,512,128]{1,2,0:T(8,128)}) %tuple.45, (f32[16,128,2048]{2,1,0:T(8,128)}, s32[]{:T(128)}, f32[512,128]{1,0:T(8,128)S(1)}, s32[]{:T(128)}, f32[17,512,128]{1,2,0:T(8,128)}, ...), branch_computations={%region_1.1_spmd, %region_2.4_spmd} | conditional | flops 1620049920 | bytes 86770328 | solution.py:95
  400.3 4.9 convolution_bitcast_fusion
  409.8 2.0 copy-done.3
  413.8 13.4 %conditional.2 = ((f32[512,2048]{0,1:T(8,128)}, f32[17,512,128]{1,2,0:T(8,128)})) conditional(s32[]{:T(128)} %convert_element_type.21, (f32[512,2048]{0,1:T(8,128)}, f32[17,512,128]{1,2,0:T(8,128)}) %tuple.45, (f32[16,128,2048]{2,1,0:T(8,128)}, s32[]{:T(128)}, f32[512,128]{1,0:T(8,128)S(1)}, s32[]{:T(128)}, f32[17,512,128]{1,2,0:T(8,128)}, ...), branch_computations={%region_1.1_spmd, %region_2.4_spmd} | conditional | flops 1620049920 | bytes 86770328 | solution.py:95
  415.0 4.9 convolution_bitcast_fusion
  424.4 2.0 copy-done.3
  428.4 13.4 %conditional.2 = ((f32[512,2048]{0,1:T(8,128)}, f32[17,512,128]{1,2,0:T(8,128)})) conditional(s32[]{:T(128)} %convert_element_type.21, (f32[512,2048]{0,1:T(8,128)}, f32[17,512,128]{1,2,0:T(8,128)}) %tuple.45, (f32[16,128,2048]{2,1,0:T(8,128)}, s32[]{:T(128)}, f32[512,128]{1,0:T(8,128)S(1)}, s32[]{:T(128)}, f32[17,512,128]{1,2,0:T(8,128)}, ...), branch_computations={%region_1.1_spmd, %region_2.4_spmd} | conditional | flops 1620049920 | bytes 86770328 | solution.py:95
  429.6 4.9 convolution_bitcast_fusion
  439.1 2.0 copy-done.3
  443.1 13.4 %conditional.2 = ((f32[512,2048]{0,1:T(8,128)}, f32[17,512,128]{1,2,0:T(8,128)})) conditional(s32[]{:T(128)} %convert_element_type.21, (f32[512,2048]{0,1:T(8,128)}, f32[17,512,128]{1,2,0:T(8,128)}) %tuple.45, (f32[16,128,2048]{2,1,0:T(8,128)}, s32[]{:T(128)}, f32[512,128]{1,0:T(8,128)S(1)}, s32[]{:T(128)}, f32[17,512,128]{1,2,0:T(8,128)}, ...), branch_computations={%region_1.1_spmd, %region_2.4_spmd} | conditional | flops 1620049920 | bytes 86770328 | solution.py:95
  444.2 4.9 convolution_bitcast_fusion
  453.7 2.0 copy-done.3
  457.7 13.3 %conditional.2 = ((f32[512,2048]{0,1:T(8,128)}, f32[17,512,128]{1,2,0:T(8,128)})) conditional(s32[]{:T(128)} %convert_element_type.21, (f32[512,2048]{0,1:T(8,128)}, f32[17,512,128]{1,2,0:T(8,128)}) %tuple.45, (f32[16,128,2048]{2,1,0:T(8,128)}, s32[]{:T(128)}, f32[512,128]{1,0:T(8,128)S(1)}, s32[]{:T(128)}, f32[17,512,128]{1,2,0:T(8,128)}, ...), branch_computations={%region_1.1_spmd, %region_2.4_spmd} | conditional | flops 1620049920 | bytes 86770328 | solution.py:95
  458.9 4.9 convolution_bitcast_fusion
  468.3 2.0 copy-done.3
  472.3 13.3 %conditional.2 = ((f32[512,2048]{0,1:T(8,128)}, f32[17,512,128]{1,2,0:T(8,128)})) conditional(s32[]{:T(128)} %convert_element_type.21, (f32[512,2048]{0,1:T(8,128)}, f32[17,512,128]{1,2,0:T(8,128)}) %tuple.45, (f32[16,128,2048]{2,1,0:T(8,128)}, s32[]{:T(128)}, f32[512,128]{1,0:T(8,128)S(1)}, s32[]{:T(128)}, f32[17,512,128]{1,2,0:T(8,128)}, ...), branch_computations={%region_1.1_spmd, %region_2.4_spmd} | conditional | flops 1620049920 | bytes 86770328 | solution.py:95
  473.5 4.9 convolution_bitcast_fusion
  483.0 2.0 copy-done.3
  486.9 13.4 %conditional.2 = ((f32[512,2048]{0,1:T(8,128)}, f32[17,512,128]{1,2,0:T(8,128)})) conditional(s32[]{:T(128)} %convert_element_type.21, (f32[512,2048]{0,1:T(8,128)}, f32[17,512,128]{1,2,0:T(8,128)}) %tuple.45, (f32[16,128,2048]{2,1,0:T(8,128)}, s32[]{:T(128)}, f32[512,128]{1,0:T(8,128)S(1)}, s32[]{:T(128)}, f32[17,512,128]{1,2,0:T(8,128)}, ...), branch_computations={%region_1.1_spmd, %region_2.4_spmd} | conditional | flops 1620049920 | bytes 86770328 | solution.py:95
  488.1 4.9 convolution_bitcast_fusion
  497.6 2.0 copy-done.3
  501.5 13.4 %conditional.2 = ((f32[512,2048]{0,1:T(8,128)}, f32[17,512,128]{1,2,0:T(8,128)})) conditional(s32[]{:T(128)} %convert_element_type.21, (f32[512,2048]{0,1:T(8,128)}, f32[17,512,128]{1,2,0:T(8,128)}) %tuple.45, (f32[16,128,2048]{2,1,0:T(8,128)}, s32[]{:T(128)}, f32[512,128]{1,0:T(8,128)S(1)}, s32[]{:T(128)}, f32[17,512,128]{1,2,0:T(8,128)}, ...), branch_computations={%region_1.1_spmd, %region_2.4_spmd} | conditional | flops 1620049920 | bytes 86770328 | solution.py:95
  502.7 4.9 convolution_bitcast_fusion
  512.2 2.0 copy-done.3
  516.2 13.4 %conditional.2 = ((f32[512,2048]{0,1:T(8,128)}, f32[17,512,128]{1,2,0:T(8,128)})) conditional(s32[]{:T(128)} %convert_element_type.21, (f32[512,2048]{0,1:T(8,128)}, f32[17,512,128]{1,2,0:T(8,128)}) %tuple.45, (f32[16,128,2048]{2,1,0:T(8,128)}, s32[]{:T(128)}, f32[512,128]{1,0:T(8,128)S(1)}, s32[]{:T(128)}, f32[17,512,128]{1,2,0:T(8,128)}, ...), branch_computations={%region_1.1_spmd, %region_2.4_spmd} | conditional | flops 1620049920 | bytes 86770328 | solution.py:95
  517.4 4.9 convolution_bitcast_fusion
  524.0 1.7 copy-done.2
  526.8 2.0 copy-done.3
  530.8 13.4 %conditional.2 = ((f32[512,2048]{0,1:T(8,128)}, f32[17,512,128]{1,2,0:T(8,128)})) conditional(s32[]{:T(128)} %convert_element_type.21, (f32[512,2048]{0,1:T(8,128)}, f32[17,512,128]{1,2,0:T(8,128)}) %tuple.45, (f32[16,128,2048]{2,1,0:T(8,128)}, s32[]{:T(128)}, f32[512,128]{1,0:T(8,128)S(1)}, s32[]{:T(128)}, f32[17,512,128]{1,2,0:T(8,128)}, ...), branch_computations={%region_1.1_spmd, %region_2.4_spmd} | conditional | flops 1620049920 | bytes 86770328 | solution.py:95
  532.0 4.9 convolution_bitcast_fusion
  541.5 2.0 copy-done.3
  544.2 5.6 convolution_bitcast_fusion.1
  551.3 7.5 %fusion.22 = f32[128,2048]{1,0:T(8,128)} fusion(f32[512,2048]{0,1:T(8,128)} %get-tuple-element.108, f32[256,512]{1,0:T(8,128)S(1)} %maximum_multiply_fusion), kind=kOutput, calls=%fused_computation.46 | convolution fusion | flops 1610612736 | bytes 5505024 | tf_op jit(solution)/shard_map/dot_general | solution.py:109
  558.8 47.2 %reduce-scatter.2.cloned.1.call-done = f32[128,128]{0,1:T(8,128)} async-done(((f32[128,2048]{0,1:T(8,128)}), f32[128,128]{0,1:T(8,128)}) %reduce-scatter.2.cloned.1.call-update) | async-done | bytes 65552 | tf_op jit(solution)/shard_map/reduce_scatter | solution.py:117
  (196 shorter events, 113.7 us)
Async XLA Ops:
  7.2 186.2 %copy-start = (f32[128,2048]{1,0:T(8,128)S(1)}, f32[128,2048]{1,0:T(8,128)}, u32[]{:S(2)}) copy-start(f32[128,2048]{1,0:T(8,128)} %param.14) | copy-start | bytes 3145732
  7.2 26.4 %all-gather.4.cloned.1.call-start = ((), (), s32[]{:S(2)}) async-start(), calls=%async_computation.1 | async-start | bytes 1572864 | tf_op jit(solution)/shard_map/all_gather | solution.py:56
  7.9 158.2 %all-gather.6.cloned.1.call-start = ((), (), s32[]{:S(2)}) async-start(), calls=%async_computation.2 | async-start | bytes 17825792 | tf_op jit(solution)/shard_map/all_gather | solution.py:59
  8.7 171.1 %copy-start.5 = (f32[128,2048]{1,0:T(8,128)S(1)}, f32[128,2048]{1,0:T(8,128)}, u32[]{:S(2)}) copy-start(f32[128,2048]{1,0:T(8,128)} %param.15) | copy-start | bytes 3145732
  8.7 296.3 %all-gather.8.cloned.1.call-start = ((), (), s32[]{:S(2)}) async-start(), calls=%async_computation.3 | async-start | bytes 17825792 | tf_op jit(solution)/shard_map/all_gather | solution.py:85
  179.7 426.3 %reduce-scatter.2.cloned.1.call-start = ((), (), s32[]{:S(2)}) async-start(), calls=%async_computation.4 | async-start | bytes 1114112 | tf_op jit(solution)/shard_map/reduce_scatter | solution.py:117
  311.4 6.1 copy-start.4
  318.8 2.2 copy-start.2
  322.1 2.0 copy-start.3
  326.0 6.1 copy-start.4
  333.4 2.2 copy-start.2
  336.7 2.0 copy-start.3
  340.7 6.1 copy-start.4
  348.0 2.2 copy-start.2
  351.3 2.0 copy-start.3
  355.3 6.1 copy-start.4
  362.6 2.2 copy-start.2
  365.9 2.0 copy-start.3
  369.9 6.1 copy-start.4
  377.3 2.2 copy-start.2
  380.6 2.0 copy-start.3
  384.6 6.1 copy-start.4
  391.9 2.2 copy-start.2
  395.2 2.0 copy-start.3
  399.2 6.1 copy-start.4
  406.5 2.2 copy-start.2
  409.8 2.0 copy-start.3
  413.8 6.1 copy-start.4
  421.2 2.2 copy-start.2
  424.4 2.0 copy-start.3
  428.4 6.1 copy-start.4
  435.8 2.2 copy-start.2
  439.1 2.0 copy-start.3
  443.1 6.1 copy-start.4
  450.4 2.2 copy-start.2
  453.7 2.0 copy-start.3
  457.7 6.1 copy-start.4
  465.1 2.2 copy-start.2
  468.3 2.0 copy-start.3
  472.3 6.1 copy-start.4
  479.7 2.2 copy-start.2
  482.9 2.0 copy-start.3
  486.9 6.1 copy-start.4
  494.3 2.2 copy-start.2
  497.6 2.0 copy-start.3
  501.6 6.1 copy-start.4
  508.9 2.2 copy-start.2
  512.2 2.0 copy-start.3
  516.2 6.1 copy-start.4
  523.6 2.2 copy-start.2
  526.8 2.0 copy-start.3
  530.8 6.1 copy-start.4
  538.2 2.2 copy-start.2
  541.5 2.0 copy-start.3
  549.9 57.7 %copy-start.1 = (f32[128,2048]{1,0:T(8,128)S(1)}, f32[128,2048]{1,0:T(8,128)}, u32[]{:S(2)}) copy-start(f32[128,2048]{1,0:T(8,128)} %param.14) | copy-start | bytes 3145732
Sparse Core Ops, SparseCore 0:
  9.6 23.9 all-gather.3
  35.7 130.3 all-gather.5
  179.9 125.0 all-gather.7
  551.4 54.5 reduce-scatter.1
where the time goes:
time: 615 us; the launch traced here: 614 us
  waiting for transfers between devices  313 us (51%)
  matrix products  116 us (19%)
  local copies, waits for them, and re-layouts  103 us (17%)
  other arithmetic  57.4 us (9%)
  between operations  13.9 us (2%)
  loops' own time  11.3 us (2%)
    all_gather x1, waiting for transfers between devices, body(): lax.all_gather(out_weight, 'ctx', axis=1, tiled=True)  133 us
    all_gather x1, waiting for transfers between devices, body(): piece_rows = lax.all_gather(seq_grad, 'ctx', axis=0, tiled=True)  107 us
    dot_general x16, matrix products, spectrum_step(): block_spectrum = jnp.dot(forward_rows, shard_block, precision=exact_mode)  78.7 us
    cond x96, local copies, waits for them, and re-layouts  59.4 us
    reduce_scatter x1, waiting for transfers between devices, body(): lax.psum_scatter(partial_sums, 'ctx', scatter_dimension=1, tiled=True)  47.2 us
    all_gather x1, waiting for transfers between devices, body(): full_cotangent = lax.all_gather(cotangent, 'ch', axis=1, tiled=True)  24.9 us
    reduce_sum x16, other arithmetic, spectrum_step(): jnp.sum(block_real * input_real + block_imag * input_imag, axis=2)  20.1 us
    mul x16, local copies, waits for them, and re-layouts, spectrum_step(): prod_real = block_real * filter_real + block_imag * filter_imag  18.3 us
  transfers between devices with their start and end apart: 4, of which 4 were waited for; matrix products, arithmetic and copies ran while one was open for 4% of the time, Pallas kernels for 0%

commit v1 on v0

v1 whole, which is shorter than its diff:
```python
import functools
import math

import jax
import jax.numpy as jnp
from jax import lax
from jax.experimental import pallas as pl
from jax.experimental.pallas import tpu as pltpu
from jax.sharding import PartitionSpec as P

LANES = 128
ROW_TILE = 16
VMEM = pl.BlockSpec(memory_space=pltpu.VMEM)


def split(value):
    high = value.astype(jnp.bfloat16)
    return high, (value - high.astype(jnp.float32)).astype(jnp.bfloat16)


def toeplitz_kernel(filter_ref, out_ref):
    tok = out_ref.shape[1] // 2
    rows = jnp.broadcast_to(filter_ref[0], (tok, filter_ref.shape[2]))
    high, low = split(pltpu.roll(rows, 0, 1, stride=1, stride_axis=0))
    out_ref[0, :tok, :] = high
    out_ref[0, tok:, :] = low


def toeplitz(filters, tok):
    groups, lags = filters.shape
    width = lags + tok
    padded = jnp.pad(filters, ((0, 0), (0, tok)))[:, None, :]
    return pl.pallas_call(
        toeplitz_kernel,
        grid=(groups,),
        in_specs=[pl.BlockSpec((1, 1, width), lambda g: (g, 0, 0))],
        out_specs=pl.BlockSpec((1, 2 * tok, width), lambda g: (g, 0, 0)),
        out_shape=jax.ShapeDtypeStruct((groups, 2 * tok, width), jnp.bfloat16),
        cost_estimate=pl.CostEstimate(
            flops=groups * tok * width * 4, bytes_accessed=groups * width * (4 + 4 * tok), transcendentals=0
        ),
        name="toeplitz",
    )(padded)


def conv_kernel(
    scale, lag_own, s_ref, x_ref, t_ref, out_ref, s_hi, s_lo, x_hi, x_lo, total, grads, cross, lag_sums
):
    blocks, tok, _ = s_ref.shape
    groups, rows, _ = x_hi.shape
    per = rows // blocks
    width = t_ref.shape[2]
    steps = width // tok
    used = min(steps, blocks)
    s_hi[:, rows:, :] = jnp.zeros_like(s_hi[:, rows:, :])
    s_lo[:, rows:, :] = jnp.zeros_like(s_lo[:, rows:, :])

    @pl.loop(0, blocks)
    def _(a):
        at = pl.ds(pl.multiple_of(a * per, per), per)
        for source, high_ref, low_ref in ((s_ref, s_hi, s_lo), (x_ref, x_hi, x_lo)):
            high, low = split(source[a].T[: groups * per])
            high_ref[:, at, :] = high.reshape(groups, per, tok)
            low_ref[:, at, :] = low.reshape(groups, per, tok)

    @pl.loop(0, groups)
    def _(g):
        for d in range(0, used, 2):
            first, second = d * per, (d + 1) * per
            count = rows - first
            left = jnp.concatenate(
                [
                    jnp.concatenate([ref[g, first : first + count, :], ref[g, second : second + count, :]], axis=1)
                    for ref in (s_hi, s_lo)
                ],
                axis=0,
            )
            if d + 2 <= steps:
                right = t_ref[g, :, d * tok : (d + 2) * tok]
            else:
                right = jnp.concatenate(
                    [t_ref[g, :, d * tok :], jnp.zeros((2 * tok, tok), jnp.bfloat16)], axis=1
                )
            product = lax.dot_general(
                left, right, (((1,), (1,)), ((), ())), preferred_element_type=jnp.float32
            )
            term = product[:count, :tok] + (product[:count, tok:] + product[count:, :tok])
            if d == 0:
                total[...] = term
            else:
                total[:count, :] += term
        grads[g] = total[...]

        left = jnp.concatenate([x_hi[g], x_lo[g]], axis=1).T
        for d in range(used):
            here = pl.ds(d * per, rows)
            right = jnp.concatenate([s_hi[g, here, :], s_lo[g, here, :]], axis=1)
            product = jnp.dot(left, right, preferred_element_type=jnp.float32)
            cross[:, d * tok : (d + 1) * tok] = product[:tok, :tok] + (product[:tok, tok:] + product[tok:, :tok])
        if used < steps:
            cross[:, used * tok :] = jnp.zeros_like(cross[:, used * tok :])
        skewed = pltpu.roll(cross[...], width - tok + 1, 1, stride=1, stride_axis=0)
        lag_sums[pl.ds(g, 1), :] = jnp.sum(skewed, axis=0, keepdims=True)[:, : width - tok] * scale

    for a in range(blocks):
        if out_ref.shape[2] > groups * per:
            out_ref[a, :tok, :] = jnp.zeros_like(out_ref[a, :tok, :])
        out_ref[a, :tok, : groups * per] = grads[:, a * per : (a + 1) * per, :].reshape(groups * per, tok).T
        out_ref[a, tok:, :] = jnp.zeros_like(out_ref[a, tok:, :])
        out_ref[a, tok : tok + groups, :lag_own] = lag_sums[:, a * lag_own : (a + 1) * lag_own]


def convolve(seq_blocks, input_blocks, moved, lag_own, scale):
    blocks, tok, own = seq_blocks.shape
    groups, _, width = moved.shape
    channels = own // groups
    per = -(-channels // ROW_TILE) * ROW_TILE
    if groups * per != LANES or channels != per:
        wide = groups * per
        lanes = -(-wide // LANES) * LANES

        def widen(v):
            v = v.reshape(blocks, tok, groups, channels)
            v = jnp.pad(v, ((0, 0), (0, 0), (0, 0), (0, per - channels))).reshape(blocks, tok, wide)
            return jnp.pad(v, ((0, 0), (0, 0), (0, lanes - wide)))

        seq_blocks, input_blocks = widen(seq_blocks), widen(input_blocks)
    rows = blocks * per
    steps = min(width // tok, blocks)
    extra = -(-groups // 8) * 8
    out_lanes = max(groups * per, lag_own)
    out = pl.pallas_call(
        functools.partial(conv_kernel, scale, lag_own),
        in_specs=[VMEM] * 3,
        out_specs=VMEM,
        out_shape=jax.ShapeDtypeStruct((blocks, tok + extra, out_lanes), jnp.float32),
        scratch_shapes=[pltpu.VMEM((groups, 2 * rows, tok), jnp.bfloat16)] * 2
        + [pltpu.VMEM((groups, rows, tok), jnp.bfloat16)] * 2
        + [
            pltpu.VMEM((rows, tok), jnp.float32),
            pltpu.VMEM((groups, rows, tok), jnp.float32),
            pltpu.VMEM((tok, width), jnp.float32),
            pltpu.VMEM((groups, width - tok), jnp.float32),
        ],
        compiler_params=pltpu.CompilerParams(vmem_limit_bytes=48 * 1024 * 1024),
        cost_estimate=pl.CostEstimate(
            flops=groups * rows * tok * tok * steps * 16,
            bytes_accessed=12 * blocks * tok * LANES + 4 * groups * tok * width,
            transcendentals=0,
        ),
        name="convolve",
    )(seq_blocks, input_blocks, moved)
    return out


def ring_chip(place, chips):
    place = lax.rem(place + chips, chips)
    return jnp.where(place < chips // 2, 2 * place, 2 * (chips - 1 - place) + 1)


def ring_pairs(chips, forward):
    order = list(range(0, chips, 2)) + list(range(chips - 1, 0, -2))
    pairs = [(2 * order[p] + k, 2 * order[(p + 1) % chips] + k) for p in range(chips) for k in range(2)]
    return pairs if forward else [(b, a) for a, b in pairs]


def pair_cotangent(cotangent, features):
    tok, held = cotangent.shape
    parts = lax.axis_size("ch")
    core = lax.rem(lax.axis_index("ctx"), 2)
    swap = [(i, i ^ 1) for i in range(lax.axis_size("ctx"))]
    pieces = [cotangent]
    for s in range(1, parts):
        pieces.append(lax.ppermute(cotangent, "ch", [(j, (j + s) % parts) for j in range(parts)]))
    mine, theirs = [], []
    for piece in pieces:
        blocks = piece.reshape(tok, held // (2 * features), 2, features)
        mine.append(lax.dynamic_index_in_dim(blocks, core, 2, keepdims=False).reshape(tok, held // 2))
        theirs.append(lax.dynamic_index_in_dim(blocks, 1 - core, 2, keepdims=False).reshape(tok, held // 2))
    arrived = lax.ppermute(jnp.concatenate(theirs, axis=1), "ctx", swap)
    return jnp.concatenate([jnp.concatenate(mine, axis=1), arrived], axis=0)


def project(cotangent, out_weight, chains):
    tok = cotangent.shape[0]
    channels, features = out_weight.shape
    devices = lax.axis_size("ctx")
    chips = devices // 2
    parts = lax.axis_size("ch")
    chip = lax.axis_index("ctx") // 2
    place = jnp.where(chip % 2 == 0, chip // 2, chips - 1 - chip // 2)
    both = pair_cotangent(cotangent, features)
    rows = channels // chains
    held = [out_weight[c * rows : (c + 1) * rows] for c in range(chains)]
    sums = [None] * chains
    chips_of_part = chips // parts
    for step in range(chips):
        for c in range(chains):
            source = ring_chip(place - step if c % 2 == 0 else place + step, chips)
            slot = lax.rem(lax.axis_index("ch") - source // chips_of_part + parts, parts)
            column = (slot * chips_of_part + lax.rem(source, chips_of_part)) * features
            term = lax.dot_general(
                lax.dynamic_slice_in_dim(both, column, features, 1),
                held[c],
                (((1,), (1,)), ((), ())),
                preferred_element_type=jnp.float32,
            )
            sums[c] = term if step == 0 else sums[c] + term
        if step < chips - 1:
            held = [lax.ppermute(v, "ctx", ring_pairs(chips, c % 2 == 0)) for c, v in enumerate(held)]
    swap = [(i, i ^ 1) for i in range(devices)]
    done = [v[:tok] + lax.ppermute(v[tok:], "ctx", swap) for v in sums]
    return jnp.concatenate(done, axis=1)


def body(cotangent, out_weight, gate_value, conv_output, conv_input, filters):
    tok, channels = gate_value.shape
    all_groups, lags = filters.shape
    devices = lax.axis_size("ctx")
    per_group = channels // all_groups
    own = channels // devices
    groups = max(1, own // per_group)
    share = max(1, per_group // own)
    lag_own = lags // devices
    me = lax.axis_index("ctx")

    def to_channels(v):
        blocks = v.reshape(tok, devices, own).transpose(1, 0, 2)
        return lax.all_to_all(blocks, "ctx", 0, 0, tiled=True)

    input_blocks = to_channels(conv_input[::-1])
    own_filters = lax.dynamic_slice_in_dim(filters, me * own // per_group, groups, 0)
    moved = toeplitz(own_filters, tok)

    grad_out = project(cotangent, out_weight, 2)
    gate_grad = grad_out * conv_output
    seq_blocks = to_channels(grad_out * gate_value)

    scale = 1.0 / math.sqrt(per_group * tok * devices)
    result = convolve(seq_blocks, input_blocks, moved, lag_own, scale)
    back = lax.all_to_all(result[:, :, : max(own, lag_own)], "ctx", 0, 0, tiled=True)
    input_grad = back[:, :tok, :own].transpose(1, 0, 2).reshape(tok, channels)
    filter_grad = back[:, tok : tok + groups, :lag_own].reshape(all_groups, share, lag_own).sum(axis=1)
    return (input_grad, gate_grad, filter_grad)


def solution(mesh):
    return jax.shard_map(
        body,
        mesh=mesh,
        in_specs=(
            P("ctx", "ch"),
            P("ch", "ctx"),
            P("ctx", "ch"),
            P("ctx", "ch"),
            P("ctx", "ch"),
            P("ch", None),
        ),
        out_specs=(P("ctx", "ch"), P("ctx", "ch"), P("ch", "ctx")),
        check_vma=False,
    )
```

time: 615 us -> 220 us (0.36)
  waiting for transfers between devices: 313 us -> 100 us
  matrix products: 116 us -> 7.78 us
  local copies, waits for them, and re-layouts: 103 us -> 17.9 us
  other arithmetic: 57.4 us -> 3.37 us
  blocking collectives: 0 us -> 35.2 us
  starting transfers between devices: 0.16 us -> 30.7 us
  Pallas kernels: 0 us -> 22.1 us
  between operations: 13.9 us -> 1.76 us
  loops' own time: 11.3 us -> 0 us
    all_gather x3 -> x0, waiting for transfers between devices: 264 us -> none  [the longest x1 133 us: body(): lax.all_gather(out_weight, 'ctx', axis=1, tiled=True)]
    dot_general x21 -> x16, matrix products: 116 us -> 7.78 us  [project(): lax.dot_general(lax.dynamic_slice_in_dim(both, column, features, 1), held...]
    ppermute x0 -> x18, waiting for transfers between devices: none -> 84.8 us  [the longest x14 75.6 us: project(): lax.ppermute(v, 'ctx', ring_pairs(chips, c % 2 == 0))]
    cond x96 -> x0, local copies, waits for them, and re-layouts: 59.4 us -> none
    reduce_scatter x1 -> x0, waiting for transfers between devices: 47.2 us -> none  [body(): lax.psum_scatter(partial_sums, 'ctx', scatter_dimension=1, tiled=True)]
    all_to_all x0 -> x1, blocking collectives: none -> 35.2 us  [body(): lax.all_to_all(result[:, :, :max(own, lag_own)], 'ctx', 0, 0, tiled=True)]
    add x32 -> x2, other arithmetic: 24.2 us -> 0.15 us  [project(): done = [v[:tok] + lax.ppermute(v[tok:], 'ctx', swap) for v in sums]]
    pallas_call x0 -> x2, Pallas kernels: none -> 22.1 us  [the longest x1 15.1 us: convolve(): pl.pallas_call(functools.partial(conv_kernel, scale, lag_own), in_specs=[...]
  transfers between devices with their start and end apart: 4 -> 20, of which waited for: 4 -> 14; matrix products, arithmetic and copies ran while one was open for 4% -> 11% of each run, Pallas kernels for 0% -> 3%
where the time goes in v1:
time: 220 us; the launch traced here: 219 us
  waiting for transfers between devices  100 us (45%)
  blocking collectives  35.2 us (16%)
  starting transfers between devices  30.7 us (14%)
  Pallas kernels  22.1 us (10%)
  local copies, waits for them, and re-layouts  17.9 us (8%)
  matrix products  7.78 us (4%)
  other arithmetic  3.37 us (2%)
    ppermute x14, waiting for transfers between devices, project(): lax.ppermute(v, 'ctx', ring_pairs(chips, c % 2 == 0))  75.6 us
    all_to_all x1, blocking collectives, body(): lax.all_to_all(result[:, :, :max(own, lag_own)], 'ctx', 0, 0, tiled=True)  35.2 us
    ppermute x14, starting transfers between devices, project(): lax.ppermute(v, 'ctx', ring_pairs(chips, c % 2 == 0))  16.1 us
    all_to_all x2, waiting for transfers between devices, to_channels(): return lax.all_to_all(blocks, 'ctx', 0, 0, tiled=True)  15.2 us
    pallas_call x1, Pallas kernels, convolve(): pl.pallas_call(functools.partial(conv_kernel, scale, lag_own), in_specs=[...  15.1 us
    all_to_all x2, starting transfers between devices, to_channels(): return lax.all_to_all(blocks, 'ctx', 0, 0, tiled=True)  10.9 us
    dot_general x16, matrix products, project(): lax.dot_general(lax.dynamic_slice_in_dim(both, column, features, 1), held...  7.78 us
    ppermute x1, waiting for transfers between devices, pair_cotangent(): lax.ppermute(cotangent, 'ch', [(j, (j + s) % parts) for j in range(parts)])  7.63 us
  transfers between devices with their start and end apart: 20, of which 14 were waited for; matrix products, arithmetic and copies ran while one was open for 11% of the time, Pallas kernels for 3%

profile of v1, /device:TPU:0, one launch (start us, length us, event | category | flops | bytes accessed | tf_op | source)
XLA Modules:
  0.0 218.8 jit_solution(2392962625150936861)
XLA Ops:
  0.6 1.4 copy.15
  2.0 3.0 %collective-permute-start = (bf16[128,2048]{0,1:T(8,128)(2,1)S(1)}, bf16[128,2048]{0,1:T(8,128)(2,1)S(1)}, u32[]{:S(2)}, u32[]{:S(2)}) collective-permute-start(bf16[128,2048]{0,1:T(8,128)(2,1)S(1)} %copy.15), channel_id=1, source_target_pairs={{0,1},{1,0},{2,3},{3,2},{4,5},{5,4},{6,7},{7,6},{8,9},{9,8},{10,11... | collective-permute-start | bytes 1572872 | tf_op jit(solution)/shard_map/ppermute | solution.py:174
  5.1 2.2 %fusion.38 = (bf16[1024,256]{1,0:T(8,128)(2,1)}, bf16[1024,256]{1,0:T(8,128)(2,1)}) fusion(bf16[2048,256]{1,0:T(8,128)(2,1)} %param.7), kind=kLoop, calls=%fused_computation.64 | loop fusion | bytes 2097152 | tf_op jit(solution)/shard_map/slice | solution.py:194
  7.3 1.6 collective-permute-start.2
  8.9 0.4 collective-permute-start.10
  9.4 7.6 %collective-permute-done = bf16[128,2048]{0,1:T(8,128)(2,1)S(1)} collective-permute-done((bf16[128,2048]{0,1:T(8,128)(2,1)S(1)}, bf16[128,2048]{0,1:T(8,128)(2,1)S(1)}, u32[]{:S(2)}, u32[]{:S(2)}) %collective-permute-start) | collective-permute-done | bytes 524320 | tf_op jit(solution)/shard_map/ppermute | solution.py:174
  17.0 0.7 constant_dynamic-slice_fusion.3
  17.7 0.8 pad_maximum_fusion.2
  18.5 1.5 copy.19
  20.1 1.4 rev.3
  21.5 1.3 copy.20
  22.9 6.3 %all-to-all-start.1 = ((f32[16,128,128]{2,1,0:T(8,128)}), f32[16,128,128]{2,1,0:T(8,128)S(1)}, u32[]{:S(2)}, u32[]{:S(2)}) async-start(f32[16,128,128]{2,1,0:T(8,128)} %bitcast.9), calls=%async_computation.1 | async-start | bytes 2097152 | tf_op jit(solution)/shard_map/all_to_all | solution.py:229
  30.0 1.4 collective-permute-start.3
  31.4 0.6 collective-permute-start.11
  32.1 1.2 pad_maximum_fusion
  33.3 1.4 fusion.8
  34.7 0.4 convolution_add_fusion.6
  35.1 23.5 %collective-permute-done.3 = bf16[1024,256]{1,0:T(8,128)(2,1)S(1)} collective-permute-done((bf16[1024,256]{1,0:T(8,128)(2,1)}, bf16[1024,256]{1,0:T(8,128)(2,1)S(1)}, u32[]{:S(2)}, u32[]{:S(2)}) %collective-permute-start.3) | collective-permute-done | bytes 524320 | tf_op jit(solution)/shard_map/ppermute | solution.py:210
  58.6 7.2 %collective-permute-start.4 = (bf16[1024,256]{1,0:T(8,128)(2,1)S(1)}, bf16[1024,256]{1,0:T(8,128)(2,1)S(1)}, u32[]{:S(2)}, u32[]{:S(2)}) collective-permute-start(bf16[1024,256]{1,0:T(8,128)(2,1)S(1)} %collective-permute-done.3), channel_id=1, source_target_pairs={{0,8},{2,10},{8,16},{10,18},{16,24},{18,26},{24,28},{26,30},{28,20... | collective-permute-start | bytes 1572872 | tf_op jit(solution)/shard_map/ppermute | solution.py:210
  65.8 1.4 fusion.16
  67.2 0.4 convolution_add_fusion.13
  67.6 0.4 convolution_add_fusion.5
  68.0 0.4 convolution_add_fusion.12
  68.4 8.4 %collective-permute-done.4 = bf16[1024,256]{1,0:T(8,128)(2,1)S(1)} collective-permute-done((bf16[1024,256]{1,0:T(8,128)(2,1)S(1)}, bf16[1024,256]{1,0:T(8,128)(2,1)S(1)}, u32[]{:S(2)}, u32[]{:S(2)}) %collective-permute-start.4) | collective-permute-done | bytes 524320 | tf_op jit(solution)/shard_map/ppermute | solution.py:210
  76.8 2.5 %collective-permute-start.5 = (bf16[1024,256]{1,0:T(8,128)(2,1)S(1)}, bf16[1024,256]{1,0:T(8,128)(2,1)S(1)}, u32[]{:S(2)}, u32[]{:S(2)}) collective-permute-start(bf16[1024,256]{1,0:T(8,128)(2,1)S(1)} %collective-permute-done.4), channel_id=1, source_target_pairs={{0,8},{2,10},{8,16},{10,18},{16,24},{18,26},{24,28},{26,30},{28,20... | collective-permute-start | bytes 1572872 | tf_op jit(solution)/shard_map/ppermute | solution.py:210
  79.3 2.2 %collective-permute-done.12 = bf16[1024,256]{1,0:T(8,128)(2,1)S(1)} collective-permute-done((bf16[1024,256]{1,0:T(8,128)(2,1)S(1)}, bf16[1024,256]{1,0:T(8,128)(2,1)S(1)}, u32[]{:S(2)}, u32[]{:S(2)}) %collective-permute-start.12) | collective-permute-done | bytes 524320 | tf_op jit(solution)/shard_map/ppermute | solution.py:210
  81.4 0.4 collective-permute-start.13
  81.9 0.4 convolution_add_fusion.4
  82.2 0.4 convolution_add_fusion.11
  82.6 9.3 %collective-permute-done.5 = bf16[1024,256]{1,0:T(8,128)(2,1)S(1)} collective-permute-done((bf16[1024,256]{1,0:T(8,128)(2,1)S(1)}, bf16[1024,256]{1,0:T(8,128)(2,1)S(1)}, u32[]{:S(2)}, u32[]{:S(2)}) %collective-permute-start.5) | collective-permute-done | bytes 524320 | tf_op jit(solution)/shard_map/ppermute | solution.py:210
  91.9 2.1 collective-permute-done.13
  94.0 0.4 collective-permute-start.14
  94.4 0.4 convolution_add_fusion.3
  94.8 0.4 convolution_add_fusion.10
  95.2 9.0 %collective-permute-done.6 = bf16[1024,256]{1,0:T(8,128)(2,1)S(1)} collective-permute-done((bf16[1024,256]{1,0:T(8,128)(2,1)S(1)}, bf16[1024,256]{1,0:T(8,128)(2,1)S(1)}, u32[]{:S(2)}, u32[]{:S(2)}) %collective-permute-start.6) | collective-permute-done | bytes 524320 | tf_op jit(solution)/shard_map/ppermute | solution.py:210
  104.2 0.3 collective-permute-start.7
  104.4 1.7 collective-permute-done.14
  106.1 0.4 collective-permute-start.15
  106.5 0.4 convolution_add_fusion.2
  106.9 0.4 convolution_add_fusion.9
  107.2 9.0 %collective-permute-done.7 = bf16[1024,256]{1,0:T(8,128)(2,1)S(1)} collective-permute-done((bf16[1024,256]{1,0:T(8,128)(2,1)S(1)}, bf16[1024,256]{1,0:T(8,128)(2,1)S(1)}, u32[]{:S(2)}, u32[]{:S(2)}) %collective-permute-start.7) | collective-permute-done | bytes 524320 | tf_op jit(solution)/shard_map/ppermute | solution.py:210
  116.5 1.7 collective-permute-done.15
  118.2 0.4 collective-permute-start.16
  118.6 0.3 convolution_add_fusion.1
  119.0 0.4 convolution_add_fusion.8
  119.3 8.8 %collective-permute-done.16 = bf16[1024,256]{1,0:T(8,128)(2,1)S(1)} collective-permute-done((bf16[1024,256]{1,0:T(8,128)(2,1)S(1)}, bf16[1024,256]{1,0:T(8,128)(2,1)S(1)}, u32[]{:S(2)}, u32[]{:S(2)}) %collective-permute-start.16) | collective-permute-done | bytes 524320 | tf_op jit(solution)/shard_map/ppermute | solution.py:210
  128.1 0.3 convolution_add_fusion
  128.6 0.4 convolution_add_fusion.7
  129.0 0.5 collective-permute-start.9
  129.6 0.9 collective-permute-done.17
  130.6 0.7 collective-permute-done.9
  131.3 1.2 fusion
  132.5 1.3 copy.17
  133.8 2.5 %copy.18 = f32[128,16,128]{2,0,1:T(8,128)} copy(f32[128,16,128]{0,2,1:T(8,128)} %bitcast.31) | data formatting | bytes 2097152 | tf_op jit(solution)/shard_map/reshape | solution.py:228
  136.4 4.6 %all-to-all-start = ((f32[16,128,128]{2,1,0:T(8,128)}), f32[16,128,128]{2,1,0:T(8,128)S(1)}, u32[]{:S(2)}, u32[]{:S(2)}) async-start(f32[16,128,128]{2,1,0:T(8,128)} %bitcast.29), calls=%async_computation | async-start | bytes 2097152 | tf_op jit(solution)/shard_map/all_to_all | solution.py:229
  141.1 0.7 broadcast_in_dim.3.filter_ref
  141.7 7.0 %toeplitz.1.t_ref = bf16[8,256,2176]{2,1,0:T(8,128)(2,1)} custom-call(f32[8,1,2176]{2,1,0:T(1,128)} %broadcast_in_dim.3.filter_ref), custom_call_target="tpu_custom_call" | custom-call | flops 8912896 | bytes 8982528 | tf_op jit(solution)/shard_map/toeplitz/pallas_call | solution.py:33
  148.8 15.2 %all-to-all-done.s_ref = f32[16,128,128]{2,1,0:T(8,128)S(1)} async-done(((f32[16,128,128]{2,1,0:T(8,128)}), f32[16,128,128]{2,1,0:T(8,128)S(1)}, u32[]{:S(2)}, u32[]{:S(2)}) %all-to-all-start) | async-done | bytes 1048608 | tf_op jit(solution)/shard_map/all_to_all | solution.py:229
  163.9 15.1 %convolve.1 = f32[16,136,128]{2,1,0:T(8,128)S(1)} custom-call(f32[16,128,128]{2,1,0:T(8,128)S(1)} %all-to-all-done.s_ref, f32[16,128,128]{2,1,0:T(8,128)S(1)} %all-to-all-done.1.x_ref, bf16[8,256,2176]{2,1,0:T(8,128)(2,1)} %toeplitz.1.t_ref), custom_call_target="tpu_custom_call" | custom-call | flops 8589934592 | bytes 12058624 | tf_op jit(solution)/shard_map/convolve/pallas_call | solution.py:132
  179.0 35.2 %all_to_all.15 = f32[16,136,128]{2,1,0:T(8,128)S(1)} all-to-all(f32[16,136,128]{2,1,0:T(8,128)S(1)} %convolve.1), channel_id=1, replica_groups=mesh['ctx'=16,'ch'=2] {'ctx'}, dimensions={0} | all-to-all | bytes 2228224 | tf_op jit(solution)/shard_map/all_to_all | solution.py:241
  214.2 1.1 slice_bitcast_fusion
  215.3 1.6 copy.21
  216.8 1.3 copy.22
  218.1 0.6 slice_bitcast_fusion.1
  (26 shorter events, 0.7 us)
Async XLA Ops:
  0.6 140.4 %copy-start = (f32[128,2048]{1,0:T(8,128)S(1)}, f32[128,2048]{1,0:T(8,128)}, u32[]{:S(2)}) copy-start(f32[128,2048]{1,0:T(8,128)} %param.11) | copy-start | bytes 3145732
  2.0 14.9 %collective-permute-start = (bf16[128,2048]{0,1:T(8,128)(2,1)S(1)}, bf16[128,2048]{0,1:T(8,128)(2,1)S(1)}, u32[]{:S(2)}, u32[]{:S(2)}) collective-permute-start(bf16[128,2048]{0,1:T(8,128)(2,1)S(1)} %copy.15), channel_id=1, source_target_pairs={{0,1},{1,0},{2,3},{3,2},{4,5},{5,4},{6,7},{7,6},{8,9},{9,8},{10,11... | collective-permute-start | bytes 1572872 | tf_op jit(solution)/shard_map/ppermute | solution.py:174
  7.3 22.7 %collective-permute-start.2 = (bf16[1024,256]{1,0:T(8,128)(2,1)}, bf16[1024,256]{1,0:T(8,128)(2,1)}, u32[]{:S(2)}, u32[]{:S(2)}) collective-permute-start(bf16[1024,256]{1,0:T(8,128)(2,1)} %get-tuple-element.11), channel_id=1, source_target_pairs={{0,8},{2,10},{8,16},{10,18},{16,24},{18,26},{24,28},{26,30},{28,20... | collective-permute-start | bytes 1572872 | tf_op jit(solution)/shard_map/ppermute | solution.py:210
  8.9 22.6 %collective-permute-start.10 = (bf16[1024,256]{1,0:T(8,128)(2,1)}, bf16[1024,256]{1,0:T(8,128)(2,1)}, u32[]{:S(2)}, u32[]{:S(2)}) collective-permute-start(bf16[1024,256]{1,0:T(8,128)(2,1)} %get-tuple-element.12), channel_id=1, source_target_pairs={{8,0},{10,2},{16,8},{18,10},{24,16},{26,18},{28,24},{30,26},{20,28... | collective-permute-start | bytes 1572872 | tf_op jit(solution)/shard_map/ppermute | solution.py:210
  18.5 13.5 %collective-permute-start.1 = (bf16[128,2048]{0,1:T(8,128)(2,1)}, bf16[128,2048]{0,1:T(8,128)(2,1)}, u32[]{:S(2)}, u32[]{:S(2)}) collective-permute-start(bf16[128,2048]{0,1:T(8,128)(2,1)} %pad_maximum_fusion.2), channel_id=1, source_target_pairs={{0,2},{2,0},{4,6},{6,4},{8,10},{10,8},{12,14},{14,12},{16,18},{18,... | collective-permute-start | bytes 1572872 | tf_op jit(solution)/shard_map/ppermute | solution.py:180
  22.9 113.5 %all-to-all-start.1 = ((f32[16,128,128]{2,1,0:T(8,128)}), f32[16,128,128]{2,1,0:T(8,128)S(1)}, u32[]{:S(2)}, u32[]{:S(2)}) async-start(f32[16,128,128]{2,1,0:T(8,128)} %bitcast.9), calls=%async_computation.1 | async-start | bytes 2097152 | tf_op jit(solution)/shard_map/all_to_all | solution.py:229
  29.7 5.0 %copy-start.1 = (bf16[2048,256]{1,0:T(8,128)(2,1)S(1)}, bf16[2048,256]{1,0:T(8,128)(2,1)}, u32[]{:S(2)}) copy-start(bf16[2048,256]{1,0:T(8,128)(2,1)} %param.7) | copy-start | bytes 3145732
  30.0 28.6 %collective-permute-start.3 = (bf16[1024,256]{1,0:T(8,128)(2,1)}, bf16[1024,256]{1,0:T(8,128)(2,1)S(1)}, u32[]{:S(2)}, u32[]{:S(2)}) collective-permute-start(bf16[1024,256]{1,0:T(8,128)(2,1)} %collective-permute-done.2), channel_id=1, source_target_pairs={{0,8},{2,10},{8,16},{10,18},{16,24},{18,26},{24,28},{26,30},{28,20... | collective-permute-start | bytes 1572872 | tf_op jit(solution)/shard_map/ppermute | solution.py:210
  31.4 36.1 %collective-permute-start.11 = (bf16[1024,256]{1,0:T(8,128)(2,1)}, bf16[1024,256]{1,0:T(8,128)(2,1)S(1)}, u32[]{:S(2)}, u32[]{:S(2)}) collective-permute-start(bf16[1024,256]{1,0:T(8,128)(2,1)} %collective-permute-done.10), channel_id=1, source_target_pairs={{8,0},{10,2},{16,8},{18,10},{24,16},{26,18},{28,24},{30,26},{20,28... | collective-permute-start | bytes 1572872 | tf_op jit(solution)/shard_map/ppermute | solution.py:210
  58.6 18.2 %collective-permute-start.4 = (bf16[1024,256]{1,0:T(8,128)(2,1)S(1)}, bf16[1024,256]{1,0:T(8,128)(2,1)S(1)}, u32[]{:S(2)}, u32[]{:S(2)}) collective-permute-start(bf16[1024,256]{1,0:T(8,128)(2,1)S(1)} %collective-permute-done.3), channel_id=1, source_target_pairs={{0,8},{2,10},{8,16},{10,18},{16,24},{18,26},{24,28},{26,30},{28,20... | collective-permute-start | bytes 1572872 | tf_op jit(solution)/shard_map/ppermute | solution.py:210
  67.6 13.9 %collective-permute-start.12 = (bf16[1024,256]{1,0:T(8,128)(2,1)S(1)}, bf16[1024,256]{1,0:T(8,128)(2,1)S(1)}, u32[]{:S(2)}, u32[]{:S(2)}) collective-permute-start(bf16[1024,256]{1,0:T(8,128)(2,1)S(1)} %collective-permute-done.11), channel_id=1, source_target_pairs={{8,0},{10,2},{16,8},{18,10},{24,16},{26,18},{28,24},{30,26},{20,28... | collective-permute-start | bytes 1572872 | tf_op jit(solution)/shard_map/ppermute | solution.py:210
  76.8 15.1 %collective-permute-start.5 = (bf16[1024,256]{1,0:T(8,128)(2,1)S(1)}, bf16[1024,256]{1,0:T(8,128)(2,1)S(1)}, u32[]{:S(2)}, u32[]{:S(2)}) collective-permute-start(bf16[1024,256]{1,0:T(8,128)(2,1)S(1)} %collective-permute-done.4), channel_id=1, source_target_pairs={{0,8},{2,10},{8,16},{10,18},{16,24},{18,26},{24,28},{26,30},{28,20... | collective-permute-start | bytes 1572872 | tf_op jit(solution)/shard_map/ppermute | solution.py:210
  81.4 12.6 %collective-permute-start.13 = (bf16[1024,256]{1,0:T(8,128)(2,1)S(1)}, bf16[1024,256]{1,0:T(8,128)(2,1)S(1)}, u32[]{:S(2)}, u32[]{:S(2)}) collective-permute-start(bf16[1024,256]{1,0:T(8,128)(2,1)S(1)} %collective-permute-done.12), channel_id=1, source_target_pairs={{8,0},{10,2},{16,8},{18,10},{24,16},{26,18},{28,24},{30,26},{20,28... | collective-permute-start | bytes 1572872 | tf_op jit(solution)/shard_map/ppermute | solution.py:210
  91.9 12.2 %collective-permute-start.6 = (bf16[1024,256]{1,0:T(8,128)(2,1)S(1)}, bf16[1024,256]{1,0:T(8,128)(2,1)S(1)}, u32[]{:S(2)}, u32[]{:S(2)}) collective-permute-start(bf16[1024,256]{1,0:T(8,128)(2,1)S(1)} %collective-permute-done.5), channel_id=1, source_target_pairs={{0,8},{2,10},{8,16},{10,18},{16,24},{18,26},{24,28},{26,30},{28,20... | collective-permute-start | bytes 1572872 | tf_op jit(solution)/shard_map/ppermute | solution.py:210
  94.0 12.1 %collective-permute-start.14 = (bf16[1024,256]{1,0:T(8,128)(2,1)S(1)}, bf16[1024,256]{1,0:T(8,128)(2,1)S(1)}, u32[]{:S(2)}, u32[]{:S(2)}) collective-permute-start(bf16[1024,256]{1,0:T(8,128)(2,1)S(1)} %collective-permute-done.13), channel_id=1, source_target_pairs={{8,0},{10,2},{16,8},{18,10},{24,16},{26,18},{28,24},{30,26},{20,28... | collective-permute-start | bytes 1572872 | tf_op jit(solution)/shard_map/ppermute | solution.py:210
  104.2 12.1 %collective-permute-start.7 = (bf16[1024,256]{1,0:T(8,128)(2,1)S(1)}, bf16[1024,256]{1,0:T(8,128)(2,1)S(1)}, u32[]{:S(2)}, u32[]{:S(2)}) collective-permute-start(bf16[1024,256]{1,0:T(8,128)(2,1)S(1)} %collective-permute-done.6), channel_id=1, source_target_pairs={{0,8},{2,10},{8,16},{10,18},{16,24},{18,26},{24,28},{26,30},{28,20... | collective-permute-start | bytes 1572872 | tf_op jit(solution)/shard_map/ppermute | solution.py:210
  106.1 12.1 %collective-permute-start.15 = (bf16[1024,256]{1,0:T(8,128)(2,1)S(1)}, bf16[1024,256]{1,0:T(8,128)(2,1)S(1)}, u32[]{:S(2)}, u32[]{:S(2)}) collective-permute-start(bf16[1024,256]{1,0:T(8,128)(2,1)S(1)} %collective-permute-done.14), channel_id=1, source_target_pairs={{8,0},{10,2},{16,8},{18,10},{24,16},{26,18},{28,24},{30,26},{20,28... | collective-permute-start | bytes 1572872 | tf_op jit(solution)/shard_map/ppermute | solution.py:210
  116.3 12.4 %collective-permute-start.8 = (bf16[1024,256]{1,0:T(8,128)(2,1)S(1)}, bf16[1024,256]{1,0:T(8,128)(2,1)S(1)}, u32[]{:S(2)}, u32[]{:S(2)}) collective-permute-start(bf16[1024,256]{1,0:T(8,128)(2,1)S(1)} %collective-permute-done.7), channel_id=1, source_target_pairs={{0,8},{2,10},{8,16},{10,18},{16,24},{18,26},{24,28},{26,30},{28,20... | collective-permute-start | bytes 1572872 | tf_op jit(solution)/shard_map/ppermute | solution.py:210
  118.2 9.9 %collective-permute-start.16 = (bf16[1024,256]{1,0:T(8,128)(2,1)S(1)}, bf16[1024,256]{1,0:T(8,128)(2,1)S(1)}, u32[]{:S(2)}, u32[]{:S(2)}) collective-permute-start(bf16[1024,256]{1,0:T(8,128)(2,1)S(1)} %collective-permute-done.15), channel_id=1, source_target_pairs={{8,0},{10,2},{16,8},{18,10},{24,16},{26,18},{28,24},{30,26},{20,28... | collective-permute-start | bytes 1572872 | tf_op jit(solution)/shard_map/ppermute | solution.py:210
  128.5 2.0 collective-permute-start.17
  129.0 2.4 %copy-start.2 = (f32[128,2048]{1,0:T(8,128)S(1)}, f32[128,2048]{1,0:T(8,128)}, u32[]{:S(2)}) copy-start(f32[128,2048]{1,0:T(8,128)} %param.9) | copy-start | bytes 3145732
  129.0 2.4 %copy-start.3 = (f32[128,2048]{1,0:T(8,128)S(1)}, f32[128,2048]{1,0:T(8,128)}, u32[]{:S(2)}) copy-start(f32[128,2048]{1,0:T(8,128)} %param.8) | copy-start | bytes 3145732
  129.0 2.2 %collective-permute-start.9 = (f32[128,1024]{1,0:T(8,128)S(1)}, f32[128,1024]{1,0:T(8,128)S(1)}, u32[]{:S(2)}, u32[]{:S(2)}) collective-permute-start(f32[128,1024]{1,0:T(8,128)S(1)} %slice.33), channel_id=1, source_target_pairs={{0,2},{2,0},{4,6},{6,4},{8,10},{10,8},{12,14},{14,12},{16,18},{18,... | collective-permute-start | bytes 1572872 | tf_op jit(solution)/shard_map/ppermute | solution.py:212
  136.4 27.6 %all-to-all-start = ((f32[16,128,128]{2,1,0:T(8,128)}), f32[16,128,128]{2,1,0:T(8,128)S(1)}, u32[]{:S(2)}, u32[]{:S(2)}) async-start(f32[16,128,128]{2,1,0:T(8,128)} %bitcast.29), calls=%async_computation | async-start | bytes 2097152 | tf_op jit(solution)/shard_map/all_to_all | solution.py:229

commit v2 on v1

v2 whole, which is shorter than its diff:
```python
import functools
import math

import jax
import jax.numpy as jnp
from jax import lax
from jax.experimental import pallas as pl
from jax.experimental.pallas import tpu as pltpu
from jax.sharding import PartitionSpec as P

LANES = 128
ROW_TILE = 16
CODE_UNIT = 8192.0
SMALLEST = 1e-30
VMEM = pl.BlockSpec(memory_space=pltpu.VMEM)


def split(value):
    high = value.astype(jnp.bfloat16)
    return high, (value - high.astype(jnp.float32)).astype(jnp.bfloat16)


def toeplitz_kernel(filter_ref, out_ref):
    tok = out_ref.shape[1] // 2
    rows = jnp.broadcast_to(filter_ref[0], (tok, filter_ref.shape[2]))
    high, low = split(pltpu.roll(rows, 0, 1, stride=1, stride_axis=0))
    out_ref[0, :tok, :] = high
    out_ref[0, tok:, :] = low


def toeplitz(filters, tok):
    groups, lags = filters.shape
    width = lags + tok
    padded = jnp.pad(filters, ((0, 0), (0, tok)))[:, None, :]
    return pl.pallas_call(
        toeplitz_kernel,
        grid=(groups,),
        in_specs=[pl.BlockSpec((1, 1, width), lambda g: (g, 0, 0))],
        out_specs=pl.BlockSpec((1, 2 * tok, width), lambda g: (g, 0, 0)),
        out_shape=jax.ShapeDtypeStruct((groups, 2 * tok, width), jnp.bfloat16),
        cost_estimate=pl.CostEstimate(
            flops=groups * tok * width * 4, bytes_accessed=groups * width * (4 + 4 * tok), transcendentals=0
        ),
        name="toeplitz",
    )(padded)


def stack_kernel(x_ref, left_ref, x_hi, x_lo):
    blocks, tok, _ = x_ref.shape
    groups, rows, _ = x_hi.shape
    per = rows // blocks

    @pl.loop(0, blocks)
    def _(a):
        at = pl.ds(pl.multiple_of(a * per, per), per)
        high, low = split(x_ref[a].T[: groups * per])
        x_hi[:, at, :] = high.reshape(groups, per, tok)
        x_lo[:, at, :] = low.reshape(groups, per, tok)

    @pl.loop(0, groups)
    def _(g):
        left_ref[g] = jnp.concatenate([x_hi[g], x_lo[g]], axis=1).T


def stack_input(input_blocks, groups, per):
    blocks, tok, lanes = input_blocks.shape
    rows = blocks * per
    return pl.pallas_call(
        stack_kernel,
        in_specs=[VMEM],
        out_specs=VMEM,
        out_shape=jax.ShapeDtypeStruct((groups, 2 * tok, rows), jnp.bfloat16),
        scratch_shapes=[pltpu.VMEM((groups, rows, tok), jnp.bfloat16)] * 2,
        compiler_params=pltpu.CompilerParams(vmem_limit_bytes=32 * 1024 * 1024),
        cost_estimate=pl.CostEstimate(
            flops=blocks * tok * lanes * 8, bytes_accessed=blocks * tok * lanes * 8, transcendentals=0
        ),
        name="stack_input",
    )(input_blocks)


def coded(value, most):
    exponent = jnp.floor(jnp.log2(jnp.maximum(most, SMALLEST)))
    v = value * jnp.exp2(-exponent)
    return v * jnp.abs(v) * CODE_UNIT, exponent


def decoded(code, exponent):
    code = code.astype(jnp.float32)
    return jnp.sign(code) * jnp.sqrt(jnp.abs(code) * (1.0 / CODE_UNIT)) * jnp.exp2(exponent.astype(jnp.float32))


def largest(value):
    return jnp.max(jnp.max(jnp.abs(value), axis=0, keepdims=True), axis=1, keepdims=True)


def conv_kernel(scale, lag_own, s_ref, left_ref, t_ref, out_ref, s_hi, s_lo, grads, cross, lag_sums):
    blocks, tok, _ = s_ref.shape
    groups, rows, _ = grads.shape
    per = rows // blocks
    width = t_ref.shape[2]
    steps = width // tok
    used = min(steps, blocks)
    g = pl.program_id(0)

    @pl.when(g == 0)
    def _():
        s_hi[:, rows:, :] = jnp.zeros_like(s_hi[:, rows:, :])
        s_lo[:, rows:, :] = jnp.zeros_like(s_lo[:, rows:, :])
        for a in range(blocks):
            high, low = split(s_ref[a].T[: groups * per])
            s_hi[:, a * per : (a + 1) * per, :] = high.reshape(groups, per, tok)
            s_lo[:, a * per : (a + 1) * per, :] = low.reshape(groups, per, tok)

    for d in range(0, used, 2):
        first, second = d * per, (d + 1) * per
        count = rows - first
        left = jnp.concatenate(
            [
                jnp.concatenate([ref[g, first : first + count, :], ref[g, second : second + count, :]], axis=1)
                for ref in (s_hi, s_lo)
            ],
            axis=0,
        )
        if d + 2 <= steps:
            right = t_ref[0, :, d * tok : (d + 2) * tok]
        else:
            right = jnp.concatenate([t_ref[0, :, d * tok :], jnp.zeros((2 * tok, tok), jnp.bfloat16)], axis=1)
        product = lax.dot_general(left, right, (((1,), (1,)), ((), ())), preferred_element_type=jnp.float32)
        term = product[:count, :tok] + (product[:count, tok:] + product[count:, :tok])
        if d == 0:
            grads[g] = term
        else:
            grads[g, :count, :] += term

    for d in range(0, used, 2):
        depth = min(rows, -(-(rows - d * per) // LANES) * LANES)
        high, low = [
            jnp.concatenate([ref[g, d * per : d * per + depth, :], ref[g, (d + 1) * per : (d + 1) * per + depth, :]], axis=1)
            for ref in (s_hi, s_lo)
        ]
        main = jnp.dot(left_ref[0, :, :depth], high, preferred_element_type=jnp.float32)
        rest = jnp.dot(left_ref[0, :tok, :depth], low, preferred_element_type=jnp.float32)
        stop = min(d + 2, steps)
        cross[:, d * tok : stop * tok] = (main[:tok] + (main[tok:] + rest))[:, : (stop - d) * tok]
    if used + used % 2 < steps:
        cross[:, (used + used % 2) * tok :] = jnp.zeros_like(cross[:, (used + used % 2) * tok :])
    skewed = pltpu.roll(cross[...], width - tok + 1, 1, stride=1, stride_axis=0)
    lag_sums[pl.ds(g, 1), :] = jnp.sum(skewed, axis=0, keepdims=True)[:, : width - tok] * scale

    @pl.when(g == groups - 1)
    def _():
        lags, lag_exponent = coded(lag_sums[...], largest(lag_sums[...]))
        held = out_ref.shape[1] - 8
        for a in range(blocks):
            out_ref[a, tok:held, :] = jnp.zeros_like(out_ref[a, tok:held, :])
            block = grads[:, a * per : (a + 1) * per, :].reshape(groups * per, tok)
            code, exponent = coded(block, largest(block))
            if out_ref.shape[2] > groups * per:
                out_ref[a, :tok, :] = jnp.zeros_like(out_ref[a, :tok, :])
            out_ref[a, :tok, : groups * per] = code.T
            out_ref[a, tok : tok + groups, :lag_own] = lags[:, a * lag_own : (a + 1) * lag_own]
            which = lax.broadcasted_iota(jnp.int32, (8, out_ref.shape[2]), 0)
            out_ref[a, held:, :] = jnp.where(which == 0, exponent, lag_exponent)


def convolve(seq_blocks, input_blocks, moved, channels, lag_own, scale):
    blocks, tok, own = seq_blocks.shape
    groups, _, width = moved.shape
    per = -(-channels // ROW_TILE) * ROW_TILE
    if groups * per != LANES or channels != per:
        wide = groups * per
        lanes = -(-wide // LANES) * LANES

        def widen(v):
            v = v.reshape(blocks, tok, groups, channels)
            v = jnp.pad(v, ((0, 0), (0, 0), (0, 0), (0, per - channels))).reshape(blocks, tok, wide)
            return jnp.pad(v, ((0, 0), (0, 0), (0, lanes - wide)))

        seq_blocks, input_blocks = widen(seq_blocks), widen(input_blocks)
    rows = blocks * per
    left = stack_input(input_blocks, groups, per)
    extra = -(-(groups + 8) // ROW_TILE) * ROW_TILE
    out_lanes = max(groups * per, lag_own)
    return pl.pallas_call(
        functools.partial(conv_kernel, scale, lag_own),
        grid=(groups,),
        in_specs=[
            pl.BlockSpec(seq_blocks.shape, lambda g: (0, 0, 0)),
            pl.BlockSpec((1, 2 * tok, rows), lambda g: (g, 0, 0)),
            pl.BlockSpec((1, 2 * tok, width), lambda g: (g, 0, 0)),
        ],
        out_specs=pl.BlockSpec((blocks, tok + extra, out_lanes), lambda g: (0, 0, 0)),
        out_shape=jax.ShapeDtypeStruct((blocks, tok + extra, out_lanes), jnp.float32),
        scratch_shapes=[pltpu.VMEM((groups, 2 * rows, tok), jnp.bfloat16)] * 2
        + [
            pltpu.VMEM((groups, rows, tok), jnp.float32),
            pltpu.VMEM((tok, width), jnp.float32),
            pltpu.VMEM((groups, width - tok), jnp.float32),
        ],
        compiler_params=pltpu.CompilerParams(vmem_limit_bytes=48 * 1024 * 1024),
        cost_estimate=pl.CostEstimate(
            flops=groups * rows * tok * width * 14,
            bytes_accessed=12 * blocks * tok * LANES + 4 * groups * tok * width,
            transcendentals=0,
        ),
        name="convolve",
    )(seq_blocks, left, moved)


def ring_chip(place, chips):
    place = lax.rem(place + chips, chips)
    return jnp.where(place < chips // 2, 2 * place, 2 * (chips - 1 - place) + 1)


def ring_pairs(chips, forward):
    order = list(range(0, chips, 2)) + list(range(chips - 1, 0, -2))
    pairs = [(2 * order[p] + k, 2 * order[(p + 1) % chips] + k) for p in range(chips) for k in range(2)]
    return pairs if forward else [(b, a) for a, b in pairs]


def pair_cotangent(cotangent, features):
    tok, held = cotangent.shape
    parts = lax.axis_size("ch")
    core = lax.rem(lax.axis_index("ctx"), 2)
    swap = [(i, i ^ 1) for i in range(lax.axis_size("ctx"))]
    pieces = [cotangent]
    for s in range(1, parts):
        pieces.append(lax.ppermute(cotangent, "ch", [(j, (j + s) % parts) for j in range(parts)]))
    mine, theirs = [], []
    for piece in pieces:
        blocks = piece.reshape(tok, held // (2 * features), 2, features)
        mine.append(lax.dynamic_index_in_dim(blocks, core, 2, keepdims=False).reshape(tok, held // 2))
        theirs.append(lax.dynamic_index_in_dim(blocks, 1 - core, 2, keepdims=False).reshape(tok, held // 2))
    arrived = lax.ppermute(jnp.concatenate(theirs, axis=1), "ctx", swap)
    return jnp.concatenate([jnp.concatenate(mine, axis=1), arrived], axis=0)


def seq_kernel(*refs):
    *parts, gate_ref, out_ref = refs
    count = len(parts) // 2
    blocks, tok, own = out_ref.shape
    width = parts[0].shape[1]
    for b in range(blocks):
        c, at = divmod(b * own, width)
        grad_out = parts[c][:, at : at + own] + parts[count + c][:, at : at + own]
        out_ref[b] = grad_out * gate_ref[:, b * own : (b + 1) * own]


def seq_blocks_of(sums, arrived, gate_value, blocks):
    tok, channels = gate_value.shape
    return pl.pallas_call(
        seq_kernel,
        in_specs=[VMEM] * (2 * len(sums) + 1),
        out_specs=VMEM,
        out_shape=jax.ShapeDtypeStruct((blocks, tok, channels // blocks), jnp.float32),
        compiler_params=pltpu.CompilerParams(vmem_limit_bytes=32 * 1024 * 1024),
        cost_estimate=pl.CostEstimate(
            flops=2 * tok * channels, bytes_accessed=16 * tok * channels, transcendentals=0
        ),
        name="seq_grad",
    )(*sums, *arrived, gate_value)


def project(cotangent, out_weight, chains):
    tok = cotangent.shape[0]
    channels, features = out_weight.shape
    devices = lax.axis_size("ctx")
    chips = devices // 2
    parts = lax.axis_size("ch")
    chip = lax.axis_index("ctx") // 2
    place = jnp.where(chip % 2 == 0, chip // 2, chips - 1 - chip // 2)
    both = pair_cotangent(cotangent, features)
    rows = channels // chains
    held = [out_weight[c * rows : (c + 1) * rows] for c in range(chains)]
    sums = [[None, None] for _ in range(chains)]
    chips_of_part = chips // parts
    for step in range(chips):
        for c in range(chains):
            source = ring_chip(place - step if c % 2 == 0 else place + step, chips)
            slot = lax.rem(lax.axis_index("ch") - source // chips_of_part + parts, parts)
            column = (slot * chips_of_part + lax.rem(source, chips_of_part)) * features
            for half in (1, 0):
                term = lax.dot_general(
                    lax.dynamic_slice(both, (half * tok, column), (tok, features)),
                    held[c],
                    (((1,), (1,)), ((), ())),
                    preferred_element_type=jnp.float32,
                )
                sums[c][half] = term if step == 0 else sums[c][half] + term
        if step < chips - 1:
            held = [lax.ppermute(v, "ctx", ring_pairs(chips, c % 2 == 0)) for c, v in enumerate(held)]
    swap = [(i, i ^ 1) for i in range(devices)]
    return [own for own, _ in sums], [lax.ppermute(other, "ctx", swap) for _, other in sums]


def body(cotangent, out_weight, gate_value, conv_output, conv_input, filters):
    tok, channels = gate_value.shape
    all_groups, lags = filters.shape
    devices = lax.axis_size("ctx")
    per_group = channels // all_groups
    own = channels // devices
    groups = max(1, own // per_group)
    share = max(1, per_group // own)
    lag_own = lags // devices
    me = lax.axis_index("ctx")

    def exchange(blocks):
        return lax.all_to_all(blocks, "ctx", 0, 0, tiled=True)

    code, exponent = coded(conv_input[::-1], largest(conv_input))
    code = code.reshape(tok, devices, own).transpose(1, 0, 2)
    code = jnp.concatenate([code, jnp.broadcast_to(exponent, (devices, ROW_TILE, own))], axis=1)
    code = exchange(code.astype(jnp.float16))
    input_blocks = decoded(code[:, :tok], code[:, tok : tok + 1, :1])
    own_filters = lax.dynamic_slice_in_dim(filters, me * own // per_group, groups, 0)
    moved = toeplitz(own_filters, tok)

    sums, arrived = project(cotangent, out_weight, 2)
    seq_blocks = exchange(seq_blocks_of(sums, arrived, gate_value, devices))
    grad_out = jnp.concatenate([a + b for a, b in zip(sums, arrived)], axis=1)
    gate_grad = grad_out * conv_output

    scale = 1.0 / math.sqrt(per_group * tok * devices)
    result = convolve(seq_blocks, input_blocks, moved, min(own, per_group), lag_own, scale)
    back = exchange(result[:, :, : max(own, lag_own)].astype(jnp.float16))
    held = back.shape[1] - 8
    input_grad = decoded(back[:, :tok, :own], back[:, held : held + 1, :1])
    input_grad = input_grad.transpose(1, 0, 2).reshape(tok, channels)
    filter_grad = decoded(back[:, tok : tok + groups, :lag_own], back[:, held + 1 : held + 2, :1])
    filter_grad = filter_grad.reshape(all_groups, share, lag_own).sum(axis=1)
    return (input_grad, gate_grad, filter_grad)


def solution(mesh):
    return jax.shard_map(
        body,
        mesh=mesh,
        in_specs=(
            P("ctx", "ch"),
            P("ch", "ctx"),
            P("ctx", "ch"),
            P("ctx", "ch"),
            P("ctx", "ch"),
            P("ch", None),
        ),
        out_specs=(P("ctx", "ch"), P("ctx", "ch"), P("ch", "ctx")),
        check_vma=False,
    )
```

time: 220 us -> 190 us (0.86)
  blocking collectives: 35.2 us -> 0 us
  waiting for transfers between devices: 100 us -> 91.5 us
  matrix products: 7.78 us -> 15.9 us
  local copies, waits for them, and re-layouts: 17.9 us -> 10.6 us
  starting transfers between devices: 30.7 us -> 37.3 us
  other arithmetic: 3.37 us -> 9.28 us
    all_to_all x1 -> x0, blocking collectives: 35.2 us -> none  [body(): lax.all_to_all(result[:, :, :max(own, lag_own)], 'ctx', 0, 0, tiled=True)]
    ppermute x14, waiting for transfers between devices: 75.6 us -> 58.3 us  [project(): lax.ppermute(v, 'ctx', ring_pairs(chips, c % 2 == 0))]
    all_to_all x2 -> x3, waiting for transfers between devices: 15.2 us -> 25.1 us  [exchange(): return lax.all_to_all(blocks, 'ctx', 0, 0, tiled=True)]
    dot_general x16 -> x32, matrix products: 7.78 us -> 15.9 us  [project(): lax.dot_general(lax.dynamic_slice(both, (half * tok, column), (tok, featu...]
    all_to_all x2 -> x3, starting transfers between devices: 10.9 us -> 17.1 us  [exchange(): return lax.all_to_all(blocks, 'ctx', 0, 0, tiled=True)]
    reshape x2 -> x1, local copies, waits for them, and re-layouts: 3.87 us -> 0.45 us  [body(): code = code.reshape(tok, devices, own).transpose(1, 0, 2)]
    transpose x2 -> x1, local copies, waits for them, and re-layouts: 2.63 us -> 0.33 us  [body(): input_grad = input_grad.transpose(1, 0, 2).reshape(tok, channels)]
    pallas_call x1 -> x3, Pallas kernels: 15.1 us -> 14.9 us  [the longest x1 11.4 us: convolve(): pl.pallas_call(functools.partial(conv_kernel, scale, lag_own), grid=(grou...]
  transfers between devices with their start and end apart: 20 -> 21, of which waited for: 14 -> 12; matrix products, arithmetic and copies ran while one was open for 11% -> 15% of each run, Pallas kernels for 3% -> 6%
where the time goes in v2:
time: 190 us; the launch traced here: 189 us
  waiting for transfers between devices  91.5 us (48%)
  starting transfers between devices  37.3 us (20%)
  Pallas kernels  21.9 us (12%)
  matrix products  15.9 us (8%)
  local copies, waits for them, and re-layouts  10.6 us (6%)
  other arithmetic  9.28 us (5%)
  between operations  2.66 us (1%)
    ppermute x14, waiting for transfers between devices, project(): lax.ppermute(v, 'ctx', ring_pairs(chips, c % 2 == 0))  58.3 us
    all_to_all x3, waiting for transfers between devices, exchange(): return lax.all_to_all(blocks, 'ctx', 0, 0, tiled=True)  25.1 us
    ppermute x14, starting transfers between devices, project(): lax.ppermute(v, 'ctx', ring_pairs(chips, c % 2 == 0))  17.1 us
    all_to_all x3, starting transfers between devices, exchange(): return lax.all_to_all(blocks, 'ctx', 0, 0, tiled=True)  17.1 us
    dot_general x32, matrix products, project(): lax.dot_general(lax.dynamic_slice(both, (half * tok, column), (tok, featu...  15.9 us
    pallas_call x1, Pallas kernels, convolve(): pl.pallas_call(functools.partial(conv_kernel, scale, lag_own), grid=(grou...  11.4 us
    ppermute x1, waiting for transfers between devices, pair_cotangent(): lax.ppermute(cotangent, 'ch', [(j, (j + s) % parts) for j in range(parts)])  7.6 us
    pallas_call x1, Pallas kernels, toeplitz(): pl.pallas_call(toeplitz_kernel, grid=(groups,), in_specs=[pl.BlockSpec((1...  7.01 us
  transfers between devices with their start and end apart: 21, of which 12 were waited for; matrix products, arithmetic and copies ran while one was open for 15% of the time, Pallas kernels for 6%

profile of v2, /device:TPU:0, one launch (start us, length us, event | category | flops | bytes accessed | tf_op | source)
XLA Modules:
  0.0 189.1 jit_solution(11800669857833524241)
XLA Ops:
  0.6 1.4 copy.13
  2.0 3.0 %collective-permute-start = (bf16[128,2048]{0,1:T(8,128)(2,1)S(1)}, bf16[128,2048]{0,1:T(8,128)(2,1)S(1)}, u32[]{:S(2)}, u32[]{:S(2)}) collective-permute-start(bf16[128,2048]{0,1:T(8,128)(2,1)S(1)} %copy.13), channel_id=1, source_target_pairs={{0,1},{1,0},{2,3},{3,2},{4,5},{5,4},{6,7},{7,6},{8,9},{9,8},{10,11... | collective-permute-start | bytes 1572872 | tf_op jit(solution)/shard_map/ppermute | solution.py:229
  5.1 2.3 %fusion.97 = (bf16[1024,256]{1,0:T(8,128)(2,1)}, bf16[1024,256]{1,0:T(8,128)(2,1)}) fusion(bf16[2048,256]{1,0:T(8,128)(2,1)} %param.7), kind=kLoop, calls=%fused_computation.144 | loop fusion | bytes 2097152 | tf_op jit(solution)/shard_map/slice | solution.py:275
  7.3 1.5 collective-permute-start.9
  8.8 0.5 collective-permute-start.2
  9.4 7.6 %collective-permute-done = bf16[128,2048]{0,1:T(8,128)(2,1)S(1)} collective-permute-done((bf16[128,2048]{0,1:T(8,128)(2,1)S(1)}, bf16[128,2048]{0,1:T(8,128)(2,1)S(1)}, u32[]{:S(2)}, u32[]{:S(2)}) %collective-permute-start) | collective-permute-done | bytes 524320 | tf_op jit(solution)/shard_map/ppermute | solution.py:229
  17.0 0.7 constant_dynamic-slice_fusion.3
  17.7 0.8 pad_maximum_fusion.1
  18.6 0.7 abs_reduce_fusion
  19.9 0.3 copy.15
  20.3 1.4 rev.3
  22.0 0.4 copy.16
  22.4 0.9 concatenate.18
  23.4 6.3 %all-to-all-start.1 = ((f16[16,144,128]{2,1,0:T(8,128)(2,1)}), f16[16,144,128]{2,1,0:T(8,128)(2,1)S(1)}, u32[]{:S(2)}, u32[]{:S(2)}) async-start(f16[16,144,128]{2,1,0:T(8,128)(2,1)} %concatenate.18), calls=%async_computation.1 | async-start | bytes 1179648 | tf_op jit(solution)/shard_map/all_to_all | solution.py:309
  30.5 1.8 collective-permute-start.10
  32.6 1.2 pad_maximum_fusion
  33.7 1.4 fusion.22
  35.1 0.3 convolution_add_fusion.6
  35.4 1.4 fusion.38
  36.8 0.3 convolution_add_fusion.20
  37.1 1.4 fusion.30
  38.5 1.3 fusion.46
  40.5 13.0 %collective-permute-done.10 = bf16[1024,256]{1,0:T(8,128)(2,1)S(1)} collective-permute-done((bf16[1024,256]{1,0:T(8,128)(2,1)}, bf16[1024,256]{1,0:T(8,128)(2,1)S(1)}, u32[]{:S(2)}, u32[]{:S(2)}) %collective-permute-start.10) | collective-permute-done | bytes 524320 | tf_op jit(solution)/shard_map/ppermute | solution.py:292
  53.8 0.3 convolution_add_fusion.19
  54.2 4.7 %collective-permute-start.4 = (bf16[1024,256]{1,0:T(8,128)(2,1)S(1)}, bf16[1024,256]{1,0:T(8,128)(2,1)S(1)}, u32[]{:S(2)}, u32[]{:S(2)}) collective-permute-start(bf16[1024,256]{1,0:T(8,128)(2,1)S(1)} %collective-permute-done.3), channel_id=1, source_target_pairs={{0,8},{2,10},{8,16},{10,18},{16,24},{18,26},{24,28},{26,30},{28,20... | collective-permute-start | bytes 1572872 | tf_op jit(solution)/shard_map/ppermute | solution.py:292
  59.2 0.3 convolution_add_fusion.26
  59.6 10.4 %collective-permute-done.11 = bf16[1024,256]{1,0:T(8,128)(2,1)S(1)} collective-permute-done((bf16[1024,256]{1,0:T(8,128)(2,1)S(1)}, bf16[1024,256]{1,0:T(8,128)(2,1)S(1)}, u32[]{:S(2)}, u32[]{:S(2)}) %collective-permute-start.11) | collective-permute-done | bytes 524320 | tf_op jit(solution)/shard_map/ppermute | solution.py:292
  70.6 2.1 %collective-permute-start.5 = (bf16[1024,256]{1,0:T(8,128)(2,1)S(1)}, bf16[1024,256]{1,0:T(8,128)(2,1)S(1)}, u32[]{:S(2)}, u32[]{:S(2)}) collective-permute-start(bf16[1024,256]{1,0:T(8,128)(2,1)S(1)} %collective-permute-done.4), channel_id=1, source_target_pairs={{0,8},{2,10},{8,16},{10,18},{16,24},{18,26},{24,28},{26,30},{28,20... | collective-permute-start | bytes 1572872 | tf_op jit(solution)/shard_map/ppermute | solution.py:292
  73.3 9.5 %collective-permute-done.12 = bf16[1024,256]{1,0:T(8,128)(2,1)S(1)} collective-permute-done((bf16[1024,256]{1,0:T(8,128)(2,1)S(1)}, bf16[1024,256]{1,0:T(8,128)(2,1)S(1)}, u32[]{:S(2)}, u32[]{:S(2)}) %collective-permute-start.12) | collective-permute-done | bytes 524320 | tf_op jit(solution)/shard_map/ppermute | solution.py:292
  83.1 0.3 convolution_add_fusion.3
  83.4 0.3 convolution_add_fusion.17
  83.7 1.8 collective-permute-start.6
  85.9 0.3 convolution_add_fusion.24
  86.2 8.7 %collective-permute-done.13 = bf16[1024,256]{1,0:T(8,128)(2,1)S(1)} collective-permute-done((bf16[1024,256]{1,0:T(8,128)(2,1)S(1)}, bf16[1024,256]{1,0:T(8,128)(2,1)S(1)}, u32[]{:S(2)}, u32[]{:S(2)}) %collective-permute-start.13) | collective-permute-done | bytes 524320 | tf_op jit(solution)/shard_map/ppermute | solution.py:292
  94.9 0.4 collective-permute-start.14
  96.0 1.6 collective-permute-start.7
  98.3 8.7 %collective-permute-done.14 = bf16[1024,256]{1,0:T(8,128)(2,1)S(1)} collective-permute-done((bf16[1024,256]{1,0:T(8,128)(2,1)S(1)}, bf16[1024,256]{1,0:T(8,128)(2,1)S(1)}, u32[]{:S(2)}, u32[]{:S(2)}) %collective-permute-start.14) | collective-permute-done | bytes 524320 | tf_op jit(solution)/shard_map/ppermute | solution.py:292
  107.0 0.4 collective-permute-start.15
  107.4 0.7 collective-permute-done.7
  108.1 1.6 collective-permute-start.8
  110.0 0.3 convolution_add_fusion.15
  110.7 6.5 %collective-permute-done.15 = bf16[1024,256]{1,0:T(8,128)(2,1)S(1)} collective-permute-done((bf16[1024,256]{1,0:T(8,128)(2,1)S(1)}, bf16[1024,256]{1,0:T(8,128)(2,1)S(1)}, u32[]{:S(2)}, u32[]{:S(2)}) %collective-permute-start.15) | collective-permute-done | bytes 524320 | tf_op jit(solution)/shard_map/ppermute | solution.py:292
  117.6 0.7 collective-permute-done.8
  118.7 0.3 convolution_add_fusion.22
  119.1 0.5 collective-permute-done.17.refs_3_
  119.5 1.1 fusion.98
  120.7 1.1 fusion.99
  121.8 1.1 seq_grad.1
  122.9 3.9 %all-to-all-start = ((f32[16,128,128]{2,1,0:T(8,128)}), f32[16,128,128]{2,1,0:T(8,128)S(1)}, u32[]{:S(2)}, u32[]{:S(2)}) async-start(f32[16,128,128]{2,1,0:T(8,128)} %seq_grad.1), calls=%async_computation | async-start | bytes 2097152 | tf_op jit(solution)/shard_map/all_to_all | solution.py:309
  126.9 0.7 broadcast_in_dim.2.filter_ref
  127.6 7.0 %toeplitz.1.t_ref = bf16[8,256,2176]{2,1,0:T(8,128)(2,1)} custom-call(f32[8,1,2176]{2,1,0:T(1,128)} %broadcast_in_dim.2.filter_ref), custom_call_target="tpu_custom_call" | custom-call | flops 8912896 | bytes 8982528 | tf_op jit(solution)/shard_map/toeplitz/pallas_call | solution.py:35
  134.8 0.7 fusion.1.x_ref
  135.4 2.4 %stack_input.1.left_ref = bf16[8,256,256]{2,1,0:T(8,128)(2,1)S(1)} custom-call(f32[16,128,128]{2,1,0:T(8,128)S(1)} %fusion.1.x_ref), custom_call_target="tpu_custom_call" | custom-call | flops 2097152 | bytes 2097152 | tf_op jit(solution)/shard_map/stack_input/pallas_call | solution.py:68
  137.8 11.9 %all-to-all-done.s_ref = f32[16,128,128]{2,1,0:T(8,128)S(1)} async-done(((f32[16,128,128]{2,1,0:T(8,128)}), f32[16,128,128]{2,1,0:T(8,128)S(1)}, u32[]{:S(2)}, u32[]{:S(2)}) %all-to-all-start) | async-done | bytes 1048608 | tf_op jit(solution)/shard_map/all_to_all | solution.py:309
  149.7 11.4 %convolve.1 = f32[16,144,128]{2,1,0:T(8,128)S(1)} custom-call(f32[16,128,128]{2,1,0:T(8,128)S(1)} %all-to-all-done.s_ref, bf16[8,256,256]{2,1,0:T(8,128)(2,1)S(1)} %stack_input.1.left_ref, bf16[8,256,2176]{2,1,0:T(8,128)(2,1)} %toeplitz.1.t_ref), custom_call_target="tpu_custom_call" | custom-call | flops 7985954816 | bytes 12058624 | tf_op jit(solution)/shard_map/convolve/pallas_call | solution.py:185
  161.1 0.9 convert_element_type.26
  162.0 6.9 %all-to-all-start.2 = ((f16[16,144,128]{2,1,0:T(8,128)(2,1)}), f16[16,144,128]{2,1,0:T(8,128)(2,1)S(1)}, u32[]{:S(2)}, u32[]{:S(2)}) async-start(f16[16,144,128]{2,1,0:T(8,128)(2,1)} %convert_element_type.26), calls=%async_computation.2 | async-start | bytes 1179648 | tf_op jit(solution)/shard_map/all_to_all | solution.py:309
  168.9 2.3 %maximum_multiply_fusion = f32[128,2048]{1,0:T(8,128)} fusion(f32[128,2048]{1,0:T(8,128)} %param.9, f32[128,1024]{1,0:T(8,128)S(1)} %copy-done.5, f32[128,1024]{1,0:T(8,128)S(1)} %copy-done.6), kind=kLoop, calls=%fused_computation.45 | loop fusion | flops 524288 | bytes 3145728 | tf_op jit(solution)/shard_map/mul | solution.py:322
  171.2 13.2 %all-to-all-done.2 = f16[16,144,128]{2,1,0:T(8,128)(2,1)S(1)} async-done(((f16[16,144,128]{2,1,0:T(8,128)(2,1)}), f16[16,144,128]{2,1,0:T(8,128)(2,1)S(1)}, u32[]{:S(2)}, u32[]{:S(2)}) %all-to-all-start.2) | async-done | bytes 589856 | tf_op jit(solution)/shard_map/all_to_all | solution.py:309
  184.7 0.6 copy-done.4
  185.3 0.6 fusion.6
  185.9 0.3 copy.17
  186.3 1.3 copy.18
  187.6 1.5 fusion.13
  (54 shorter events, 6.9 us)
Async XLA Ops:
  0.6 126.2 %copy-start = (f32[128,2048]{1,0:T(8,128)S(1)}, f32[128,2048]{1,0:T(8,128)}, u32[]{:S(2)}) copy-start(f32[128,2048]{1,0:T(8,128)} %param.11) | copy-start | bytes 3145732
  2.0 14.9 %collective-permute-start = (bf16[128,2048]{0,1:T(8,128)(2,1)S(1)}, bf16[128,2048]{0,1:T(8,128)(2,1)S(1)}, u32[]{:S(2)}, u32[]{:S(2)}) collective-permute-start(bf16[128,2048]{0,1:T(8,128)(2,1)S(1)} %copy.13), channel_id=1, source_target_pairs={{0,1},{1,0},{2,3},{3,2},{4,5},{5,4},{6,7},{7,6},{8,9},{9,8},{10,11... | collective-permute-start | bytes 1572872 | tf_op jit(solution)/shard_map/ppermute | solution.py:229
  7.3 11.3 %copy-start.3 = (f32[128,2048]{1,0:T(8,128)S(1)}, f32[128,2048]{1,0:T(8,128)}, u32[]{:S(2)}) copy-start(f32[128,2048]{1,0:T(8,128)} %param.10) | copy-start | bytes 3145732
  7.3 23.2 %collective-permute-start.9 = (bf16[1024,256]{1,0:T(8,128)(2,1)}, bf16[1024,256]{1,0:T(8,128)(2,1)}, u32[]{:S(2)}, u32[]{:S(2)}) collective-permute-start(bf16[1024,256]{1,0:T(8,128)(2,1)} %get-tuple-element.11), channel_id=1, source_target_pairs={{8,0},{10,2},{16,8},{18,10},{24,16},{26,18},{28,24},{30,26},{20,28... | collective-permute-start | bytes 1572872 | tf_op jit(solution)/shard_map/ppermute | solution.py:292
  8.8 23.4 %collective-permute-start.2 = (bf16[1024,256]{1,0:T(8,128)(2,1)}, bf16[1024,256]{1,0:T(8,128)(2,1)}, u32[]{:S(2)}, u32[]{:S(2)}) collective-permute-start(bf16[1024,256]{1,0:T(8,128)(2,1)} %get-tuple-element.12), channel_id=1, source_target_pairs={{0,8},{2,10},{8,16},{10,18},{16,24},{18,26},{24,28},{26,30},{28,20... | collective-permute-start | bytes 1572872 | tf_op jit(solution)/shard_map/ppermute | solution.py:292
  18.6 14.0 %collective-permute-start.1 = (bf16[128,2048]{0,1:T(8,128)(2,1)}, bf16[128,2048]{0,1:T(8,128)(2,1)}, u32[]{:S(2)}, u32[]{:S(2)}) collective-permute-start(bf16[128,2048]{0,1:T(8,128)(2,1)} %pad_maximum_fusion.1), channel_id=1, source_target_pairs={{0,2},{2,0},{4,6},{6,4},{8,10},{10,8},{12,14},{14,12},{16,18},{18,... | collective-permute-start | bytes 1572872 | tf_op jit(solution)/shard_map/ppermute | solution.py:235
  22.0 10.6 %copy-start.7 = (bf16[128,4,1,256]{0,3,2,1:T(8,128)(2,1)S(1)}, bf16[128,4,1,256]{0,3,2,1:T(8,128)(2,1)}, u32[]{:S(2)}) copy-start(bf16[128,4,1,256]{0,3,2,1:T(8,128)(2,1)} %get-tuple-element.15) | copy-start | bytes 786436
  23.4 99.6 %all-to-all-start.1 = ((f16[16,144,128]{2,1,0:T(8,128)(2,1)}), f16[16,144,128]{2,1,0:T(8,128)(2,1)S(1)}, u32[]{:S(2)}, u32[]{:S(2)}) async-start(f16[16,144,128]{2,1,0:T(8,128)(2,1)} %concatenate.18), calls=%async_computation.1 | async-start | bytes 1179648 | tf_op jit(solution)/shard_map/all_to_all | solution.py:309
  29.9 5.2 %copy-start.2 = (bf16[2048,256]{1,0:T(8,128)(2,1)S(1)}, bf16[2048,256]{1,0:T(8,128)(2,1)}, u32[]{:S(2)}) copy-start(bf16[2048,256]{1,0:T(8,128)(2,1)} %param.7) | copy-start | bytes 3145732
  30.5 23.0 %collective-permute-start.10 = (bf16[1024,256]{1,0:T(8,128)(2,1)}, bf16[1024,256]{1,0:T(8,128)(2,1)S(1)}, u32[]{:S(2)}, u32[]{:S(2)}) collective-permute-start(bf16[1024,256]{1,0:T(8,128)(2,1)} %collective-permute-done.9), channel_id=1, source_target_pairs={{8,0},{10,2},{16,8},{18,10},{24,16},{26,18},{28,24},{30,26},{20,28... | collective-permute-start | bytes 1572872 | tf_op jit(solution)/shard_map/ppermute | solution.py:292
  32.3 21.9 %collective-permute-start.3 = (bf16[1024,256]{1,0:T(8,128)(2,1)}, bf16[1024,256]{1,0:T(8,128)(2,1)S(1)}, u32[]{:S(2)}, u32[]{:S(2)}) collective-permute-start(bf16[1024,256]{1,0:T(8,128)(2,1)} %collective-permute-done.2), channel_id=1, source_target_pairs={{0,8},{2,10},{8,16},{10,18},{16,24},{18,26},{24,28},{26,30},{28,20... | collective-permute-start | bytes 1572872 | tf_op jit(solution)/shard_map/ppermute | solution.py:292
  53.5 16.4 %collective-permute-start.11 = (bf16[1024,256]{1,0:T(8,128)(2,1)S(1)}, bf16[1024,256]{1,0:T(8,128)(2,1)S(1)}, u32[]{:S(2)}, u32[]{:S(2)}) collective-permute-start(bf16[1024,256]{1,0:T(8,128)(2,1)S(1)} %collective-permute-done.10), channel_id=1, source_target_pairs={{8,0},{10,2},{16,8},{18,10},{24,16},{26,18},{28,24},{30,26},{20,28... | collective-permute-start | bytes 1572872 | tf_op jit(solution)/shard_map/ppermute | solution.py:292
  54.2 16.4 %collective-permute-start.4 = (bf16[1024,256]{1,0:T(8,128)(2,1)S(1)}, bf16[1024,256]{1,0:T(8,128)(2,1)S(1)}, u32[]{:S(2)}, u32[]{:S(2)}) collective-permute-start(bf16[1024,256]{1,0:T(8,128)(2,1)S(1)} %collective-permute-done.3), channel_id=1, source_target_pairs={{0,8},{2,10},{8,16},{10,18},{16,24},{18,26},{24,28},{26,30},{28,20... | collective-permute-start | bytes 1572872 | tf_op jit(solution)/shard_map/ppermute | solution.py:292
  69.9 12.9 %collective-permute-start.12 = (bf16[1024,256]{1,0:T(8,128)(2,1)S(1)}, bf16[1024,256]{1,0:T(8,128)(2,1)S(1)}, u32[]{:S(2)}, u32[]{:S(2)}) collective-permute-start(bf16[1024,256]{1,0:T(8,128)(2,1)S(1)} %collective-permute-done.11), channel_id=1, source_target_pairs={{8,0},{10,2},{16,8},{18,10},{24,16},{26,18},{28,24},{30,26},{20,28... | collective-permute-start | bytes 1572872 | tf_op jit(solution)/shard_map/ppermute | solution.py:292
  70.6 13.2 %collective-permute-start.5 = (bf16[1024,256]{1,0:T(8,128)(2,1)S(1)}, bf16[1024,256]{1,0:T(8,128)(2,1)S(1)}, u32[]{:S(2)}, u32[]{:S(2)}) collective-permute-start(bf16[1024,256]{1,0:T(8,128)(2,1)S(1)} %collective-permute-done.4), channel_id=1, source_target_pairs={{0,8},{2,10},{8,16},{10,18},{16,24},{18,26},{24,28},{26,30},{28,20... | collective-permute-start | bytes 1572872 | tf_op jit(solution)/shard_map/ppermute | solution.py:292
  82.8 12.1 %collective-permute-start.13 = (bf16[1024,256]{1,0:T(8,128)(2,1)S(1)}, bf16[1024,256]{1,0:T(8,128)(2,1)S(1)}, u32[]{:S(2)}, u32[]{:S(2)}) collective-permute-start(bf16[1024,256]{1,0:T(8,128)(2,1)S(1)} %collective-permute-done.12), channel_id=1, source_target_pairs={{8,0},{10,2},{16,8},{18,10},{24,16},{26,18},{28,24},{30,26},{20,28... | collective-permute-start | bytes 1572872 | tf_op jit(solution)/shard_map/ppermute | solution.py:292
  83.7 12.2 %collective-permute-start.6 = (bf16[1024,256]{1,0:T(8,128)(2,1)S(1)}, bf16[1024,256]{1,0:T(8,128)(2,1)S(1)}, u32[]{:S(2)}, u32[]{:S(2)}) collective-permute-start(bf16[1024,256]{1,0:T(8,128)(2,1)S(1)} %collective-permute-done.5), channel_id=1, source_target_pairs={{0,8},{2,10},{8,16},{10,18},{16,24},{18,26},{24,28},{26,30},{28,20... | collective-permute-start | bytes 1572872 | tf_op jit(solution)/shard_map/ppermute | solution.py:292
  94.9 12.1 %collective-permute-start.14 = (bf16[1024,256]{1,0:T(8,128)(2,1)S(1)}, bf16[1024,256]{1,0:T(8,128)(2,1)S(1)}, u32[]{:S(2)}, u32[]{:S(2)}) collective-permute-start(bf16[1024,256]{1,0:T(8,128)(2,1)S(1)} %collective-permute-done.13), channel_id=1, source_target_pairs={{8,0},{10,2},{16,8},{18,10},{24,16},{26,18},{28,24},{30,26},{20,28... | collective-permute-start | bytes 1572872 | tf_op jit(solution)/shard_map/ppermute | solution.py:292
  96.0 12.1 %collective-permute-start.7 = (bf16[1024,256]{1,0:T(8,128)(2,1)S(1)}, bf16[1024,256]{1,0:T(8,128)(2,1)S(1)}, u32[]{:S(2)}, u32[]{:S(2)}) collective-permute-start(bf16[1024,256]{1,0:T(8,128)(2,1)S(1)} %collective-permute-done.6), channel_id=1, source_target_pairs={{0,8},{2,10},{8,16},{10,18},{16,24},{18,26},{24,28},{26,30},{28,20... | collective-permute-start | bytes 1572872 | tf_op jit(solution)/shard_map/ppermute | solution.py:292
  107.0 10.3 %collective-permute-start.15 = (bf16[1024,256]{1,0:T(8,128)(2,1)S(1)}, bf16[1024,256]{1,0:T(8,128)(2,1)S(1)}, u32[]{:S(2)}, u32[]{:S(2)}) collective-permute-start(bf16[1024,256]{1,0:T(8,128)(2,1)S(1)} %collective-permute-done.14), channel_id=1, source_target_pairs={{8,0},{10,2},{16,8},{18,10},{24,16},{26,18},{28,24},{30,26},{20,28... | collective-permute-start | bytes 1572872 | tf_op jit(solution)/shard_map/ppermute | solution.py:292
  108.1 10.2 %collective-permute-start.8 = (bf16[1024,256]{1,0:T(8,128)(2,1)S(1)}, bf16[1024,256]{1,0:T(8,128)(2,1)S(1)}, u32[]{:S(2)}, u32[]{:S(2)}) collective-permute-start(bf16[1024,256]{1,0:T(8,128)(2,1)S(1)} %collective-permute-done.7), channel_id=1, source_target_pairs={{0,8},{2,10},{8,16},{10,18},{16,24},{18,26},{24,28},{26,30},{28,20... | collective-permute-start | bytes 1572872 | tf_op jit(solution)/shard_map/ppermute | solution.py:292
  117.6 2.0 %collective-permute-start.17 = (f32[128,1024]{1,0:T(8,128)S(1)}, f32[128,1024]{1,0:T(8,128)S(1)}, u32[]{:S(2)}, u32[]{:S(2)}) collective-permute-start(f32[128,1024]{1,0:T(8,128)S(1)} %convolution_add_fusion), channel_id=1, source_target_pairs={{0,2},{2,0},{4,6},{6,4},{8,10},{10,8},{12,14},{14,12},{16,18},{18,... | collective-permute-start | bytes 1572872 | tf_op jit(solution)/shard_map/ppermute | solution.py:294
  118.6 2.0 %collective-permute-start.16 = (f32[128,1024]{1,0:T(8,128)S(1)}, f32[128,1024]{1,0:T(8,128)S(1)}, u32[]{:S(2)}, u32[]{:S(2)}) collective-permute-start(f32[128,1024]{1,0:T(8,128)S(1)} %convolution_add_fusion.7), channel_id=1, source_target_pairs={{0,2},{2,0},{4,6},{6,4},{8,10},{10,8},{12,14},{14,12},{16,18},{18,... | collective-permute-start | bytes 1572872 | tf_op jit(solution)/shard_map/ppermute | solution.py:294
  119.0 2.7 %copy-start.1 = (f32[128,2048]{1,0:T(8,128)S(1)}, f32[128,2048]{1,0:T(8,128)}, u32[]{:S(2)}) copy-start(f32[128,2048]{1,0:T(8,128)} %refs_4_.1) | copy-start | bytes 3145732
  122.9 26.8 %all-to-all-start = ((f32[16,128,128]{2,1,0:T(8,128)}), f32[16,128,128]{2,1,0:T(8,128)S(1)}, u32[]{:S(2)}, u32[]{:S(2)}) async-start(f32[16,128,128]{2,1,0:T(8,128)} %seq_grad.1), calls=%async_computation | async-start | bytes 2097152 | tf_op jit(solution)/shard_map/all_to_all | solution.py:309
  161.1 7.8 %copy-start.5 = (f32[128,1024]{1,0:T(8,128)S(1)}, f32[128,1024]{1,0:T(8,128)}, u32[]{:S(2)}) copy-start(f32[128,1024]{1,0:T(8,128)} %get-tuple-element.17) | copy-start | bytes 1572868
  161.1 7.8 %copy-start.6 = (f32[128,1024]{1,0:T(8,128)S(1)}, f32[128,1024]{1,0:T(8,128)}, u32[]{:S(2)}) copy-start(f32[128,1024]{1,0:T(8,128)} %get-tuple-element.19) | copy-start | bytes 1572868
  162.0 22.4 %all-to-all-start.2 = ((f16[16,144,128]{2,1,0:T(8,128)(2,1)}), f16[16,144,128]{2,1,0:T(8,128)(2,1)S(1)}, u32[]{:S(2)}, u32[]{:S(2)}) async-start(f16[16,144,128]{2,1,0:T(8,128)(2,1)} %convert_element_type.26), calls=%async_computation.2 | async-start | bytes 1179648 | tf_op jit(solution)/shard_map/all_to_all | solution.py:309
  184.4 0.9 copy-start.4

commit v3 on v2

--- a/solution.py
+++ b/solution.py
@@ -10,9 +10,12 @@
 
 LANES = 128
 ROW_TILE = 16
+GRANT = 60 * 1024 * 1024
 CODE_UNIT = 8192.0
 SMALLEST = 1e-30
 VMEM = pl.BlockSpec(memory_space=pltpu.VMEM)
+SMEM = pl.BlockSpec(memory_space=pltpu.SMEM)
+ANY = pl.BlockSpec(memory_space=pl.ANY)
 
 
 def split(value):
@@ -57,9 +60,14 @@
         x_hi[:, at, :] = high.reshape(groups, per, tok)
         x_lo[:, at, :] = low.reshape(groups, per, tok)
 
+    last = lax.broadcasted_iota(jnp.int32, (tok, tok), 0) + lax.broadcasted_iota(jnp.int32, (tok, tok), 1)
+    turn = jnp.where(last == tok - 1, 1.0, 0.0).astype(jnp.bfloat16)
+
     @pl.loop(0, groups)
     def _(g):
-        left_ref[g] = jnp.concatenate([x_hi[g], x_lo[g]], axis=1).T
+        for half, ref in ((0, x_hi), (1, x_lo)):
+            turned = lax.dot_general(turn, ref[g], (((1,), (1,)), ((), ())), preferred_element_type=jnp.float32)
+            left_ref[g, half * tok : (half + 1) * tok, :] = turned.astype(jnp.bfloat16)
 
 
 def stack_input(input_blocks, groups, per):
@@ -95,7 +103,7 @@
 
 
 def conv_kernel(scale, lag_own, s_ref, left_ref, t_ref, out_ref, s_hi, s_lo, grads, cross, lag_sums):
-    blocks, tok, _ = s_ref.shape
+    blocks, tok = 2 * s_ref.shape[0] * s_ref.shape[1], s_ref.shape[3]
     groups, rows, _ = grads.shape
     per = rows // blocks
     width = t_ref.shape[2]
@@ -108,7 +116,8 @@
         s_hi[:, rows:, :] = jnp.zeros_like(s_hi[:, rows:, :])
         s_lo[:, rows:, :] = jnp.zeros_like(s_lo[:, rows:, :])
         for a in range(blocks):
-            high, low = split(s_ref[a].T[: groups * per])
+            z, rest = divmod(a, s_ref.shape[1])
+            high, low = split(s_ref[z // 2, rest, z % 2].T[: groups * per])
             s_hi[:, a * per : (a + 1) * per, :] = high.reshape(groups, per, tok)
             s_lo[:, a * per : (a + 1) * per, :] = low.reshape(groups, per, tok)
 
@@ -165,7 +174,7 @@
 
 
 def convolve(seq_blocks, input_blocks, moved, channels, lag_own, scale):
-    blocks, tok, own = seq_blocks.shape
+    blocks, tok, own = input_blocks.shape
     groups, _, width = moved.shape
     per = -(-channels // ROW_TILE) * ROW_TILE
     if groups * per != LANES or channels != per:
@@ -173,9 +182,10 @@
         lanes = -(-wide // LANES) * LANES
 
         def widen(v):
-            v = v.reshape(blocks, tok, groups, channels)
-            v = jnp.pad(v, ((0, 0), (0, 0), (0, 0), (0, per - channels))).reshape(blocks, tok, wide)
-            return jnp.pad(v, ((0, 0), (0, 0), (0, lanes - wide)))
+            shape = v.shape[:-1]
+            v = v.reshape(-1, groups, channels)
+            v = jnp.pad(v, ((0, 0), (0, 0), (0, per - channels))).reshape(-1, wide)
+            return jnp.pad(v, ((0, 0), (0, lanes - wide))).reshape(shape + (lanes,))
 
         seq_blocks, input_blocks = widen(seq_blocks), widen(input_blocks)
     rows = blocks * per
@@ -186,7 +196,7 @@
         functools.partial(conv_kernel, scale, lag_own),
         grid=(groups,),
         in_specs=[
-            pl.BlockSpec(seq_blocks.shape, lambda g: (0, 0, 0)),
+            pl.BlockSpec(seq_blocks.shape, lambda g: (0, 0, 0, 0, 0)),
             pl.BlockSpec((1, 2 * tok, rows), lambda g: (g, 0, 0)),
             pl.BlockSpec((1, 2 * tok, width), lambda g: (g, 0, 0)),
         ],
@@ -208,126 +218,302 @@
     )(seq_blocks, left, moved)
 
 
-def ring_chip(place, chips):
-    place = lax.rem(place + chips, chips)
-    return jnp.where(place < chips // 2, 2 * place, 2 * (chips - 1 - place) + 1)
-
-
-def ring_pairs(chips, forward):
-    order = list(range(0, chips, 2)) + list(range(chips - 1, 0, -2))
-    pairs = [(2 * order[p] + k, 2 * order[(p + 1) % chips] + k) for p in range(chips) for k in range(2)]
-    return pairs if forward else [(b, a) for a, b in pairs]
-
-
-def pair_cotangent(cotangent, features):
+def nothing(*refs):
+    del refs
+
+
+def after(value, *earlier):
+    return pl.pallas_call(
+        nothing,
+        in_specs=[ANY] * (1 + len(earlier)),
+        out_specs=ANY,
+        out_shape=jax.ShapeDtypeStruct(value.shape, value.dtype),
+        input_output_aliases={0: 0},
+        cost_estimate=pl.CostEstimate(flops=0, bytes_accessed=0, transcendentals=0),
+        name="after",
+    )(value, *earlier)
+
+
+class Place:
+    def __init__(self):
+        self.devices = lax.axis_size("ctx")
+        self.ys = self.devices // 8
+        assert self.devices == 8 * self.ys
+        me = lax.axis_index("ctx")
+        self.core, chip = lax.rem(me, 2), me // 2
+        self.y, z = lax.rem(chip, self.ys), chip // self.ys
+        self.p, self.h = lax.rem(z, 2), z // 2
+        self.block = (self.h * self.ys + self.y) * 2 + self.core
+
+    def index(self, h, p, y, core):
+        return ((h * 2 + p) * self.ys + y) * 2 + core
+
+    def all(self):
+        return [(h, p, y, c) for h in range(2) for p in range(2) for y in range(self.ys) for c in range(2)]
+
+    def swap_core(self, v):
+        return lax.ppermute(v, "ctx", [(self.index(h, p, y, c), self.index(h, p, y, 1 - c)) for h, p, y, c in self.all()])
+
+    def swap_pair(self, v):
+        return lax.ppermute(v, "ctx", [(self.index(h, p, y, c), self.index(h, 1 - p, y, c)) for h, p, y, c in self.all()])
+
+    def swap_half(self, v):
+        return lax.ppermute(v, "ctx", [(self.index(h, p, y, c), self.index(1 - h, p, y, c)) for h, p, y, c in self.all()])
+
+    def swap_half_and_pair(self, v):
+        pairs = [(self.index(h, p, y, c), self.index(1 - h, 1 - p, y, c)) for h, p, y, c in self.all()]
+        return lax.ppermute(v, "ctx", pairs)
+
+    def along_y(self, v, shift):
+        ys = self.ys
+        return lax.ppermute(
+            v, "ctx", [(self.index(h, p, y, c), self.index(h, p, (y + shift) % ys, c)) for h, p, y, c in self.all()]
+        )
+
+    def same_p(self):
+        return [[self.index(h, p, y, c) for h in range(2) for y in range(self.ys) for c in range(2)] for p in range(2)]
+
+
+def pick_kernel(features, slots, core_ref, *refs):
+    parts, (mine_ref, theirs_ref) = refs[: 2 * slots], refs[-2:]
+    tok, held = parts[0].shape
+    first = core_ref[0] == 0
+    for row in range(2):
+        rows = slice(row * tok, (row + 1) * tok)
+        for s in range(slots):
+            part = parts[row * slots + s]
+            for b in range(held // (2 * features)):
+                even = part[:, 2 * b * features : (2 * b + 1) * features]
+                odd = part[:, (2 * b + 1) * features : (2 * b + 2) * features]
+                at = s * held // 2 + b * features
+                mine_ref[rows, at : at + features] = jnp.where(first, even, odd)
+                theirs_ref[rows, at : at + features] = jnp.where(first, odd, even)
+
+
+def gather_cotangent(cotangent, features, place, earlier):
     tok, held = cotangent.shape
     parts = lax.axis_size("ch")
-    core = lax.rem(lax.axis_index("ctx"), 2)
-    swap = [(i, i ^ 1) for i in range(lax.axis_size("ctx"))]
-    pieces = [cotangent]
-    for s in range(1, parts):
-        pieces.append(lax.ppermute(cotangent, "ch", [(j, (j + s) % parts) for j in range(parts)]))
-    mine, theirs = [], []
-    for piece in pieces:
-        blocks = piece.reshape(tok, held // (2 * features), 2, features)
-        mine.append(lax.dynamic_index_in_dim(blocks, core, 2, keepdims=False).reshape(tok, held // 2))
-        theirs.append(lax.dynamic_index_in_dim(blocks, 1 - core, 2, keepdims=False).reshape(tok, held // 2))
-    arrived = lax.ppermute(jnp.concatenate(theirs, axis=1), "ctx", swap)
-    return jnp.concatenate([jnp.concatenate(mine, axis=1), arrived], axis=0)
-
-
-def seq_kernel(*refs):
-    *parts, gate_ref, out_ref = refs
-    count = len(parts) // 2
-    blocks, tok, own = out_ref.shape
-    width = parts[0].shape[1]
+    far = place.swap_pair(cotangent)
+
+    def along_ch(v):
+        return [v] + [lax.ppermute(v, "ch", [(j, (j + s) % parts) for j in range(parts)]) for s in range(1, parts)]
+
+    whole = jax.ShapeDtypeStruct((2 * tok, parts * held // 2), cotangent.dtype)
+    mine, theirs = pl.pallas_call(
+        functools.partial(pick_kernel, features, parts),
+        in_specs=[SMEM] + [VMEM] * (2 * parts),
+        out_specs=[VMEM] * 2,
+        out_shape=[whole, whole],
+        compiler_params=pltpu.CompilerParams(vmem_limit_bytes=GRANT),
+        cost_estimate=pl.CostEstimate(flops=0, bytes_accessed=8 * tok * held * parts, transcendentals=0),
+        name="pick_features",
+    )(place.core.reshape(1), *along_ch(cotangent), *along_ch(far))
+    return mine, place.swap_core(after(theirs, *earlier))
+
+
+def seq_kernel(p_ref, sum_ref, arrived_ref, gate_ref, far_gate_ref, out_ref, near_ref, far_ref):
+    p = p_ref[0]
+    blocks, _, tok, own = out_ref.shape
+    near_ref[...] = sum_ref[:tok, :] + arrived_ref[:tok, :]
+    far_ref[...] = sum_ref[tok:, :] + arrived_ref[tok:, :]
+    near = near_ref[...] * gate_ref[...]
+    far = far_ref[...] * far_gate_ref[...]
     for b in range(blocks):
-        c, at = divmod(b * own, width)
-        grad_out = parts[c][:, at : at + own] + parts[count + c][:, at : at + own]
-        out_ref[b] = grad_out * gate_ref[:, b * own : (b + 1) * own]
-
-
-def seq_blocks_of(sums, arrived, gate_value, blocks):
+        out_ref[b, p] = near[:, b * own : (b + 1) * own]
+        out_ref[b, 1 - p] = far[:, b * own : (b + 1) * own]
+
+
+def seq_blocks_of(total, arrived, gate_value, far_gate, place):
     tok, channels = gate_value.shape
+    blocks = place.devices // 2
+    half = channels // 2
+    own = half // blocks
+    steps = max(1, min(4, half // LANES))
+    width, count = half // steps, blocks // steps
     return pl.pallas_call(
         seq_kernel,
-        in_specs=[VMEM] * (2 * len(sums) + 1),
-        out_specs=VMEM,
-        out_shape=jax.ShapeDtypeStruct((blocks, tok, channels // blocks), jnp.float32),
-        compiler_params=pltpu.CompilerParams(vmem_limit_bytes=32 * 1024 * 1024),
+        grid_spec=pltpu.PrefetchScalarGridSpec(
+            num_scalar_prefetch=1,
+            grid=(steps,),
+            in_specs=[
+                pl.BlockSpec((2 * tok, width), lambda i, p: (0, i)),
+                pl.BlockSpec((2 * tok, width), lambda i, p: (0, i)),
+                pl.BlockSpec((tok, width), lambda i, p: (0, p[0] * steps + i)),
+                pl.BlockSpec((tok, width), lambda i, p: (0, i)),
+            ],
+            out_specs=[
+                pl.BlockSpec((count, 2, tok, own), lambda i, p: (i, 0, 0, 0)),
+                pl.BlockSpec((tok, width), lambda i, p: (0, i)),
+                pl.BlockSpec((tok, width), lambda i, p: (0, i)),
+            ],
+        ),
+        out_shape=[
+            jax.ShapeDtypeStruct((blocks, 2, tok, own), jnp.float32),
+            jax.ShapeDtypeStruct((tok, half), jnp.float32),
+            jax.ShapeDtypeStruct((tok, half), jnp.float32),
+        ],
+        compiler_params=pltpu.CompilerParams(vmem_limit_bytes=GRANT),
         cost_estimate=pl.CostEstimate(
-            flops=2 * tok * channels, bytes_accessed=16 * tok * channels, transcendentals=0
+            flops=2 * tok * channels, bytes_accessed=24 * tok * channels, transcendentals=0
         ),
         name="seq_grad",
-    )(*sums, *arrived, gate_value)
-
-
-def project(cotangent, out_weight, chains):
-    tok = cotangent.shape[0]
-    channels, features = out_weight.shape
-    devices = lax.axis_size("ctx")
-    chips = devices // 2
-    parts = lax.axis_size("ch")
-    chip = lax.axis_index("ctx") // 2
-    place = jnp.where(chip % 2 == 0, chip // 2, chips - 1 - chip // 2)
-    both = pair_cotangent(cotangent, features)
-    rows = channels // chains
-    held = [out_weight[c * rows : (c + 1) * rows] for c in range(chains)]
-    sums = [[None, None] for _ in range(chains)]
-    chips_of_part = chips // parts
-    for step in range(chips):
-        for c in range(chains):
-            source = ring_chip(place - step if c % 2 == 0 else place + step, chips)
-            slot = lax.rem(lax.axis_index("ch") - source // chips_of_part + parts, parts)
-            column = (slot * chips_of_part + lax.rem(source, chips_of_part)) * features
-            for half in (1, 0):
-                term = lax.dot_general(
-                    lax.dynamic_slice(both, (half * tok, column), (tok, features)),
-                    held[c],
+    )(place.p.reshape(1), total, arrived, gate_value, far_gate)
+
+
+def share_kernel(columns_ref, mine_ref, theirs_ref, *refs):
+    shares, (own_ref, other_ref) = refs[:-2], refs[-2:]
+    rows, features = mine_ref.shape[0], shares[0].shape[1]
+    left = []
+    for s in range(len(shares)):
+        at = pl.ds(pl.multiple_of(columns_ref[s], features), features)
+        left.append(jnp.concatenate([mine_ref[:, at], theirs_ref[:, at]], axis=0))
+    term = lax.dot_general(
+        jnp.concatenate(left, axis=1),
+        jnp.concatenate([share[...] for share in shares], axis=1),
+        (((1,), (1,)), ((), ())),
+        preferred_element_type=jnp.float32,
+    )
+    own_ref[...] = term[:rows]
+    other_ref[...] = term[rows:]
+
+
+def add_shares(columns, mine, theirs, shares):
+    rows, (half, features) = mine.shape[0], shares[0].shape
+    if features % LANES:
+        sums = [0.0, 0.0]
+        for column, share in zip(columns, shares):
+            terms = [
+                lax.dot_general(
+                    lax.dynamic_slice_in_dim(v, column, features, 1),
+                    share,
                     (((1,), (1,)), ((), ())),
                     preferred_element_type=jnp.float32,
                 )
-                sums[c][half] = term if step == 0 else sums[c][half] + term
-        if step < chips - 1:
-            held = [lax.ppermute(v, "ctx", ring_pairs(chips, c % 2 == 0)) for c, v in enumerate(held)]
-    swap = [(i, i ^ 1) for i in range(devices)]
-    return [own for own, _ in sums], [lax.ppermute(other, "ctx", swap) for _, other in sums]
+                for v in (mine, theirs)
+            ]
+            sums = [a + b for a, b in zip(sums, terms)]
+        return sums
+    tile = min(256, half)
+    whole = jax.ShapeDtypeStruct((rows, half), jnp.float32)
+    return pl.pallas_call(
+        share_kernel,
+        grid=(half // tile,),
+        in_specs=[SMEM]
+        + [pl.BlockSpec(mine.shape, lambda n: (0, 0))] * 2
+        + [pl.BlockSpec((tile, features), lambda n: (n, 0))] * len(shares),
+        out_specs=[pl.BlockSpec((rows, tile), lambda n: (0, n))] * 2,
+        out_shape=[whole, whole],
+        compiler_params=pltpu.CompilerParams(vmem_limit_bytes=GRANT),
+        cost_estimate=pl.CostEstimate(
+            flops=4 * rows * half * len(shares) * features,
+            bytes_accessed=2 * (mine.size * 2 + half * len(shares) * features) + 16 * rows * half,
+            transcendentals=0,
+        ),
+        name="add_shares",
+    )(jnp.stack(columns), mine, theirs, *shares)
+
+
+def project(cotangent, out_weight, place, *waited):
+    channels, features = out_weight.shape
+    chips = place.devices // 2
+    parts = lax.axis_size("ch")
+    half = channels // 2
+    near = lax.dynamic_slice_in_dim(out_weight, place.p * half, half, 0)
+    given = lax.dynamic_slice_in_dim(out_weight, (1 - place.p) * half, half, 0)
+    far = place.swap_half(near)
+    paired = place.swap_pair(given)
+    far_paired = place.swap_half_and_pair(after(given, far))
+
+    def along_y(v):
+        return [v] + [place.along_y(v, shift) for shift in range(1, place.ys)]
+
+    held = [along_y(near)]
+    held.append(along_y(after(paired, *held[0][1:])))
+    held.append(along_y(far))
+    held.append(along_y(after(far_paired, *held[1][1:], *held[2][1:])))
+    mine, theirs = gather_cotangent(cotangent, features, place, [*held[3][1:], *waited])
+    chips_of_part = chips // parts
+
+    def column(other_h, other_p, shift):
+        h = 1 - place.h if other_h else place.h
+        p = 1 - place.p if other_p else place.p
+        source = (h * 2 + p) * place.ys + lax.rem(place.y - shift + place.ys, place.ys)
+        slot = lax.rem(lax.axis_index("ch") - source // chips_of_part + parts, parts)
+        return (slot * chips_of_part + lax.rem(source, chips_of_part)) * features
+
+    shares = [
+        (column(other // 2, other % 2, shift), held[other][shift]) for other in range(4) for shift in range(place.ys)
+    ]
+    own, other = add_shares([c for c, _ in shares], mine, theirs, [v for _, v in shares])
+    return own, place.swap_core(other), far_paired
+
+
+def code_kernel(x_ref, *refs):
+    out_ref = refs[-1]
+    devices, rows, own = out_ref.shape
+    tok = x_ref.shape[0]
+    code, exponent = coded(x_ref[...], largest(x_ref[...]))
+    quarter = devices // 4
+    for i in range(devices):
+        h, p, rest = i // (2 * quarter), i // quarter % 2, i % quarter
+        block = (p * 2 + h) * quarter + rest
+        out_ref[i, :tok, :] = code[:, block * own : (block + 1) * own]
+        out_ref[i, tok:, :] = jnp.broadcast_to(exponent, (rows - tok, own))
+
+
+def code_blocks(value, devices, *awaited):
+    tok, channels = value.shape
+    return pl.pallas_call(
+        code_kernel,
+        in_specs=[VMEM] + [ANY] * len(awaited),
+        out_specs=VMEM,
+        out_shape=jax.ShapeDtypeStruct((devices, tok + ROW_TILE, channels // devices), jnp.float32),
+        compiler_params=pltpu.CompilerParams(vmem_limit_bytes=32 * 1024 * 1024),
+        cost_estimate=pl.CostEstimate(flops=4 * tok * channels, bytes_accessed=8 * tok * channels, transcendentals=0),
+        name="code_input",
+    )(value, *awaited)
 
 
 def body(cotangent, out_weight, gate_value, conv_output, conv_input, filters):
     tok, channels = gate_value.shape
     all_groups, lags = filters.shape
-    devices = lax.axis_size("ctx")
+    place = Place()
+    devices = place.devices
     per_group = channels // all_groups
     own = channels // devices
+    half = channels // 2
     groups = max(1, own // per_group)
     share = max(1, per_group // own)
     lag_own = lags // devices
-    me = lax.axis_index("ctx")
-
-    def exchange(blocks):
-        return lax.all_to_all(blocks, "ctx", 0, 0, tiled=True)
-
-    code, exponent = coded(conv_input[::-1], largest(conv_input))
-    code = code.reshape(tok, devices, own).transpose(1, 0, 2)
-    code = jnp.concatenate([code, jnp.broadcast_to(exponent, (devices, ROW_TILE, own))], axis=1)
-    code = exchange(code.astype(jnp.float16))
+
+    def exchange(blocks, groups=None):
+        return lax.all_to_all(blocks, "ctx", 0, 0, tiled=True, axis_index_groups=groups)
+
+    def reorder(blocks):
+        return blocks.reshape((2, 2, devices // 4) + blocks.shape[1:]).swapaxes(0, 1).reshape(blocks.shape)
+
+    far_gate = place.swap_pair(lax.dynamic_slice_in_dim(gate_value, (1 - place.p) * half, half, 1))
+    total, arrived, late = project(cotangent, out_weight, place, far_gate)
+    code = exchange(code_blocks(conv_input, devices, late).astype(jnp.float16))
     input_blocks = decoded(code[:, :tok], code[:, tok : tok + 1, :1])
-    own_filters = lax.dynamic_slice_in_dim(filters, me * own // per_group, groups, 0)
-    moved = toeplitz(own_filters, tok)
-
-    sums, arrived = project(cotangent, out_weight, 2)
-    seq_blocks = exchange(seq_blocks_of(sums, arrived, gate_value, devices))
-    grad_out = jnp.concatenate([a + b for a, b in zip(sums, arrived)], axis=1)
-    gate_grad = grad_out * conv_output
+    first_group = (place.p * half + place.block * own) // per_group
+    moved = toeplitz(lax.dynamic_slice_in_dim(filters, first_group, groups, 0), tok)
+
+    seq_blocks, near, far = seq_blocks_of(total, arrived, gate_value, far_gate, place)
+    seq_blocks = exchange(seq_blocks, place.same_p())
+    seq_blocks = seq_blocks.reshape(2, devices // 4, 2, tok, own)
+    far = place.swap_pair(far)
+    left = jnp.where(place.p == 0, near, far)
+    right = jnp.where(place.p == 0, far, near)
+    gate_grad = jnp.concatenate([left, right], axis=1) * conv_output
 
     scale = 1.0 / math.sqrt(per_group * tok * devices)
     result = convolve(seq_blocks, input_blocks, moved, min(own, per_group), lag_own, scale)
     back = exchange(result[:, :, : max(own, lag_own)].astype(jnp.float16))
     held = back.shape[1] - 8
-    input_grad = decoded(back[:, :tok, :own], back[:, held : held + 1, :1])
+    input_grad = reorder(decoded(back[:, :tok, :own], back[:, held : held + 1, :1]))
     input_grad = input_grad.transpose(1, 0, 2).reshape(tok, channels)
-    filter_grad = decoded(back[:, tok : tok + groups, :lag_own], back[:, held + 1 : held + 2, :1])
+    filter_grad = reorder(decoded(back[:, tok : tok + groups, :lag_own], back[:, held + 1 : held + 2, :1]))
     filter_grad = filter_grad.reshape(all_groups, share, lag_own).sum(axis=1)
     return (input_grad, gate_grad, filter_grad)
 

time: 190 us -> 161 us (0.85)
  waiting for transfers between devices: 91.5 us -> 68.3 us
  matrix products: 15.9 us -> 0 us
  Pallas kernels: 21.9 us -> 35.6 us
  local copies, waits for them, and re-layouts: 10.6 us -> 14.6 us
  other arithmetic: 9.28 us -> 6.1 us
  starting transfers between devices: 37.3 us -> 34.3 us
    ppermute x18 -> x14, waiting for transfers between devices: 66.3 us -> 42.9 us  [the longest x4 21.2 us: swap_pair(): lax.ppermute(v, 'ctx', [(self.index(h, p, y, c), self.index(h, 1 - p, y,...]
    dot_general x32 -> x0, matrix products: 15.9 us -> none  [project(): lax.dot_general(lax.dynamic_slice(both, (half * tok, column), (tok, featu...]
    pallas_call x1 -> x8, Pallas kernels: 1.14 us -> 14 us  [the longest x1 6.66 us: add_shares(): pl.pallas_call(share_kernel, grid=(half // tile,), in_specs=[SMEM] + [pl....]
    unnamed x19 -> x29, local copies, waits for them, and re-layouts: 3.71 us -> 9.19 us
    all_to_all x3, starting transfers between devices: 17.1 us -> 12.4 us  [exchange(): lax.all_to_all(blocks, 'ctx', 0, 0, tiled=True, axis_index_groups=groups)]
    slice x1 -> x0, local copies, waits for them, and re-layouts: 2.26 us -> none  [project(): held = [out_weight[c * rows:(c + 1) * rows] for c in range(chains)]]
    dynamic_slice x3, local copies, waits for them, and re-layouts: 0.79 us -> 3.02 us  [the longest x1 2.14 us: project(): near = lax.dynamic_slice_in_dim(out_weight, place.p * half, half, 0)]
    concatenate x2 -> x0, other arithmetic: 2 us -> none  [the longest x1 1.16 us: pair_cotangent(): return jnp.concatenate([jnp.concatenate(mine, axis=1), arrived], axis=0)]
  transfers between devices with their start and end apart: 21 -> 17, of which waited for: 12 -> 10; matrix products, arithmetic and copies ran while one was open for 15% -> 5% of each run, Pallas kernels for 6% -> 22%
where the time goes in v3:
time: 161 us; the launch traced here: 160 us
  waiting for transfers between devices  68.3 us (42%)
  Pallas kernels  35.6 us (22%)
  starting transfers between devices  34.3 us (21%)
  local copies, waits for them, and re-layouts  14.6 us (9%)
  other arithmetic  6.1 us (4%)
    all_to_all x3, waiting for transfers between devices, exchange(): lax.all_to_all(blocks, 'ctx', 0, 0, tiled=True, axis_index_groups=groups)  25.4 us
    ppermute x4, waiting for transfers between devices, swap_pair(): lax.ppermute(v, 'ctx', [(self.index(h, p, y, c), self.index(h, 1 - p, y,...  21.2 us
    all_to_all x3, starting transfers between devices, exchange(): lax.all_to_all(blocks, 'ctx', 0, 0, tiled=True, axis_index_groups=groups)  12.4 us
    ppermute x1, waiting for transfers between devices, swap_half_and_pair(): return lax.ppermute(v, 'ctx', pairs)  11.6 us
    pallas_call x1, Pallas kernels, convolve(): pl.pallas_call(functools.partial(conv_kernel, scale, lag_own), grid=(grou...  11.3 us
    unnamed x29, local copies, waits for them, and re-layouts  9.19 us
    ppermute x4, starting transfers between devices, swap_pair(): lax.ppermute(v, 'ctx', [(self.index(h, p, y, c), self.index(h, 1 - p, y,...  7.43 us
    pallas_call x1, Pallas kernels, toeplitz(): pl.pallas_call(toeplitz_kernel, grid=(groups,), in_specs=[pl.BlockSpec((1...  7.02 us
  transfers between devices with their start and end apart: 17, of which 10 were waited for; matrix products, arithmetic and copies ran while one was open for 5% of the time, Pallas kernels for 22%

profile of v3, /device:TPU:0, one launch (start us, length us, event | category | flops | bytes accessed | tf_op | source)
XLA Modules:
  0.0 159.9 jit_solution(17625344525499411927)
XLA Ops:
  0.6 0.0 copy-start
  0.7 2.1 %constant_dynamic-slice_fusion.2 = (bf16[1024,256]{1,0:T(8,128)(2,1)}, bf16[1024,256]{1,0:T(8,128)(2,1)S(1)}) fusion(bf16[2048,256]{1,0:T(8,128)(2,1)} %param.7, s32[]{:T(128)S(6)} %select_n.72, s32[]{:T(128)S(6)} %select_n.71), kind=kLoop, calls=%fused_computation.35 | loop fusion | bytes 2097160 | tf_op jit(solution)/shard_map/dynamic_slice | solution.py:421
  2.8 3.0 %collective-permute-start.5 = (bf16[1024,256]{1,0:T(8,128)(2,1)S(1)}, bf16[1024,256]{1,0:T(8,128)(2,1)S(1)}, u32[]{:S(2)}, u32[]{:S(2)}) collective-permute-start(bf16[1024,256]{1,0:T(8,128)(2,1)S(1)} %get-tuple-element.25.refs_0_), channel_id=1, source_target_pairs={{0,8},{2,10},{4,12},{6,14},{8,0},{10,2},{12,4},{14,6},{16,24},{18,... | collective-permute-start | bytes 1572872 | tf_op jit(solution)/shard_map/ppermute | solution.py:258
  5.9 2.6 %collective-permute-start.3 = (bf16[1024,256]{1,0:T(8,128)(2,1)}, bf16[1024,256]{1,0:T(8,128)(2,1)}, u32[]{:S(2)}, u32[]{:S(2)}) collective-permute-start(bf16[1024,256]{1,0:T(8,128)(2,1)} %get-tuple-element.24.refs_0_), channel_id=1, source_target_pairs={{0,16},{2,18},{4,20},{6,22},{8,24},{10,26},{12,28},{14,30},{16,0},... | collective-permute-start | bytes 1572872 | tf_op jit(solution)/shard_map/ppermute | solution.py:261
  8.5 1.5 collective-permute-start.6
  10.0 0.4 collective-permute-start.1
  10.4 19.1 %collective-permute-done.5.refs_0_ = bf16[1024,256]{1,0:T(8,128)(2,1)S(1)} collective-permute-done((bf16[1024,256]{1,0:T(8,128)(2,1)S(1)}, bf16[1024,256]{1,0:T(8,128)(2,1)S(1)}, u32[]{:S(2)}, u32[]{:S(2)}) %collective-permute-start.5) | collective-permute-done | bytes 524320 | tf_op jit(solution)/shard_map/ppermute | solution.py:258
  29.5 0.8 copy-done.10
  30.3 0.7 collective-permute-done.3.refs_1_.refs_4_
  31.0 3.3 %collective-permute-start.4 = (bf16[1024,256]{1,0:T(8,128)(2,1)}, bf16[1024,256]{1,0:T(8,128)(2,1)S(1)}, u32[]{:S(2)}, u32[]{:S(2)}) collective-permute-start(bf16[1024,256]{1,0:T(8,128)(2,1)} %after.4), channel_id=1, source_target_pairs={{0,24},{2,26},{4,28},{6,30},{8,16},{10,18},{12,20},{14,22},{16,8},... | collective-permute-start | bytes 1572872 | tf_op jit(solution)/shard_map/ppermute | solution.py:265
  34.3 1.5 collective-permute-start.7
  35.9 0.5 collective-permute-start.8
  36.4 1.5 collective-permute-start
  37.9 0.9 constant_dynamic-slice_fusion.1
  38.7 2.1 %collective-permute-done.1.refs_2_ = bf16[128,2048]{1,0:T(8,128)(2,1)} collective-permute-done((bf16[128,2048]{1,0:T(8,128)(2,1)}, bf16[128,2048]{1,0:T(8,128)(2,1)}, u32[]{:S(2)}, u32[]{:S(2)}) %collective-permute-start.1) | collective-permute-done | bytes 524320 | tf_op jit(solution)/shard_map/ppermute | solution.py:258
  40.8 2.5 %collective-permute-start.10 = (f32[128,1024]{1,0:T(8,128)}, f32[128,1024]{1,0:T(8,128)S(1)}, u32[]{:S(2)}, u32[]{:S(2)}) collective-permute-start(f32[128,1024]{1,0:T(8,128)} %constant_dynamic-slice_fusion.1), channel_id=1, source_target_pairs={{0,8},{2,10},{4,12},{6,14},{8,0},{10,2},{12,4},{14,6},{16,24},{18,... | collective-permute-start | bytes 1572872 | tf_op jit(solution)/shard_map/ppermute | solution.py:258
  43.3 11.6 %collective-permute-done.4.refs_0_ = bf16[1024,256]{1,0:T(8,128)(2,1)S(1)} collective-permute-done((bf16[1024,256]{1,0:T(8,128)(2,1)}, bf16[1024,256]{1,0:T(8,128)(2,1)S(1)}, u32[]{:S(2)}, u32[]{:S(2)}) %collective-permute-start.4) | collective-permute-done | bytes 524320 | tf_op jit(solution)/shard_map/ppermute | solution.py:265
  54.9 1.5 collective-permute-start.2
  56.4 1.2 copy-done.2
  57.6 0.4 code_input.1
  58.1 0.8 copy-done.11
  58.9 1.5 collective-permute-start.9
  60.4 6.5 %collective-permute-done.2.refs_3_ = bf16[128,2048]{1,0:T(8,128)(2,1)} collective-permute-done((bf16[128,2048]{1,0:T(8,128)(2,1)}, bf16[128,2048]{1,0:T(8,128)(2,1)}, u32[]{:S(2)}, u32[]{:S(2)}) %collective-permute-start.2) | collective-permute-done | bytes 524320 | tf_op jit(solution)/shard_map/ppermute | solution.py:299
  66.9 3.1 %pick_features.1 = (bf16[256,2048]{1,0:T(8,128)(2,1)}, bf16[256,2048]{1,0:T(8,128)(2,1)}) custom-call(s32[1]{0:T(128)} %bitcast.9.core_ref, bf16[128,2048]{1,0:T(8,128)(2,1)} %refs_0_.1, bf16[128,2048]{1,0:T(8,128)(2,1)} %collective-permute-done.refs_1_, bf16[128,2048]{1,0:T(8,128)(2,1)} %collective-permute-done.1.refs_2_, ...), custom_call_target="tpu_custom_call" | custom-call | bytes 4194304 | tf_op jit(solution)/shard_map/pick_features/pallas_call | solution.py:302
  70.0 0.5 collective-permute-done.9.refs_1_.refs_7_
  70.5 0.3 copy-done.7
  70.8 0.5 copy-done.12
  71.3 0.7 stack.35.columns_ref
  71.9 0.9 convert_element_type.26
  72.8 3.8 %all-to-all-start.1 = ((f16[16,144,128]{2,1,0:T(8,128)(2,1)}), f16[16,144,128]{2,1,0:T(8,128)(2,1)S(1)}, u32[]{:S(2)}, u32[]{:S(2)}) async-start(f16[16,144,128]{2,1,0:T(8,128)(2,1)} %convert_element_type.26), calls=%async_computation.1 | async-start | bytes 1179648 | tf_op jit(solution)/shard_map/all_to_all | solution.py:490
  76.7 0.0 copy-start.13
  76.7 1.0 copy-done.13
  77.6 6.7 %add_shares.1 = (f32[256,1024]{1,0:T(8,128)}, f32[256,1024]{1,0:T(8,128)}) custom-call(s32[8]{0:T(128)} %stack.35.columns_ref, bf16[256,2048]{1,0:T(8,128)(2,1)} %get-tuple-element.10.mine_ref, bf16[256,2048]{1,0:T(8,128)(2,1)} %copy-done.13, bf16[1024,256]{1,0:T(8,128)(2,1)} %get-tuple-element.24.refs_0_, bf16[1024,256]{1,0:T(8,128)(2,1)} %collective-permute-done.6.refs_1_, ...), custom_call_target="tpu_custom_call" | custom-call | flops 2147483648 | bytes 10485760 | tf_op jit(solution)/shard_map/add_shares/pallas_call | solution.py:398
  84.3 0.5 collective-permute-start.12
  84.8 2.5 %collective-permute-done.12.arrived_ref = f32[256,1024]{1,0:T(8,128)S(1)} collective-permute-done((f32[256,1024]{1,0:T(8,128)}, f32[256,1024]{1,0:T(8,128)S(1)}, u32[]{:S(2)}, u32[]{:S(2)}) %collective-permute-start.12) | collective-permute-done | bytes 1048608 | tf_op jit(solution)/shard_map/ppermute | solution.py:255
  87.3 1.0 copy-done.9
  88.2 3.9 %seq_grad.1 = (f32[8,2,128,128]{3,2,1,0:T(8,128)}, f32[128,1024]{1,0:T(8,128)}, f32[128,1024]{1,0:T(8,128)}) custom-call(s32[1]{0:T(128)} %bitcast.p_ref, f32[256,1024]{1,0:T(8,128)} %get-tuple-element.12.sum_ref, f32[256,1024]{1,0:T(8,128)} %copy-done.9, f32[128,2048]{1,0:T(8,128)} %gate_ref.1, f32[128,1024]{1,0:T(8,128)} %copy-done.7), custom_call_target="tpu_custom_call" | custom-call | flops 524288 | bytes 6291456 | tf_op jit(solution)/shard_map/seq_grad/pallas_call | solution.py:333
  92.1 0.1 all-to-all-done.1
  92.2 4.9 %all-to-all-start = ((f32[8,2,128,128]{3,2,1,0:T(8,128)}), f32[8,2,128,128]{3,2,1,0:T(8,128)S(1)}, u32[]{:S(2)}, u32[]{:S(2)}) async-start(f32[8,2,128,128]{3,2,1,0:T(8,128)} %get-tuple-element.14), calls=%async_computation | async-start | bytes 2097152 | tf_op jit(solution)/shard_map/all_to_all | solution.py:490
  97.1 0.7 broadcast_in_dim.3.filter_ref
  97.8 7.0 %toeplitz.1.t_ref = bf16[8,256,2176]{2,1,0:T(8,128)(2,1)} custom-call(f32[8,1,2176]{2,1,0:T(1,128)} %broadcast_in_dim.3.filter_ref), custom_call_target="tpu_custom_call" | custom-call | flops 8912896 | bytes 8982528 | tf_op jit(solution)/shard_map/toeplitz/pallas_call | solution.py:38
  104.8 0.2 fusion.18
  105.1 0.7 fusion.1.x_ref
  105.7 3.2 %stack_input.1.left_ref = bf16[8,256,256]{2,1,0:T(8,128)(2,1)S(1)} custom-call(f32[16,128,128]{2,1,0:T(8,128)S(1)} %fusion.1.x_ref), custom_call_target="tpu_custom_call" | custom-call | flops 2097152 | bytes 2097152 | tf_op jit(solution)/shard_map/stack_input/pallas_call | solution.py:76
  108.9 0.0 copy-start.3
  109.0 1.0 copy-done.3
  109.9 1.5 collective-permute-start.13
  111.4 12.4 %all-to-all-done = f32[8,2,128,128]{3,2,1,0:T(8,128)S(1)} async-done(((f32[8,2,128,128]{3,2,1,0:T(8,128)}), f32[8,2,128,128]{3,2,1,0:T(8,128)S(1)}, u32[]{:S(2)}, u32[]{:S(2)}) %all-to-all-start) | async-done | bytes 1048608 | tf_op jit(solution)/shard_map/all_to_all | solution.py:490
  123.8 1.2 copy-done.4
  125.0 11.3 %convolve.1 = f32[16,144,128]{2,1,0:T(8,128)S(1)} custom-call(f32[2,4,2,128,128]{4,3,2,1,0:T(8,128)S(1)} %bitcast.22, bf16[8,256,256]{2,1,0:T(8,128)(2,1)S(1)} %copy-done.4, bf16[8,256,2176]{2,1,0:T(8,128)(2,1)} %toeplitz.1.t_ref), custom_call_target="tpu_custom_call" | custom-call | flops 7985954816 | bytes 12058624 | tf_op jit(solution)/shard_map/convolve/pallas_call | solution.py:195
  136.4 0.9 convert_element_type.29
  137.3 3.7 %all-to-all-start.2 = ((f16[16,144,128]{2,1,0:T(8,128)(2,1)}), f16[16,144,128]{2,1,0:T(8,128)(2,1)S(1)}, u32[]{:S(2)}, u32[]{:S(2)}) async-start(f16[16,144,128]{2,1,0:T(8,128)(2,1)} %convert_element_type.29), calls=%async_computation.2 | async-start | bytes 1179648 | tf_op jit(solution)/shard_map/all_to_all | solution.py:490
  141.0 0.0 copy-start.8
  141.0 1.4 broadcast_select_fusion.1
  142.4 0.1 copy-done.8
  142.6 1.1 maximum_multiply_fusion
  143.7 12.9 %all-to-all-done.2 = f16[16,144,128]{2,1,0:T(8,128)(2,1)S(1)} async-done(((f16[16,144,128]{2,1,0:T(8,128)(2,1)}), f16[16,144,128]{2,1,0:T(8,128)(2,1)S(1)}, u32[]{:S(2)}, u32[]{:S(2)}) %all-to-all-start.2) | async-done | bytes 589856 | tf_op jit(solution)/shard_map/all_to_all | solution.py:490
  156.6 0.2 fusion.20
  156.8 0.1 fusion.9
  156.9 0.6 copy.18
  157.5 0.6 fusion.5
  158.2 0.1 copy.16
  158.3 0.3 copy.17
  158.6 1.3 copy.19
  (28 shorter events, 0.1 us)
Async XLA Ops:
  0.6 96.5 %copy-start = (f32[128,2048]{1,0:T(8,128)S(1)}, f32[128,2048]{1,0:T(8,128)}, u32[]{:S(2)}) copy-start(f32[128,2048]{1,0:T(8,128)} %param.11) | copy-start | bytes 3145732
  2.8 28.1 %copy-start.6 = (bf16[1024,256]{1,0:T(8,128)(2,1)}, bf16[1024,256]{1,0:T(8,128)(2,1)S(1)}, u32[]{:S(2)}) copy-start(bf16[1024,256]{1,0:T(8,128)(2,1)S(1)} %get-tuple-element.25.refs_0_) | copy-start | bytes 1572868
  2.8 26.7 %collective-permute-start.5 = (bf16[1024,256]{1,0:T(8,128)(2,1)S(1)}, bf16[1024,256]{1,0:T(8,128)(2,1)S(1)}, u32[]{:S(2)}, u32[]{:S(2)}) collective-permute-start(bf16[1024,256]{1,0:T(8,128)(2,1)S(1)} %get-tuple-element.25.refs_0_), channel_id=1, source_target_pairs={{0,8},{2,10},{4,12},{6,14},{8,0},{10,2},{12,4},{14,6},{16,24},{18,... | collective-permute-start | bytes 1572872 | tf_op jit(solution)/shard_map/ppermute | solution.py:258
  5.9 32.0 %copy-start.5 = (f32[128,2048]{1,0:T(8,128)S(1)}, f32[128,2048]{1,0:T(8,128)}, u32[]{:S(2)}) copy-start(f32[128,2048]{1,0:T(8,128)} %gate_ref.1) | copy-start | bytes 3145732
  5.9 25.1 %collective-permute-start.3 = (bf16[1024,256]{1,0:T(8,128)(2,1)}, bf16[1024,256]{1,0:T(8,128)(2,1)}, u32[]{:S(2)}, u32[]{:S(2)}) collective-permute-start(bf16[1024,256]{1,0:T(8,128)(2,1)} %get-tuple-element.24.refs_0_), channel_id=1, source_target_pairs={{0,16},{2,18},{4,20},{6,22},{8,24},{10,26},{12,28},{14,30},{16,0},... | collective-permute-start | bytes 1572872 | tf_op jit(solution)/shard_map/ppermute | solution.py:261
  8.5 25.9 %collective-permute-start.6 = (bf16[1024,256]{1,0:T(8,128)(2,1)}, bf16[1024,256]{1,0:T(8,128)(2,1)}, u32[]{:S(2)}, u32[]{:S(2)}) collective-permute-start(bf16[1024,256]{1,0:T(8,128)(2,1)} %get-tuple-element.24.refs_0_), channel_id=1, source_target_pairs={{0,4},{2,6},{4,0},{6,2},{8,12},{10,14},{12,8},{14,10},{16,20},{18,... | collective-permute-start | bytes 1572872 | tf_op jit(solution)/shard_map/ppermute | solution.py:269
  10.0 30.8 %collective-permute-start.1 = (bf16[128,2048]{1,0:T(8,128)(2,1)}, bf16[128,2048]{1,0:T(8,128)(2,1)}, u32[]{:S(2)}, u32[]{:S(2)}) collective-permute-start(bf16[128,2048]{1,0:T(8,128)(2,1)} %refs_0_.1), channel_id=1, source_target_pairs={{0,8},{2,10},{4,12},{6,14},{8,0},{10,2},{12,4},{14,6},{16,24},{18,... | collective-permute-start | bytes 1572872 | tf_op jit(solution)/shard_map/ppermute | solution.py:258
  29.5 0.8 copy-start.10
  31.0 23.9 %collective-permute-start.4 = (bf16[1024,256]{1,0:T(8,128)(2,1)}, bf16[1024,256]{1,0:T(8,128)(2,1)S(1)}, u32[]{:S(2)}, u32[]{:S(2)}) collective-permute-start(bf16[1024,256]{1,0:T(8,128)(2,1)} %after.4), channel_id=1, source_target_pairs={{0,24},{2,26},{4,28},{6,30},{8,16},{10,18},{12,20},{14,22},{16,8},... | collective-permute-start | bytes 1572872 | tf_op jit(solution)/shard_map/ppermute | solution.py:265
  34.3 23.7 %collective-permute-start.7 = (bf16[1024,256]{1,0:T(8,128)(2,1)}, bf16[1024,256]{1,0:T(8,128)(2,1)S(1)}, u32[]{:S(2)}, u32[]{:S(2)}) collective-permute-start(bf16[1024,256]{1,0:T(8,128)(2,1)} %after.5.refs_2_), channel_id=1, source_target_pairs={{0,4},{2,6},{4,0},{6,2},{8,12},{10,14},{12,8},{14,10},{16,20},{18,... | collective-permute-start | bytes 1572872 | tf_op jit(solution)/shard_map/ppermute | solution.py:269
  35.9 23.0 %collective-permute-start.8 = (bf16[1024,256]{1,0:T(8,128)(2,1)}, bf16[1024,256]{1,0:T(8,128)(2,1)}, u32[]{:S(2)}, u32[]{:S(2)}) collective-permute-start(bf16[1024,256]{1,0:T(8,128)(2,1)} %collective-permute-done.3.refs_1_.refs_4_), channel_id=1, source_target_pairs={{0,4},{2,6},{4,0},{6,2},{8,12},{10,14},{12,8},{14,10},{16,20},{18,... | collective-permute-start | bytes 1572872 | tf_op jit(solution)/shard_map/ppermute | solution.py:269
  36.4 24.1 %collective-permute-start = (bf16[128,2048]{1,0:T(8,128)(2,1)}, bf16[128,2048]{1,0:T(8,128)(2,1)}, u32[]{:S(2)}, u32[]{:S(2)}) collective-permute-start(bf16[128,2048]{1,0:T(8,128)(2,1)} %refs_0_.1), channel_id=1, source_target_pairs={{0,1},{1,0},{2,3},{3,2},{4,5},{5,4},{6,7},{7,6},{8,9},{9,8},{10,11... | collective-permute-start | bytes 1572872 | tf_op jit(solution)/shard_map/ppermute | solution.py:299
  40.8 29.2 %collective-permute-start.10 = (f32[128,1024]{1,0:T(8,128)}, f32[128,1024]{1,0:T(8,128)S(1)}, u32[]{:S(2)}, u32[]{:S(2)}) collective-permute-start(f32[128,1024]{1,0:T(8,128)} %constant_dynamic-slice_fusion.1), channel_id=1, source_target_pairs={{0,8},{2,10},{4,12},{6,14},{8,0},{10,2},{12,4},{14,6},{16,24},{18,... | collective-permute-start | bytes 1572872 | tf_op jit(solution)/shard_map/ppermute | solution.py:258
  54.9 3.1 %copy-start.1 = (bf16[1024,256]{1,0:T(8,128)(2,1)}, bf16[1024,256]{1,0:T(8,128)(2,1)S(1)}, u32[]{:S(2)}) copy-start(bf16[1024,256]{1,0:T(8,128)(2,1)S(1)} %collective-permute-done.4.refs_0_) | copy-start | bytes 1572868
  54.9 12.0 %collective-permute-start.2 = (bf16[128,2048]{1,0:T(8,128)(2,1)}, bf16[128,2048]{1,0:T(8,128)(2,1)}, u32[]{:S(2)}, u32[]{:S(2)}) collective-permute-start(bf16[128,2048]{1,0:T(8,128)(2,1)} %collective-permute-done.1.refs_2_), channel_id=1, source_target_pairs={{0,1},{1,0},{2,3},{3,2},{4,5},{5,4},{6,7},{7,6},{8,9},{9,8},{10,11... | collective-permute-start | bytes 1572872 | tf_op jit(solution)/shard_map/ppermute | solution.py:299
  56.4 1.2 copy-start.2
  58.1 0.8 copy-start.11
  58.9 11.6 %collective-permute-start.9 = (bf16[1024,256]{1,0:T(8,128)(2,1)}, bf16[1024,256]{1,0:T(8,128)(2,1)S(1)}, u32[]{:S(2)}, u32[]{:S(2)}) collective-permute-start(bf16[1024,256]{1,0:T(8,128)(2,1)} %after.6.refs_6_), channel_id=1, source_target_pairs={{0,4},{2,6},{4,0},{6,2},{8,12},{10,14},{12,8},{14,10},{16,20},{18,... | collective-permute-start | bytes 1572872 | tf_op jit(solution)/shard_map/ppermute | solution.py:269
  70.0 0.8 copy-start.7
  70.5 0.8 copy-start.12
  71.3 5.4 %collective-permute-start.11 = (bf16[256,2048]{1,0:T(8,128)(2,1)}, bf16[256,2048]{1,0:T(8,128)(2,1)S(1)}, u32[]{:S(2)}, u32[]{:S(2)}) collective-permute-start(bf16[256,2048]{1,0:T(8,128)(2,1)} %after.7), channel_id=1, source_target_pairs={{0,2},{2,0},{4,6},{6,4},{8,10},{10,8},{12,14},{14,12},{16,18},{18,... | collective-permute-start | bytes 3145736 | tf_op jit(solution)/shard_map/ppermute | solution.py:255
  72.8 19.4 %all-to-all-start.1 = ((f16[16,144,128]{2,1,0:T(8,128)(2,1)}), f16[16,144,128]{2,1,0:T(8,128)(2,1)S(1)}, u32[]{:S(2)}, u32[]{:S(2)}) async-start(f16[16,144,128]{2,1,0:T(8,128)(2,1)} %convert_element_type.26), calls=%async_computation.1 | async-start | bytes 1179648 | tf_op jit(solution)/shard_map/all_to_all | solution.py:490
  76.7 1.0 copy-start.13
  84.3 3.0 %collective-permute-start.12 = (f32[256,1024]{1,0:T(8,128)}, f32[256,1024]{1,0:T(8,128)S(1)}, u32[]{:S(2)}, u32[]{:S(2)}) collective-permute-start(f32[256,1024]{1,0:T(8,128)} %get-tuple-element.13), channel_id=1, source_target_pairs={{0,2},{2,0},{4,6},{6,4},{8,10},{10,8},{12,14},{14,12},{16,18},{18,... | collective-permute-start | bytes 3145736 | tf_op jit(solution)/shard_map/ppermute | solution.py:255
  87.3 1.0 copy-start.9
  92.2 31.6 %all-to-all-start = ((f32[8,2,128,128]{3,2,1,0:T(8,128)}), f32[8,2,128,128]{3,2,1,0:T(8,128)S(1)}, u32[]{:S(2)}, u32[]{:S(2)}) async-start(f32[8,2,128,128]{3,2,1,0:T(8,128)} %get-tuple-element.14), calls=%async_computation | async-start | bytes 2097152 | tf_op jit(solution)/shard_map/all_to_all | solution.py:490
  108.9 1.0 copy-start.3
  109.9 31.1 %collective-permute-start.13 = (f32[128,1024]{1,0:T(8,128)}, f32[128,1024]{1,0:T(8,128)}, u32[]{:S(2)}, u32[]{:S(2)}) collective-permute-start(f32[128,1024]{1,0:T(8,128)} %get-tuple-element.16), channel_id=1, source_target_pairs={{0,8},{2,10},{4,12},{6,14},{8,0},{10,2},{12,4},{14,6},{16,24},{18,... | collective-permute-start | bytes 1572872 | tf_op jit(solution)/shard_map/ppermute | solution.py:258
  123.8 1.2 copy-start.4
  137.3 19.3 %all-to-all-start.2 = ((f16[16,144,128]{2,1,0:T(8,128)(2,1)}), f16[16,144,128]{2,1,0:T(8,128)(2,1)S(1)}, u32[]{:S(2)}, u32[]{:S(2)}) async-start(f16[16,144,128]{2,1,0:T(8,128)(2,1)} %convert_element_type.29), calls=%async_computation.2 | async-start | bytes 1179648 | tf_op jit(solution)/shard_map/all_to_all | solution.py:490
  141.0 1.5 copy-start.8

commit v4 on v3

--- a/solution.py
+++ b/solution.py
@@ -95,15 +95,16 @@
 
 def decoded(code, exponent):
     code = code.astype(jnp.float32)
-    return jnp.sign(code) * jnp.sqrt(jnp.abs(code) * (1.0 / CODE_UNIT)) * jnp.exp2(exponent.astype(jnp.float32))
+    value = jnp.sqrt(jnp.abs(code) * (1.0 / CODE_UNIT)) * jnp.exp2(exponent.astype(jnp.float32))
+    return jnp.where(code < 0, -value, value)
 
 
 def largest(value):
-    return jnp.max(jnp.max(jnp.abs(value), axis=0, keepdims=True), axis=1, keepdims=True)
+    return jnp.max(jnp.abs(value), axis=0, keepdims=True)
 
 
 def conv_kernel(scale, lag_own, s_ref, left_ref, t_ref, out_ref, s_hi, s_lo, grads, cross, lag_sums):
-    blocks, tok = 2 * s_ref.shape[0] * s_ref.shape[1], s_ref.shape[3]
+    blocks, tok = 2 * s_ref.shape[0], left_ref.shape[1] // 2
     groups, rows, _ = grads.shape
     per = rows // blocks
     width = t_ref.shape[2]
@@ -116,8 +117,10 @@
         s_hi[:, rows:, :] = jnp.zeros_like(s_hi[:, rows:, :])
         s_lo[:, rows:, :] = jnp.zeros_like(s_lo[:, rows:, :])
         for a in range(blocks):
-            z, rest = divmod(a, s_ref.shape[1])
-            high, low = split(s_ref[z // 2, rest, z % 2].T[: groups * per])
+            z, rest = divmod(a, blocks // 4)
+            source, first = z // 2 * (blocks // 4) + rest, z % 2 * tok
+            code, exponent = s_ref[source, first : first + tok, :], s_ref[source, 2 * tok : 2 * tok + 1, :]
+            high, low = split(decoded(code, exponent).T[: groups * per])
             s_hi[:, a * per : (a + 1) * per, :] = high.reshape(groups, per, tok)
             s_lo[:, a * per : (a + 1) * per, :] = low.reshape(groups, per, tok)
 
@@ -163,14 +166,16 @@
         held = out_ref.shape[1] - 8
         for a in range(blocks):
             out_ref[a, tok:held, :] = jnp.zeros_like(out_ref[a, tok:held, :])
-            block = grads[:, a * per : (a + 1) * per, :].reshape(groups * per, tok)
+            block = grads[:, a * per : (a + 1) * per, :].reshape(groups * per, tok).T
             code, exponent = coded(block, largest(block))
             if out_ref.shape[2] > groups * per:
                 out_ref[a, :tok, :] = jnp.zeros_like(out_ref[a, :tok, :])
-            out_ref[a, :tok, : groups * per] = code.T
-            out_ref[a, tok : tok + groups, :lag_own] = lags[:, a * lag_own : (a + 1) * lag_own]
-            which = lax.broadcasted_iota(jnp.int32, (8, out_ref.shape[2]), 0)
-            out_ref[a, held:, :] = jnp.where(which == 0, exponent, lag_exponent)
+            out_ref[a, held:, :] = jnp.zeros_like(out_ref[a, held:, :])
+            out_ref[a, :tok, : groups * per] = code
+            out_ref[a, held : held + 1, : groups * per] = exponent
+            own_lags = slice(a * lag_own, (a + 1) * lag_own)
+            out_ref[a, tok : tok + groups, :lag_own] = lags[:, own_lags]
+            out_ref[a, held + 1 : held + 2, :lag_own] = lag_exponent[:, own_lags]
 
 
 def convolve(seq_blocks, input_blocks, moved, channels, lag_own, scale):
@@ -196,7 +201,7 @@
         functools.partial(conv_kernel, scale, lag_own),
         grid=(groups,),
         in_specs=[
-            pl.BlockSpec(seq_blocks.shape, lambda g: (0, 0, 0, 0, 0)),
+            pl.BlockSpec(seq_blocks.shape, lambda g: (0, 0, 0)),
             pl.BlockSpec((1, 2 * tok, rows), lambda g: (g, 0, 0)),
             pl.BlockSpec((1, 2 * tok, width), lambda g: (g, 0, 0)),
         ],
@@ -311,19 +316,25 @@
     return mine, place.swap_core(after(theirs, *earlier))
 
 
-def seq_kernel(p_ref, sum_ref, arrived_ref, gate_ref, far_gate_ref, out_ref, near_ref, far_ref):
+def seq_kernel(p_ref, sum_ref, arrived_ref, gate_ref, far_gate_ref, *refs):
+    out_ref, near_ref, far_ref = refs[-3:]
     p = p_ref[0]
-    blocks, _, tok, own = out_ref.shape
+    blocks, _, own = out_ref.shape
+    tok = near_ref.shape[0]
     near_ref[...] = sum_ref[:tok, :] + arrived_ref[:tok, :]
     far_ref[...] = sum_ref[tok:, :] + arrived_ref[tok:, :]
     near = near_ref[...] * gate_ref[...]
     far = far_ref[...] * far_gate_ref[...]
     for b in range(blocks):
-        out_ref[b, p] = near[:, b * own : (b + 1) * own]
-        out_ref[b, 1 - p] = far[:, b * own : (b + 1) * own]
-
-
-def seq_blocks_of(total, arrived, gate_value, far_gate, place):
+        here = slice(b * own, (b + 1) * own)
+        most = jnp.maximum(largest(near[:, here]), largest(far[:, here]))
+        for value, place in ((near, p), (far, 1 - p)):
+            code, exponent = coded(value[:, here], most)
+            out_ref[b, pl.ds(pl.multiple_of(place * tok, tok), tok), :] = code
+        out_ref[b, 2 * tok :, :] = jnp.broadcast_to(exponent, (ROW_TILE, own))
+
+
+def seq_blocks_of(total, arrived, gate_value, far_gate, place, *awaited):
     tok, channels = gate_value.shape
     blocks = place.devices // 2
     half = channels // 2
@@ -340,32 +351,44 @@
                 pl.BlockSpec((2 * tok, width), lambda i, p: (0, i)),
                 pl.BlockSpec((tok, width), lambda i, p: (0, p[0] * steps + i)),
                 pl.BlockSpec((tok, width), lambda i, p: (0, i)),
-            ],
+            ]
+            + [ANY] * len(awaited),
             out_specs=[
-                pl.BlockSpec((count, 2, tok, own), lambda i, p: (i, 0, 0, 0)),
+                pl.BlockSpec((count, 2 * tok + ROW_TILE, own), lambda i, p: (i, 0, 0)),
                 pl.BlockSpec((tok, width), lambda i, p: (0, i)),
                 pl.BlockSpec((tok, width), lambda i, p: (0, i)),
             ],
         ),
         out_shape=[
-            jax.ShapeDtypeStruct((blocks, 2, tok, own), jnp.float32),
+            jax.ShapeDtypeStruct((blocks, 2 * tok + ROW_TILE, own), jnp.float32),
             jax.ShapeDtypeStruct((tok, half), jnp.float32),
             jax.ShapeDtypeStruct((tok, half), jnp.float32),
         ],
-        compiler_params=pltpu.CompilerParams(vmem_limit_bytes=GRANT),
+        compiler_params=pltpu.CompilerParams(vmem_limit_bytes=24 * 1024 * 1024),
         cost_estimate=pl.CostEstimate(
             flops=2 * tok * channels, bytes_accessed=24 * tok * channels, transcendentals=0
         ),
         name="seq_grad",
-    )(place.p.reshape(1), total, arrived, gate_value, far_gate)
-
-
-def share_kernel(columns_ref, mine_ref, theirs_ref, *refs):
-    shares, (own_ref, other_ref) = refs[:-2], refs[-2:]
+    )(place.p.reshape(1), total, arrived, gate_value, far_gate, *awaited)
+
+
+def column_of(share, ctx, ch, ys, parts, features):
+    other_h, other_p, shift = share
+    chip = ctx // 2
+    z, y = chip // ys, lax.rem(chip, ys)
+    h, p = z // 2, lax.rem(z, 2)
+    source = ((1 - h if other_h else h) * 2 + (1 - p if other_p else p)) * ys + lax.rem(y - shift + ys, ys)
+    chips = 4 * ys // parts
+    return (lax.rem(ch - source // chips + parts, parts) * chips + lax.rem(source, chips)) * features
+
+
+def share_kernel(where, ys, parts, ctx_ref, ch_ref, mine_ref, theirs_ref, *refs):
+    shares, before, (own_ref, other_ref) = refs[: len(where)], refs[len(where) : -2], refs[-2:]
     rows, features = mine_ref.shape[0], shares[0].shape[1]
     left = []
-    for s in range(len(shares)):
-        at = pl.ds(pl.multiple_of(columns_ref[s], features), features)
+    for share in where:
+        column = column_of(share, ctx_ref[0], ch_ref[0], ys, parts, features)
+        at = pl.ds(pl.multiple_of(column, features), features)
         left.append(jnp.concatenate([mine_ref[:, at], theirs_ref[:, at]], axis=0))
     term = lax.dot_general(
         jnp.concatenate(left, axis=1),
@@ -373,35 +396,41 @@
         (((1,), (1,)), ((), ())),
         preferred_element_type=jnp.float32,
     )
-    own_ref[...] = term[:rows]
-    other_ref[...] = term[rows:]
-
-
-def add_shares(columns, mine, theirs, shares):
+    for i, ref in enumerate((own_ref, other_ref)):
+        part = term[i * rows : (i + 1) * rows]
+        ref[...] = part + before[i][...] if before else part
+
+
+def add_shares(where, mine, theirs, shares, before, place):
     rows, (half, features) = mine.shape[0], shares[0].shape
+    parts = lax.axis_size("ch")
+    ctx, ch = lax.axis_index("ctx"), lax.axis_index("ch")
     if features % LANES:
-        sums = [0.0, 0.0]
-        for column, share in zip(columns, shares):
+        sums = list(before)
+        for share, held in zip(where, shares):
+            column = column_of(share, ctx, ch, place.ys, parts, features)
             terms = [
                 lax.dot_general(
                     lax.dynamic_slice_in_dim(v, column, features, 1),
-                    share,
+                    held,
                     (((1,), (1,)), ((), ())),
                     preferred_element_type=jnp.float32,
                 )
                 for v in (mine, theirs)
             ]
-            sums = [a + b for a, b in zip(sums, terms)]
+            sums = [a + b for a, b in zip(sums, terms)] if sums else terms
         return sums
     tile = min(256, half)
     whole = jax.ShapeDtypeStruct((rows, half), jnp.float32)
-    return pl.pallas_call(
-        share_kernel,
+    tiles = pl.BlockSpec((rows, tile), lambda n: (0, n))
+    return pl.pallas_call(
+        functools.partial(share_kernel, where, place.ys, parts),
         grid=(half // tile,),
-        in_specs=[SMEM]
+        in_specs=[SMEM] * 2
         + [pl.BlockSpec(mine.shape, lambda n: (0, 0))] * 2
-        + [pl.BlockSpec((tile, features), lambda n: (n, 0))] * len(shares),
-        out_specs=[pl.BlockSpec((rows, tile), lambda n: (0, n))] * 2,
+        + [pl.BlockSpec((tile, features), lambda n: (n, 0))] * len(shares)
+        + [tiles] * len(before),
+        out_specs=[tiles] * 2,
         out_shape=[whole, whole],
         compiler_params=pltpu.CompilerParams(vmem_limit_bytes=GRANT),
         cost_estimate=pl.CostEstimate(
@@ -410,13 +439,11 @@
             transcendentals=0,
         ),
         name="add_shares",
-    )(jnp.stack(columns), mine, theirs, *shares)
+    )(ctx.reshape(1), ch.reshape(1), mine, theirs, *shares, *before)
 
 
 def project(cotangent, out_weight, place, *waited):
     channels, features = out_weight.shape
-    chips = place.devices // 2
-    parts = lax.axis_size("ch")
     half = channels // 2
     near = lax.dynamic_slice_in_dim(out_weight, place.p * half, half, 0)
     given = lax.dynamic_slice_in_dim(out_weight, (1 - place.p) * half, half, 0)
@@ -432,19 +459,13 @@
     held.append(along_y(far))
     held.append(along_y(after(far_paired, *held[1][1:], *held[2][1:])))
     mine, theirs = gather_cotangent(cotangent, features, place, [*held[3][1:], *waited])
-    chips_of_part = chips // parts
-
-    def column(other_h, other_p, shift):
-        h = 1 - place.h if other_h else place.h
-        p = 1 - place.p if other_p else place.p
-        source = (h * 2 + p) * place.ys + lax.rem(place.y - shift + place.ys, place.ys)
-        slot = lax.rem(lax.axis_index("ch") - source // chips_of_part + parts, parts)
-        return (slot * chips_of_part + lax.rem(source, chips_of_part)) * features
-
     shares = [
-        (column(other // 2, other % 2, shift), held[other][shift]) for other in range(4) for shift in range(place.ys)
+        ((other // 2, other % 2, shift), held[other][shift]) for other in range(4) for shift in range(place.ys)
     ]
-    own, other = add_shares([c for c, _ in shares], mine, theirs, [v for _, v in shares])
+    sums = []
+    for some in (shares,):
+        sums = add_shares([at for at, _ in some], mine, theirs, [v for _, v in some], sums, place)
+    own, other = sums
     return own, place.swap_core(other), far_paired
 
 
@@ -458,7 +479,7 @@
         h, p, rest = i // (2 * quarter), i // quarter % 2, i % quarter
         block = (p * 2 + h) * quarter + rest
         out_ref[i, :tok, :] = code[:, block * own : (block + 1) * own]
-        out_ref[i, tok:, :] = jnp.broadcast_to(exponent, (rows - tok, own))
+        out_ref[i, tok:, :] = jnp.broadcast_to(exponent[:, block * own : (block + 1) * own], (rows - tok, own))
 
 
 def code_blocks(value, devices, *awaited):
@@ -495,13 +516,13 @@
     far_gate = place.swap_pair(lax.dynamic_slice_in_dim(gate_value, (1 - place.p) * half, half, 1))
     total, arrived, late = project(cotangent, out_weight, place, far_gate)
     code = exchange(code_blocks(conv_input, devices, late).astype(jnp.float16))
-    input_blocks = decoded(code[:, :tok], code[:, tok : tok + 1, :1])
+    input_blocks = decoded(code[:, :tok], code[:, tok : tok + 1])
     first_group = (place.p * half + place.block * own) // per_group
     moved = toeplitz(lax.dynamic_slice_in_dim(filters, first_group, groups, 0), tok)
 
-    seq_blocks, near, far = seq_blocks_of(total, arrived, gate_value, far_gate, place)
-    seq_blocks = exchange(seq_blocks, place.same_p())
-    seq_blocks = seq_blocks.reshape(2, devices // 4, 2, tok, own)
+    seq_code, near, far = seq_blocks_of(total, arrived, gate_value, far_gate, place)
+    seq_code = exchange(seq_code.astype(jnp.float16), place.same_p())
+    seq_blocks = seq_code.astype(jnp.float32)
     far = place.swap_pair(far)
     left = jnp.where(place.p == 0, near, far)
     right = jnp.where(place.p == 0, far, near)
@@ -511,9 +532,9 @@
     result = convolve(seq_blocks, input_blocks, moved, min(own, per_group), lag_own, scale)
     back = exchange(result[:, :, : max(own, lag_own)].astype(jnp.float16))
     held = back.shape[1] - 8
-    input_grad = reorder(decoded(back[:, :tok, :own], back[:, held : held + 1, :1]))
+    input_grad = reorder(decoded(back[:, :tok, :own], back[:, held : held + 1, :own]))
     input_grad = input_grad.transpose(1, 0, 2).reshape(tok, channels)
-    filter_grad = reorder(decoded(back[:, tok : tok + groups, :lag_own], back[:, held + 1 : held + 2, :1]))
+    filter_grad = reorder(decoded(back[:, tok : tok + groups, :lag_own], back[:, held + 1 : held + 2, :lag_own]))
     filter_grad = filter_grad.reshape(all_groups, share, lag_own).sum(axis=1)
     return (input_grad, gate_grad, filter_grad)
 

time: 161 us -> 149 us (0.925)
  waiting for transfers between devices: 68.3 us -> 59.4 us
  local copies, waits for them, and re-layouts: 14.6 us -> 10.2 us
  other arithmetic: 6.1 us -> 8.96 us
    all_to_all x3, waiting for transfers between devices: 25.4 us -> 15.9 us  [exchange(): lax.all_to_all(blocks, 'ctx', 0, 0, tiled=True, axis_index_groups=groups)]
    unnamed x29 -> x17, local copies, waits for them, and re-layouts: 9.19 us -> 5.32 us
    select_n x0 -> x3, other arithmetic: none -> 2.05 us  [decoded(): return jnp.where(code < 0, -value, value)]
    convert_element_type x0 -> x2, other arithmetic: none -> 2.01 us  [the longest x1 1.13 us: body(): seq_blocks = seq_code.astype(jnp.float32)]
  transfers between devices with their start and end apart: 17 -> 17, of which waited for: 10 -> 9; matrix products, arithmetic and copies ran while one was open for 5% -> 7% of each run, Pallas kernels for 22% -> 23%
where the time goes in v4:
time: 149 us; the launch traced here: 148 us
  waiting for transfers between devices  59.4 us (40%)
  starting transfers between devices  34.4 us (23%)
  Pallas kernels  34.1 us (23%)
  local copies, waits for them, and re-layouts  10.2 us (7%)
  other arithmetic  8.96 us (6%)
    ppermute x4, waiting for transfers between devices, swap_pair(): lax.ppermute(v, 'ctx', [(self.index(h, p, y, c), self.index(h, 1 - p, y,...  21.1 us
    all_to_all x3, waiting for transfers between devices, exchange(): lax.all_to_all(blocks, 'ctx', 0, 0, tiled=True, axis_index_groups=groups)  15.9 us
    all_to_all x3, starting transfers between devices, exchange(): lax.all_to_all(blocks, 'ctx', 0, 0, tiled=True, axis_index_groups=groups)  12.2 us
    ppermute x1, waiting for transfers between devices, swap_half_and_pair(): return lax.ppermute(v, 'ctx', pairs)  11.6 us
    pallas_call x1, Pallas kernels, convolve(): pl.pallas_call(functools.partial(conv_kernel, scale, lag_own), grid=(grou...  11.6 us
    ppermute x2, waiting for transfers between devices, along_ch(): lax.ppermute(v, 'ch', [(j, (j + s) % parts) for j in range(parts)])  7.59 us
    ppermute x4, starting transfers between devices, swap_pair(): lax.ppermute(v, 'ctx', [(self.index(h, p, y, c), self.index(h, 1 - p, y,...  7.36 us
    pallas_call x1, Pallas kernels, toeplitz(): pl.pallas_call(toeplitz_kernel, grid=(groups,), in_specs=[pl.BlockSpec((1...  7 us
  transfers between devices with their start and end apart: 17, of which 9 were waited for; matrix products, arithmetic and copies ran while one was open for 7% of the time, Pallas kernels for 23%

profile of v4, /device:TPU:0, one launch (start us, length us, event | category | flops | bytes accessed | tf_op | source)
XLA Modules:
  0.0 148.1 jit_solution(9310279959411618047)
XLA Ops:
  0.6 0.0 copy-start
  0.7 2.3 %constant_dynamic-slice_fusion.2 = (bf16[1024,256]{1,0:T(8,128)(2,1)}, bf16[1024,256]{1,0:T(8,128)(2,1)}) fusion(bf16[2048,256]{1,0:T(8,128)(2,1)} %param.7, s32[]{:T(128)S(6)} %select_n.50, s32[]{:T(128)S(6)} %select_n.49), kind=kLoop, calls=%fused_computation.32 | loop fusion | bytes 2097160 | tf_op jit(solution)/shard_map/dynamic_slice | solution.py:448
  3.0 3.0 %collective-permute-start.5 = (bf16[1024,256]{1,0:T(8,128)(2,1)}, bf16[1024,256]{1,0:T(8,128)(2,1)}, u32[]{:S(2)}, u32[]{:S(2)}) collective-permute-start(bf16[1024,256]{1,0:T(8,128)(2,1)} %get-tuple-element.23.refs_0_), channel_id=1, source_target_pairs={{0,8},{2,10},{4,12},{6,14},{8,0},{10,2},{12,4},{14,6},{16,24},{18,... | collective-permute-start | bytes 1572872 | tf_op jit(solution)/shard_map/ppermute | solution.py:263
  6.0 2.6 %collective-permute-start.3 = (bf16[1024,256]{1,0:T(8,128)(2,1)}, bf16[1024,256]{1,0:T(8,128)(2,1)}, u32[]{:S(2)}, u32[]{:S(2)}) collective-permute-start(bf16[1024,256]{1,0:T(8,128)(2,1)} %get-tuple-element.22.refs_0_), channel_id=1, source_target_pairs={{0,16},{2,18},{4,20},{6,22},{8,24},{10,26},{12,28},{14,30},{16,0},... | collective-permute-start | bytes 1572872 | tf_op jit(solution)/shard_map/ppermute | solution.py:266
  8.6 1.5 %collective-permute-start.6 = (bf16[1024,256]{1,0:T(8,128)(2,1)}, bf16[1024,256]{1,0:T(8,128)(2,1)S(1)}, u32[]{:S(2)}, u32[]{:S(2)}) collective-permute-start(bf16[1024,256]{1,0:T(8,128)(2,1)} %get-tuple-element.22.refs_0_), channel_id=1, source_target_pairs={{0,4},{2,6},{4,0},{6,2},{8,12},{10,14},{12,8},{14,10},{16,20},{18,... | collective-permute-start | bytes 1572872 | tf_op jit(solution)/shard_map/ppermute | solution.py:274
  10.2 0.4 collective-permute-start.1
  10.6 19.6 %collective-permute-done.5.refs_0_ = bf16[1024,256]{1,0:T(8,128)(2,1)} collective-permute-done((bf16[1024,256]{1,0:T(8,128)(2,1)}, bf16[1024,256]{1,0:T(8,128)(2,1)}, u32[]{:S(2)}, u32[]{:S(2)}) %collective-permute-start.5) | collective-permute-done | bytes 524320 | tf_op jit(solution)/shard_map/ppermute | solution.py:263
  30.2 0.7 collective-permute-done.3.refs_1_.refs_4_
  30.9 3.6 %collective-permute-start.4 = (bf16[1024,256]{1,0:T(8,128)(2,1)}, bf16[1024,256]{1,0:T(8,128)(2,1)S(1)}, u32[]{:S(2)}, u32[]{:S(2)}) collective-permute-start(bf16[1024,256]{1,0:T(8,128)(2,1)} %after.4), channel_id=1, source_target_pairs={{0,24},{2,26},{4,28},{6,30},{8,16},{10,18},{12,20},{14,22},{16,8},... | collective-permute-start | bytes 1572872 | tf_op jit(solution)/shard_map/ppermute | solution.py:270
  34.5 0.0 collective-permute-done.6.refs_1_
  34.5 0.8 copy-done.7
  35.3 1.5 %collective-permute-start.7 = (bf16[1024,256]{1,0:T(8,128)(2,1)}, bf16[1024,256]{1,0:T(8,128)(2,1)}, u32[]{:S(2)}, u32[]{:S(2)}) collective-permute-start(bf16[1024,256]{1,0:T(8,128)(2,1)} %after.5.refs_2_), channel_id=1, source_target_pairs={{0,4},{2,6},{4,0},{6,2},{8,12},{10,14},{12,8},{14,10},{16,20},{18,... | collective-permute-start | bytes 1572872 | tf_op jit(solution)/shard_map/ppermute | solution.py:274
  36.8 0.5 collective-permute-start.8
  37.3 1.5 %collective-permute-start = (bf16[128,2048]{1,0:T(8,128)(2,1)}, bf16[128,2048]{1,0:T(8,128)(2,1)}, u32[]{:S(2)}, u32[]{:S(2)}) collective-permute-start(bf16[128,2048]{1,0:T(8,128)(2,1)} %refs_0_.1), channel_id=1, source_target_pairs={{0,1},{1,0},{2,3},{3,2},{4,5},{5,4},{6,7},{7,6},{8,9},{9,8},{10,11... | collective-permute-start | bytes 1572872 | tf_op jit(solution)/shard_map/ppermute | solution.py:304
  38.8 0.8 constant_dynamic-slice_fusion.1
  39.7 1.5 %collective-permute-done.1.refs_2_ = bf16[128,2048]{1,0:T(8,128)(2,1)} collective-permute-done((bf16[128,2048]{1,0:T(8,128)(2,1)}, bf16[128,2048]{1,0:T(8,128)(2,1)}, u32[]{:S(2)}, u32[]{:S(2)}) %collective-permute-start.1) | collective-permute-done | bytes 524320 | tf_op jit(solution)/shard_map/ppermute | solution.py:263
  41.2 2.5 %collective-permute-start.10 = (f32[128,1024]{1,0:T(8,128)}, f32[128,1024]{1,0:T(8,128)}, u32[]{:S(2)}, u32[]{:S(2)}) collective-permute-start(f32[128,1024]{1,0:T(8,128)} %constant_dynamic-slice_fusion.1), channel_id=1, source_target_pairs={{0,8},{2,10},{4,12},{6,14},{8,0},{10,2},{12,4},{14,6},{16,24},{18,... | collective-permute-start | bytes 1572872 | tf_op jit(solution)/shard_map/ppermute | solution.py:263
  43.7 11.6 %collective-permute-done.4.refs_0_ = bf16[1024,256]{1,0:T(8,128)(2,1)S(1)} collective-permute-done((bf16[1024,256]{1,0:T(8,128)(2,1)}, bf16[1024,256]{1,0:T(8,128)(2,1)S(1)}, u32[]{:S(2)}, u32[]{:S(2)}) %collective-permute-start.4) | collective-permute-done | bytes 524320 | tf_op jit(solution)/shard_map/ppermute | solution.py:270
  55.3 0.8 copy-done.2
  56.1 1.5 %collective-permute-start.2 = (bf16[128,2048]{1,0:T(8,128)(2,1)}, bf16[128,2048]{1,0:T(8,128)(2,1)}, u32[]{:S(2)}, u32[]{:S(2)}) collective-permute-start(bf16[128,2048]{1,0:T(8,128)(2,1)} %collective-permute-done.1.refs_2_), channel_id=1, source_target_pairs={{0,1},{1,0},{2,3},{3,2},{4,5},{5,4},{6,7},{7,6},{8,9},{9,8},{10,11... | collective-permute-start | bytes 1572872 | tf_op jit(solution)/shard_map/ppermute | solution.py:304
  57.6 1.0 copy-done.3
  58.6 0.2 code_input.1
  58.8 0.0 collective-permute-done.7.refs_1_.refs_3_
  58.9 0.0 collective-permute-done.8.refs_2_.refs_5_
  58.9 1.6 %collective-permute-start.9 = (bf16[1024,256]{1,0:T(8,128)(2,1)}, bf16[1024,256]{1,0:T(8,128)(2,1)}, u32[]{:S(2)}, u32[]{:S(2)}) collective-permute-start(bf16[1024,256]{1,0:T(8,128)(2,1)} %after.6.refs_6_), channel_id=1, source_target_pairs={{0,4},{2,6},{4,0},{6,2},{8,12},{10,14},{12,8},{14,10},{16,20},{18,... | collective-permute-start | bytes 1572872 | tf_op jit(solution)/shard_map/ppermute | solution.py:274
  60.5 0.0 collective-permute-done.refs_1_
  60.5 7.6 %collective-permute-done.2.refs_3_ = bf16[128,2048]{1,0:T(8,128)(2,1)} collective-permute-done((bf16[128,2048]{1,0:T(8,128)(2,1)}, bf16[128,2048]{1,0:T(8,128)(2,1)}, u32[]{:S(2)}, u32[]{:S(2)}) %collective-permute-start.2) | collective-permute-done | bytes 524320 | tf_op jit(solution)/shard_map/ppermute | solution.py:304
  68.0 3.1 %pick_features.1 = (bf16[256,2048]{1,0:T(8,128)(2,1)}, bf16[256,2048]{1,0:T(8,128)(2,1)}) custom-call(s32[1]{0:T(128)} %bitcast.3.core_ref, bf16[128,2048]{1,0:T(8,128)(2,1)} %refs_0_.1, bf16[128,2048]{1,0:T(8,128)(2,1)} %collective-permute-done.refs_1_, bf16[128,2048]{1,0:T(8,128)(2,1)} %collective-permute-done.1.refs_2_, ...), custom_call_target="tpu_custom_call" | custom-call | bytes 4194304 | tf_op jit(solution)/shard_map/pick_features/pallas_call | solution.py:307
  71.1 0.0 collective-permute-done.10.refs_2_.far_gate_ref
  71.1 0.0 collective-permute-done.9.refs_1_.refs_7_
  71.2 0.1 collective-permute-start.11
  71.2 0.9 convert_element_type.34
  72.1 4.3 %all-to-all-start.1 = ((f16[16,144,128]{2,1,0:T(8,128)(2,1)}), f16[16,144,128]{2,1,0:T(8,128)(2,1)}, u32[]{:S(2)}, u32[]{:S(2)}) async-start(f16[16,144,128]{2,1,0:T(8,128)(2,1)} %convert_element_type.34), calls=%async_computation.1 | async-start | bytes 1179648 | tf_op jit(solution)/shard_map/all_to_all | solution.py:511
  76.4 0.0 collective-permute-done.11.theirs_ref
  76.4 6.6 %add_shares.1 = (f32[256,1024]{1,0:T(8,128)}, f32[256,1024]{1,0:T(8,128)}) custom-call(s32[1]{0:T(128)} %bitcast.1.ctx_ref, s32[1]{0:T(128)} %bitcast.2.ch_ref, bf16[256,2048]{1,0:T(8,128)(2,1)} %get-tuple-element.10.mine_ref, bf16[256,2048]{1,0:T(8,128)(2,1)} %collective-permute-done.11.theirs_ref, bf16[1024,256]{1,0:T(8,128)(2,1)} %get-tuple-element.22.refs_0_, ...), custom_call_target="tpu_custom_call" | custom-call | flops 2147483648 | bytes 10485760 | tf_op jit(solution)/shard_map/add_shares/pallas_call | solution.py:426
  83.0 0.4 collective-permute-start.12
  83.5 2.5 %collective-permute-done.12.arrived_ref = f32[256,1024]{1,0:T(8,128)S(1)} collective-permute-done((f32[256,1024]{1,0:T(8,128)}, f32[256,1024]{1,0:T(8,128)S(1)}, u32[]{:S(2)}, u32[]{:S(2)}) %collective-permute-start.12) | collective-permute-done | bytes 1048608 | tf_op jit(solution)/shard_map/ppermute | solution.py:260
  86.0 1.2 copy-done.5
  87.2 2.4 %seq_grad.1 = (f32[8,272,128]{2,1,0:T(8,128)S(1)}, f32[128,1024]{1,0:T(8,128)S(1)}, f32[128,1024]{1,0:T(8,128)S(1)}) custom-call(s32[1]{0:T(128)} %bitcast.p_ref, f32[256,1024]{1,0:T(8,128)S(1)} %copy-done.5, f32[256,1024]{1,0:T(8,128)S(1)} %collective-permute-done.12.arrived_ref, f32[128,2048]{1,0:T(8,128)S(1)} %copy-done.1, ...), custom_call_target="tpu_custom_call" | custom-call | flops 524288 | bytes 6291456 | tf_op jit(solution)/shard_map/seq_grad/pallas_call | solution.py:344
  89.6 0.9 convert_element_type.32
  90.5 1.5 all-to-all-done.1
  92.0 4.2 %all-to-all-start = ((f16[8,272,128]{2,1,0:T(8,128)(2,1)}), f16[8,272,128]{2,1,0:T(8,128)(2,1)}, u32[]{:S(2)}, u32[]{:S(2)}) async-start(f16[8,272,128]{2,1,0:T(8,128)(2,1)} %convert_element_type.32), calls=%async_computation | async-start | bytes 1114112 | tf_op jit(solution)/shard_map/all_to_all | solution.py:511
  96.3 0.7 broadcast_in_dim.3.filter_ref
  97.0 7.0 %toeplitz.1.t_ref = bf16[8,256,2176]{2,1,0:T(8,128)(2,1)} custom-call(f32[8,1,2176]{2,1,0:T(1,128)} %broadcast_in_dim.3.filter_ref), custom_call_target="tpu_custom_call" | custom-call | flops 8912896 | bytes 8982528 | tf_op jit(solution)/shard_map/toeplitz/pallas_call | solution.py:38
  103.9 0.8 fusion.14
  104.7 1.5 %negate_select_fusion.1.x_ref = f32[16,128,128]{2,1,0:T(8,128)S(1)} fusion(f16[16,144,128]{2,1,0:T(8,128)(2,1)} %all-to-all-done.1, f32[16,128]{1,0:T(8,128)S(1)} %bitcast.23), kind=kLoop, calls=%fused_computation.1 | loop fusion | flops 1835008 | bytes 1581056 | tf_op jit(solution)/shard_map/jit(_where)/select_n | solution.py:99
  106.3 3.2 %stack_input.1.left_ref = bf16[8,256,256]{2,1,0:T(8,128)(2,1)S(1)} custom-call(f32[16,128,128]{2,1,0:T(8,128)S(1)} %negate_select_fusion.1.x_ref), custom_call_target="tpu_custom_call" | custom-call | flops 2097152 | bytes 2097152 | tf_op jit(solution)/shard_map/stack_input/pallas_call | solution.py:76
  109.5 1.4 collective-permute-start.13
  110.9 1.3 all-to-all-done
  112.2 1.1 convert_element_type.33.s_ref
  113.3 11.6 %convolve.1 = f32[16,144,128]{2,1,0:T(8,128)S(1)} custom-call(f32[8,272,128]{2,1,0:T(8,128)S(1)} %convert_element_type.33.s_ref, bf16[8,256,256]{2,1,0:T(8,128)(2,1)S(1)} %stack_input.1.left_ref, bf16[8,256,2176]{2,1,0:T(8,128)(2,1)} %toeplitz.1.t_ref), custom_call_target="tpu_custom_call" | custom-call | flops 7985954816 | bytes 12058624 | tf_op jit(solution)/shard_map/convolve/pallas_call | solution.py:200
  124.9 0.9 convert_element_type.37
  125.8 3.8 %all-to-all-start.2 = ((f16[16,144,128]{2,1,0:T(8,128)(2,1)}), f16[16,144,128]{2,1,0:T(8,128)(2,1)S(1)}, u32[]{:S(2)}, u32[]{:S(2)}) async-start(f16[16,144,128]{2,1,0:T(8,128)(2,1)} %convert_element_type.37), calls=%async_computation.2 | async-start | bytes 1179648 | tf_op jit(solution)/shard_map/all_to_all | solution.py:511
  129.6 0.0 copy-start.6
  129.6 0.0 collective-permute-done.13
  129.6 1.2 broadcast_select_fusion.1
  130.9 0.1 copy-done.6
  131.0 1.1 maximum_multiply_fusion
  132.1 13.1 %all-to-all-done.2 = f16[16,144,128]{2,1,0:T(8,128)(2,1)S(1)} async-done(((f16[16,144,128]{2,1,0:T(8,128)(2,1)}), f16[16,144,128]{2,1,0:T(8,128)(2,1)S(1)}, u32[]{:S(2)}, u32[]{:S(2)}) %all-to-all-start.2) | async-done | bytes 589856 | tf_op jit(solution)/shard_map/all_to_all | solution.py:511
  145.2 0.6 copy.18
  145.9 0.5 negate_select_fusion
  146.4 0.1 copy.16
  146.4 0.3 copy.17
  146.8 1.3 copy.19
  (17 shorter events, 0.1 us)
Async XLA Ops:
  0.6 95.6 %copy-start = (f32[128,2048]{1,0:T(8,128)S(1)}, f32[128,2048]{1,0:T(8,128)}, u32[]{:S(2)}) copy-start(f32[128,2048]{1,0:T(8,128)} %param.11) | copy-start | bytes 3145732
  3.0 27.2 %collective-permute-start.5 = (bf16[1024,256]{1,0:T(8,128)(2,1)}, bf16[1024,256]{1,0:T(8,128)(2,1)}, u32[]{:S(2)}, u32[]{:S(2)}) collective-permute-start(bf16[1024,256]{1,0:T(8,128)(2,1)} %get-tuple-element.23.refs_0_), channel_id=1, source_target_pairs={{0,8},{2,10},{4,12},{6,14},{8,0},{10,2},{12,4},{14,6},{16,24},{18,... | collective-permute-start | bytes 1572872 | tf_op jit(solution)/shard_map/ppermute | solution.py:263
  6.0 24.9 %collective-permute-start.3 = (bf16[1024,256]{1,0:T(8,128)(2,1)}, bf16[1024,256]{1,0:T(8,128)(2,1)}, u32[]{:S(2)}, u32[]{:S(2)}) collective-permute-start(bf16[1024,256]{1,0:T(8,128)(2,1)} %get-tuple-element.22.refs_0_), channel_id=1, source_target_pairs={{0,16},{2,18},{4,20},{6,22},{8,24},{10,26},{12,28},{14,30},{16,0},... | collective-permute-start | bytes 1572872 | tf_op jit(solution)/shard_map/ppermute | solution.py:266
  8.6 25.9 %collective-permute-start.6 = (bf16[1024,256]{1,0:T(8,128)(2,1)}, bf16[1024,256]{1,0:T(8,128)(2,1)S(1)}, u32[]{:S(2)}, u32[]{:S(2)}) collective-permute-start(bf16[1024,256]{1,0:T(8,128)(2,1)} %get-tuple-element.22.refs_0_), channel_id=1, source_target_pairs={{0,4},{2,6},{4,0},{6,2},{8,12},{10,14},{12,8},{14,10},{16,20},{18,... | collective-permute-start | bytes 1572872 | tf_op jit(solution)/shard_map/ppermute | solution.py:274
  10.2 31.1 %collective-permute-start.1 = (bf16[128,2048]{1,0:T(8,128)(2,1)}, bf16[128,2048]{1,0:T(8,128)(2,1)}, u32[]{:S(2)}, u32[]{:S(2)}) collective-permute-start(bf16[128,2048]{1,0:T(8,128)(2,1)} %refs_0_.1), channel_id=1, source_target_pairs={{0,8},{2,10},{4,12},{6,14},{8,0},{10,2},{12,4},{14,6},{16,24},{18,... | collective-permute-start | bytes 1572872 | tf_op jit(solution)/shard_map/ppermute | solution.py:263
  30.9 7.9 %copy-start.1 = (f32[128,2048]{1,0:T(8,128)S(1)}, f32[128,2048]{1,0:T(8,128)}, u32[]{:S(2)}) copy-start(f32[128,2048]{1,0:T(8,128)} %gate_ref.1) | copy-start | bytes 3145732
  30.9 24.4 %collective-permute-start.4 = (bf16[1024,256]{1,0:T(8,128)(2,1)}, bf16[1024,256]{1,0:T(8,128)(2,1)S(1)}, u32[]{:S(2)}, u32[]{:S(2)}) collective-permute-start(bf16[1024,256]{1,0:T(8,128)(2,1)} %after.4), channel_id=1, source_target_pairs={{0,24},{2,26},{4,28},{6,30},{8,16},{10,18},{12,20},{14,22},{16,8},... | collective-permute-start | bytes 1572872 | tf_op jit(solution)/shard_map/ppermute | solution.py:270
  34.5 0.8 copy-start.7
  35.3 22.3 %copy-start.4 = (f32[128,2048]{1,0:T(8,128)S(1)}, f32[128,2048]{1,0:T(8,128)}, u32[]{:S(2)}) copy-start(f32[128,2048]{1,0:T(8,128)} %x_ref.1) | copy-start | bytes 3145732
  35.3 23.5 %collective-permute-start.7 = (bf16[1024,256]{1,0:T(8,128)(2,1)}, bf16[1024,256]{1,0:T(8,128)(2,1)}, u32[]{:S(2)}, u32[]{:S(2)}) collective-permute-start(bf16[1024,256]{1,0:T(8,128)(2,1)} %after.5.refs_2_), channel_id=1, source_target_pairs={{0,4},{2,6},{4,0},{6,2},{8,12},{10,14},{12,8},{14,10},{16,20},{18,... | collective-permute-start | bytes 1572872 | tf_op jit(solution)/shard_map/ppermute | solution.py:274
  36.8 22.0 %collective-permute-start.8 = (bf16[1024,256]{1,0:T(8,128)(2,1)}, bf16[1024,256]{1,0:T(8,128)(2,1)}, u32[]{:S(2)}, u32[]{:S(2)}) collective-permute-start(bf16[1024,256]{1,0:T(8,128)(2,1)} %collective-permute-done.3.refs_1_.refs_4_), channel_id=1, source_target_pairs={{0,4},{2,6},{4,0},{6,2},{8,12},{10,14},{12,8},{14,10},{16,20},{18,... | collective-permute-start | bytes 1572872 | tf_op jit(solution)/shard_map/ppermute | solution.py:274
  37.3 23.1 %collective-permute-start = (bf16[128,2048]{1,0:T(8,128)(2,1)}, bf16[128,2048]{1,0:T(8,128)(2,1)}, u32[]{:S(2)}, u32[]{:S(2)}) collective-permute-start(bf16[128,2048]{1,0:T(8,128)(2,1)} %refs_0_.1), channel_id=1, source_target_pairs={{0,1},{1,0},{2,3},{3,2},{4,5},{5,4},{6,7},{7,6},{8,9},{9,8},{10,11... | collective-permute-start | bytes 1572872 | tf_op jit(solution)/shard_map/ppermute | solution.py:304
  41.2 29.9 %collective-permute-start.10 = (f32[128,1024]{1,0:T(8,128)}, f32[128,1024]{1,0:T(8,128)}, u32[]{:S(2)}, u32[]{:S(2)}) collective-permute-start(f32[128,1024]{1,0:T(8,128)} %constant_dynamic-slice_fusion.1), channel_id=1, source_target_pairs={{0,8},{2,10},{4,12},{6,14},{8,0},{10,2},{12,4},{14,6},{16,24},{18,... | collective-permute-start | bytes 1572872 | tf_op jit(solution)/shard_map/ppermute | solution.py:263
  55.3 0.8 copy-start.2
  56.1 12.0 %collective-permute-start.2 = (bf16[128,2048]{1,0:T(8,128)(2,1)}, bf16[128,2048]{1,0:T(8,128)(2,1)}, u32[]{:S(2)}, u32[]{:S(2)}) collective-permute-start(bf16[128,2048]{1,0:T(8,128)(2,1)} %collective-permute-done.1.refs_2_), channel_id=1, source_target_pairs={{0,1},{1,0},{2,3},{3,2},{4,5},{5,4},{6,7},{7,6},{8,9},{9,8},{10,11... | collective-permute-start | bytes 1572872 | tf_op jit(solution)/shard_map/ppermute | solution.py:304
  57.6 1.0 copy-start.3
  58.9 12.3 %collective-permute-start.9 = (bf16[1024,256]{1,0:T(8,128)(2,1)}, bf16[1024,256]{1,0:T(8,128)(2,1)}, u32[]{:S(2)}, u32[]{:S(2)}) collective-permute-start(bf16[1024,256]{1,0:T(8,128)(2,1)} %after.6.refs_6_), channel_id=1, source_target_pairs={{0,4},{2,6},{4,0},{6,2},{8,12},{10,14},{12,8},{14,10},{16,20},{18,... | collective-permute-start | bytes 1572872 | tf_op jit(solution)/shard_map/ppermute | solution.py:274
  71.2 5.2 %collective-permute-start.11 = (bf16[256,2048]{1,0:T(8,128)(2,1)}, bf16[256,2048]{1,0:T(8,128)(2,1)}, u32[]{:S(2)}, u32[]{:S(2)}) collective-permute-start(bf16[256,2048]{1,0:T(8,128)(2,1)} %after.7), channel_id=1, source_target_pairs={{0,2},{2,0},{4,6},{6,4},{8,10},{10,8},{12,14},{14,12},{16,18},{18,... | collective-permute-start | bytes 3145736 | tf_op jit(solution)/shard_map/ppermute | solution.py:260
  72.1 19.8 %all-to-all-start.1 = ((f16[16,144,128]{2,1,0:T(8,128)(2,1)}), f16[16,144,128]{2,1,0:T(8,128)(2,1)}, u32[]{:S(2)}, u32[]{:S(2)}) async-start(f16[16,144,128]{2,1,0:T(8,128)(2,1)} %convert_element_type.34), calls=%async_computation.1 | async-start | bytes 1179648 | tf_op jit(solution)/shard_map/all_to_all | solution.py:511
  83.0 2.9 %collective-permute-start.12 = (f32[256,1024]{1,0:T(8,128)}, f32[256,1024]{1,0:T(8,128)S(1)}, u32[]{:S(2)}, u32[]{:S(2)}) collective-permute-start(f32[256,1024]{1,0:T(8,128)} %get-tuple-element.13), channel_id=1, source_target_pairs={{0,2},{2,0},{4,6},{6,4},{8,10},{10,8},{12,14},{14,12},{16,18},{18,... | collective-permute-start | bytes 3145736 | tf_op jit(solution)/shard_map/ppermute | solution.py:260
  86.0 1.2 copy-start.5
  92.0 20.3 %all-to-all-start = ((f16[8,272,128]{2,1,0:T(8,128)(2,1)}), f16[8,272,128]{2,1,0:T(8,128)(2,1)}, u32[]{:S(2)}, u32[]{:S(2)}) async-start(f16[8,272,128]{2,1,0:T(8,128)(2,1)} %convert_element_type.32), calls=%async_computation | async-start | bytes 1114112 | tf_op jit(solution)/shard_map/all_to_all | solution.py:511
  109.5 20.2 %collective-permute-start.13 = (f32[128,1024]{1,0:T(8,128)S(1)}, f32[128,1024]{1,0:T(8,128)}, u32[]{:S(2)}, u32[]{:S(2)}) collective-permute-start(f32[128,1024]{1,0:T(8,128)S(1)} %get-tuple-element.16), channel_id=1, source_target_pairs={{0,8},{2,10},{4,12},{6,14},{8,0},{10,2},{12,4},{14,6},{16,24},{18,... | collective-permute-start | bytes 1572872 | tf_op jit(solution)/shard_map/ppermute | solution.py:263
  125.8 19.4 %all-to-all-start.2 = ((f16[16,144,128]{2,1,0:T(8,128)(2,1)}), f16[16,144,128]{2,1,0:T(8,128)(2,1)S(1)}, u32[]{:S(2)}, u32[]{:S(2)}) async-start(f16[16,144,128]{2,1,0:T(8,128)(2,1)} %convert_element_type.37), calls=%async_computation.2 | async-start | bytes 1179648 | tf_op jit(solution)/shard_map/all_to_all | solution.py:511
  129.6 1.4 copy-start.6

commit v5 on v4

--- a/solution.py
+++ b/solution.py
@@ -442,7 +442,7 @@
     )(ctx.reshape(1), ch.reshape(1), mine, theirs, *shares, *before)
 
 
-def project(cotangent, out_weight, place, *waited):
+def project(cotangent, out_weight, place, waited, between):
     channels, features = out_weight.shape
     half = channels // 2
     near = lax.dynamic_slice_in_dim(out_weight, place.p * half, half, 0)
@@ -458,7 +458,8 @@
     held.append(along_y(after(paired, *held[0][1:])))
     held.append(along_y(far))
     held.append(along_y(after(far_paired, *held[1][1:], *held[2][1:])))
-    mine, theirs = gather_cotangent(cotangent, features, place, [*held[3][1:], *waited])
+    made = between(held[2][-1])
+    mine, theirs = gather_cotangent(cotangent, features, place, [*held[3][1:], waited, made])
     shares = [
         ((other // 2, other % 2, shift), held[other][shift]) for other in range(4) for shift in range(place.ys)
     ]
@@ -466,7 +467,7 @@
     for some in (shares,):
         sums = add_shares([at for at, _ in some], mine, theirs, [v for _, v in some], sums, place)
     own, other = sums
-    return own, place.swap_core(other), far_paired
+    return own, place.swap_core(other), made
 
 
 def code_kernel(x_ref, *refs):
@@ -514,8 +515,10 @@
         return blocks.reshape((2, 2, devices // 4) + blocks.shape[1:]).swapaxes(0, 1).reshape(blocks.shape)
 
     far_gate = place.swap_pair(lax.dynamic_slice_in_dim(gate_value, (1 - place.p) * half, half, 1))
-    total, arrived, late = project(cotangent, out_weight, place, far_gate)
-    code = exchange(code_blocks(conv_input, devices, late).astype(jnp.float16))
+    total, arrived, code = project(
+        cotangent, out_weight, place, far_gate, lambda earlier: code_blocks(conv_input, devices, earlier)
+    )
+    code = exchange(code.astype(jnp.float16))
     input_blocks = decoded(code[:, :tok], code[:, tok : tok + 1])
     first_group = (place.p * half + place.block * own) // per_group
     moved = toeplitz(lax.dynamic_slice_in_dim(filters, first_group, groups, 0), tok)

time: 149 us -> 148 us (level)
  local copies, waits for them, and re-layouts: 10.2 us -> 17.4 us
  other arithmetic: 8.96 us -> 6.09 us
  starting transfers between devices: 34.4 us -> 32.2 us
  waiting for transfers between devices: 59.4 us -> 57.3 us
  Pallas kernels: 34.1 us -> 32.6 us
    unnamed x17 -> x45, local copies, waits for them, and re-layouts: 5.32 us -> 12.7 us
    ppermute x4, waiting for transfers between devices: 0.01 us -> 5.47 us  [along_y(): lax.ppermute(v, 'ctx', [(self.index(h, p, y, c), self.index(h, p, (y + sh...]
    ppermute x2, waiting for transfers between devices: 7.59 us -> 2.14 us  [along_ch(): lax.ppermute(v, 'ch', [(j, (j + s) % parts) for j in range(parts)])]
    ppermute x1, waiting for transfers between devices: 11.6 us -> 9.04 us  [swap_half_and_pair(): return lax.ppermute(v, 'ctx', pairs)]
    ppermute x4, starting transfers between devices: 7.36 us -> 4.8 us  [swap_pair(): lax.ppermute(v, 'ctx', [(self.index(h, p, y, c), self.index(h, 1 - p, y,...]
    all_to_all x3, waiting for transfers between devices: 15.9 us -> 17.7 us  [exchange(): lax.all_to_all(blocks, 'ctx', 0, 0, tiled=True, axis_index_groups=groups)]
    pallas_call x1, Pallas kernels: 2.39 us -> 0.8 us  [seq_blocks_of(): pl.pallas_call(seq_kernel, grid_spec=pltpu.PrefetchScalarGridSpec(num_sca...]
  transfers between devices with their start and end apart: 17 -> 17, of which waited for: 9 -> 11; matrix products, arithmetic and copies ran while one was open for 7% -> 5% of each run, Pallas kernels for 23% -> 22%
where the time goes in v5:
time: 148 us; the launch traced here: 147 us
  waiting for transfers between devices  57.3 us (39%)
  Pallas kernels  32.6 us (22%)
  starting transfers between devices  32.2 us (22%)
  local copies, waits for them, and re-layouts  17.4 us (12%)
  other arithmetic  6.09 us (4%)
    ppermute x4, waiting for transfers between devices, swap_pair(): lax.ppermute(v, 'ctx', [(self.index(h, p, y, c), self.index(h, 1 - p, y,...  20.3 us
    all_to_all x3, waiting for transfers between devices, exchange(): lax.all_to_all(blocks, 'ctx', 0, 0, tiled=True, axis_index_groups=groups)  17.7 us
    unnamed x45, local copies, waits for them, and re-layouts  12.7 us
    all_to_all x3, starting transfers between devices, exchange(): lax.all_to_all(blocks, 'ctx', 0, 0, tiled=True, axis_index_groups=groups)  12.3 us
    pallas_call x1, Pallas kernels, convolve(): pl.pallas_call(functools.partial(conv_kernel, scale, lag_own), grid=(grou...  11.6 us
    ppermute x1, waiting for transfers between devices, swap_half_and_pair(): return lax.ppermute(v, 'ctx', pairs)  9.04 us
    pallas_call x1, Pallas kernels, toeplitz(): pl.pallas_call(toeplitz_kernel, grid=(groups,), in_specs=[pl.BlockSpec((1...  7.03 us
    pallas_call x1, Pallas kernels, add_shares(): pl.pallas_call(functools.partial(share_kernel, where, place.ys, parts), g...  6.7 us
  transfers between devices with their start and end apart: 17, of which 11 were waited for; matrix products, arithmetic and copies ran while one was open for 5% of the time, Pallas kernels for 22%

profile of v5, /device:TPU:0, one launch (start us, length us, event | category | flops | bytes accessed | tf_op | source)
XLA Modules:
  0.0 146.5 jit_solution(4238341043443674049)
XLA Ops:
  0.6 0.0 copy-start
  0.7 2.1 %constant_dynamic-slice_fusion.2 = (bf16[1024,256]{1,0:T(8,128)(2,1)}, bf16[1024,256]{1,0:T(8,128)(2,1)S(1)}) fusion(bf16[2048,256]{1,0:T(8,128)(2,1)} %param.7, s32[]{:T(128)S(6)} %select_n.50, s32[]{:T(128)S(6)} %select_n.49), kind=kLoop, calls=%fused_computation.32 | loop fusion | bytes 2097160 | tf_op jit(solution)/shard_map/dynamic_slice | solution.py:448
  2.8 3.0 %collective-permute-start.5 = (bf16[1024,256]{1,0:T(8,128)(2,1)S(1)}, bf16[1024,256]{1,0:T(8,128)(2,1)S(1)}, u32[]{:S(2)}, u32[]{:S(2)}) collective-permute-start(bf16[1024,256]{1,0:T(8,128)(2,1)S(1)} %get-tuple-element.23.refs_0_), channel_id=1, source_target_pairs={{0,8},{2,10},{4,12},{6,14},{8,0},{10,2},{12,4},{14,6},{16,24},{18,... | collective-permute-start | bytes 1572872 | tf_op jit(solution)/shard_map/ppermute | solution.py:263
  5.9 1.5 %collective-permute-start.6 = (bf16[1024,256]{1,0:T(8,128)(2,1)}, bf16[1024,256]{1,0:T(8,128)(2,1)S(1)}, u32[]{:S(2)}, u32[]{:S(2)}) collective-permute-start(bf16[1024,256]{1,0:T(8,128)(2,1)} %get-tuple-element.22.refs_0_), channel_id=1, source_target_pairs={{0,4},{2,6},{4,0},{6,2},{8,12},{10,14},{12,8},{14,10},{16,20},{18,... | collective-permute-start | bytes 1572872 | tf_op jit(solution)/shard_map/ppermute | solution.py:274
  7.4 2.6 %collective-permute-start.3 = (bf16[1024,256]{1,0:T(8,128)(2,1)}, bf16[1024,256]{1,0:T(8,128)(2,1)S(1)}, u32[]{:S(2)}, u32[]{:S(2)}) collective-permute-start(bf16[1024,256]{1,0:T(8,128)(2,1)} %get-tuple-element.22.refs_0_), channel_id=1, source_target_pairs={{0,16},{2,18},{4,20},{6,22},{8,24},{10,26},{12,28},{14,30},{16,0},... | collective-permute-start | bytes 1572872 | tf_op jit(solution)/shard_map/ppermute | solution.py:266
  10.0 0.4 collective-permute-start.1
  10.4 17.8 %collective-permute-done.5.refs_0_ = bf16[1024,256]{1,0:T(8,128)(2,1)S(1)} collective-permute-done((bf16[1024,256]{1,0:T(8,128)(2,1)S(1)}, bf16[1024,256]{1,0:T(8,128)(2,1)S(1)}, u32[]{:S(2)}, u32[]{:S(2)}) %collective-permute-start.5) | collective-permute-done | bytes 524320 | tf_op jit(solution)/shard_map/ppermute | solution.py:263
  28.3 0.0 collective-permute-done.6.refs_1_
  28.3 0.8 copy-done.21
  29.1 0.8 copy-done.18
  29.9 3.0 %collective-permute-start.7 = (bf16[1024,256]{1,0:T(8,128)(2,1)}, bf16[1024,256]{1,0:T(8,128)(2,1)}, u32[]{:S(2)}, u32[]{:S(2)}) collective-permute-start(bf16[1024,256]{1,0:T(8,128)(2,1)} %after.5.refs_2_), channel_id=1, source_target_pairs={{0,4},{2,6},{4,0},{6,2},{8,12},{10,14},{12,8},{14,10},{16,20},{18,... | collective-permute-start | bytes 1572872 | tf_op jit(solution)/shard_map/ppermute | solution.py:274
  32.9 0.1 collective-permute-done.3.refs_1_.refs_4_
  33.0 0.8 copy-done.19
  33.8 3.0 %collective-permute-start.4 = (bf16[1024,256]{1,0:T(8,128)(2,1)}, bf16[1024,256]{1,0:T(8,128)(2,1)}, u32[]{:S(2)}, u32[]{:S(2)}) collective-permute-start(bf16[1024,256]{1,0:T(8,128)(2,1)} %after.4), channel_id=1, source_target_pairs={{0,24},{2,26},{4,28},{6,30},{8,16},{10,18},{12,20},{14,22},{16,8},... | collective-permute-start | bytes 1572872 | tf_op jit(solution)/shard_map/ppermute | solution.py:270
  36.9 0.0 collective-permute-start.8
  36.9 1.5 %collective-permute-start = (bf16[128,2048]{1,0:T(8,128)(2,1)}, bf16[128,2048]{1,0:T(8,128)(2,1)}, u32[]{:S(2)}, u32[]{:S(2)}) collective-permute-start(bf16[128,2048]{1,0:T(8,128)(2,1)} %refs_0_.1), channel_id=1, source_target_pairs={{0,1},{1,0},{2,3},{3,2},{4,5},{5,4},{6,7},{7,6},{8,9},{9,8},{10,11... | collective-permute-start | bytes 1572872 | tf_op jit(solution)/shard_map/ppermute | solution.py:304
  38.4 2.5 %collective-permute-done.1.refs_2_ = bf16[128,2048]{1,0:T(8,128)(2,1)} collective-permute-done((bf16[128,2048]{1,0:T(8,128)(2,1)}, bf16[128,2048]{1,0:T(8,128)(2,1)}, u32[]{:S(2)}, u32[]{:S(2)}) %collective-permute-start.1) | collective-permute-done | bytes 524320 | tf_op jit(solution)/shard_map/ppermute | solution.py:263
  40.8 1.5 %collective-permute-start.2 = (bf16[128,2048]{1,0:T(8,128)(2,1)}, bf16[128,2048]{1,0:T(8,128)(2,1)}, u32[]{:S(2)}, u32[]{:S(2)}) collective-permute-start(bf16[128,2048]{1,0:T(8,128)(2,1)} %collective-permute-done.1.refs_2_), channel_id=1, source_target_pairs={{0,1},{1,0},{2,3},{3,2},{4,5},{5,4},{6,7},{7,6},{8,9},{9,8},{10,11... | collective-permute-start | bytes 1572872 | tf_op jit(solution)/shard_map/ppermute | solution.py:304
  42.3 0.8 constant_dynamic-slice_fusion.1
  43.2 2.9 %collective-permute-done.7.refs_1_.refs_3_ = bf16[1024,256]{1,0:T(8,128)(2,1)} collective-permute-done((bf16[1024,256]{1,0:T(8,128)(2,1)}, bf16[1024,256]{1,0:T(8,128)(2,1)}, u32[]{:S(2)}, u32[]{:S(2)}) %collective-permute-start.7) | collective-permute-done | bytes 524320 | tf_op jit(solution)/shard_map/ppermute | solution.py:274
  46.0 9.0 %collective-permute-done.4.refs_0_ = bf16[1024,256]{1,0:T(8,128)(2,1)} collective-permute-done((bf16[1024,256]{1,0:T(8,128)(2,1)}, bf16[1024,256]{1,0:T(8,128)(2,1)}, u32[]{:S(2)}, u32[]{:S(2)}) %collective-permute-start.4) | collective-permute-done | bytes 524320 | tf_op jit(solution)/shard_map/ppermute | solution.py:270
  55.1 0.8 copy-done.6
  55.9 1.5 %collective-permute-start.9 = (bf16[1024,256]{1,0:T(8,128)(2,1)}, bf16[1024,256]{1,0:T(8,128)(2,1)S(1)}, u32[]{:S(2)}, u32[]{:S(2)}) collective-permute-start(bf16[1024,256]{1,0:T(8,128)(2,1)} %after.6.refs_6_), channel_id=1, source_target_pairs={{0,4},{2,6},{4,0},{6,2},{8,12},{10,14},{12,8},{14,10},{16,20},{18,... | collective-permute-start | bytes 1572872 | tf_op jit(solution)/shard_map/ppermute | solution.py:274
  57.4 2.1 %collective-permute-done.2.refs_3_ = bf16[128,2048]{1,0:T(8,128)(2,1)} collective-permute-done((bf16[128,2048]{1,0:T(8,128)(2,1)}, bf16[128,2048]{1,0:T(8,128)(2,1)}, u32[]{:S(2)}, u32[]{:S(2)}) %collective-permute-start.2) | collective-permute-done | bytes 524320 | tf_op jit(solution)/shard_map/ppermute | solution.py:304
  59.6 3.1 %pick_features.1 = (bf16[256,2048]{1,0:T(8,128)(2,1)}, bf16[256,2048]{1,0:T(8,128)(2,1)}) custom-call(s32[1]{0:T(128)} %bitcast.3.core_ref, bf16[128,2048]{1,0:T(8,128)(2,1)} %refs_0_.1, bf16[128,2048]{1,0:T(8,128)(2,1)} %collective-permute-done.refs_1_, bf16[128,2048]{1,0:T(8,128)(2,1)} %collective-permute-done.1.refs_2_, ...), custom_call_target="tpu_custom_call" | custom-call | bytes 4194304 | tf_op jit(solution)/shard_map/pick_features/pallas_call | solution.py:307
  62.7 1.2 copy-done.8
  63.9 0.2 code_input.1.refs_3_
  64.1 1.0 copy-done.1
  65.1 2.6 %collective-permute-done.9.refs_1_.refs_7_ = bf16[1024,256]{1,0:T(8,128)(2,1)S(1)} collective-permute-done((bf16[1024,256]{1,0:T(8,128)(2,1)}, bf16[1024,256]{1,0:T(8,128)(2,1)S(1)}, u32[]{:S(2)}, u32[]{:S(2)}) %collective-permute-start.9) | collective-permute-done | bytes 524320 | tf_op jit(solution)/shard_map/ppermute | solution.py:274
  67.7 0.8 copy-done.20
  68.6 1.3 copy-done.2
  69.8 0.9 convert_element_type.34
  70.7 4.8 %all-to-all-start.1 = ((f16[16,144,128]{2,1,0:T(8,128)(2,1)}), f16[16,144,128]{2,1,0:T(8,128)(2,1)S(1)}, u32[]{:S(2)}, u32[]{:S(2)}) async-start(f16[16,144,128]{2,1,0:T(8,128)(2,1)} %convert_element_type.34), calls=%async_computation.1 | async-start | bytes 1179648 | tf_op jit(solution)/shard_map/all_to_all | solution.py:512
  75.6 6.7 %add_shares.1 = (f32[256,1024]{1,0:T(8,128)}, f32[256,1024]{1,0:T(8,128)}) custom-call(s32[1]{0:T(128)} %bitcast.1.ctx_ref, s32[1]{0:T(128)} %bitcast.2.ch_ref, bf16[256,2048]{1,0:T(8,128)(2,1)} %get-tuple-element.10.mine_ref, bf16[256,2048]{1,0:T(8,128)(2,1)} %collective-permute-done.11.theirs_ref, bf16[1024,256]{1,0:T(8,128)(2,1)} %get-tuple-element.22.refs_0_, ...), custom_call_target="tpu_custom_call" | custom-call | flops 2147483648 | bytes 10485760 | tf_op jit(solution)/shard_map/add_shares/pallas_call | solution.py:426
  82.3 0.5 collective-permute-start.12
  82.8 2.5 %collective-permute-done.12.arrived_ref = f32[256,1024]{1,0:T(8,128)S(1)} collective-permute-done((f32[256,1024]{1,0:T(8,128)}, f32[256,1024]{1,0:T(8,128)S(1)}, u32[]{:S(2)}, u32[]{:S(2)}) %collective-permute-start.12) | collective-permute-done | bytes 1048608 | tf_op jit(solution)/shard_map/ppermute | solution.py:260
  85.3 1.2 copy-done.9
  86.5 0.8 seq_grad.1
  87.3 0.8 copy-done.10
  88.1 0.8 copy-done.12
  88.9 0.9 convert_element_type.32
  89.8 1.3 all-to-all-done.1
  91.1 0.8 copy-done.14
  91.9 3.9 %all-to-all-start = ((f16[8,272,128]{2,1,0:T(8,128)(2,1)}), f16[8,272,128]{2,1,0:T(8,128)(2,1)S(1)}, u32[]{:S(2)}, u32[]{:S(2)}) async-start(f16[8,272,128]{2,1,0:T(8,128)(2,1)} %convert_element_type.32), calls=%async_computation | async-start | bytes 1114112 | tf_op jit(solution)/shard_map/all_to_all | solution.py:512
  95.8 0.7 broadcast_in_dim.3.filter_ref
  96.5 7.0 %toeplitz.1.t_ref = bf16[8,256,2176]{2,1,0:T(8,128)(2,1)} custom-call(f32[8,1,2176]{2,1,0:T(1,128)} %broadcast_in_dim.3.filter_ref), custom_call_target="tpu_custom_call" | custom-call | flops 8912896 | bytes 8982528 | tf_op jit(solution)/shard_map/toeplitz/pallas_call | solution.py:38
  103.6 0.5 negate_select_fusion.1.x_ref
  104.1 3.2 %stack_input.1.left_ref = bf16[8,256,256]{2,1,0:T(8,128)(2,1)S(1)} custom-call(f32[16,128,128]{2,1,0:T(8,128)S(1)} %negate_select_fusion.1.x_ref), custom_call_target="tpu_custom_call" | custom-call | flops 2097152 | bytes 2097152 | tf_op jit(solution)/shard_map/stack_input/pallas_call | solution.py:76
  107.3 1.3 collective-permute-start.13
  108.6 3.3 %all-to-all-done = f16[8,272,128]{2,1,0:T(8,128)(2,1)S(1)} async-done(((f16[8,272,128]{2,1,0:T(8,128)(2,1)}), f16[8,272,128]{2,1,0:T(8,128)(2,1)S(1)}, u32[]{:S(2)}, u32[]{:S(2)}) %all-to-all-start) | async-done | bytes 557088 | tf_op jit(solution)/shard_map/all_to_all | solution.py:512
  112.0 0.1 convert_element_type.33.s_ref
  112.0 11.6 %convolve.1 = f32[16,144,128]{2,1,0:T(8,128)S(1)} custom-call(f32[8,272,128]{2,1,0:T(8,128)S(1)} %convert_element_type.33.s_ref, bf16[8,256,256]{2,1,0:T(8,128)(2,1)S(1)} %stack_input.1.left_ref, bf16[8,256,2176]{2,1,0:T(8,128)(2,1)} %toeplitz.1.t_ref), custom_call_target="tpu_custom_call" | custom-call | flops 7985954816 | bytes 12058624 | tf_op jit(solution)/shard_map/convolve/pallas_call | solution.py:200
  123.6 0.9 convert_element_type.37
  124.5 3.6 %all-to-all-start.2 = ((f16[16,144,128]{2,1,0:T(8,128)(2,1)}), f16[16,144,128]{2,1,0:T(8,128)(2,1)S(1)}, u32[]{:S(2)}, u32[]{:S(2)}) async-start(f16[16,144,128]{2,1,0:T(8,128)(2,1)} %convert_element_type.37), calls=%async_computation.2 | async-start | bytes 1179648 | tf_op jit(solution)/shard_map/all_to_all | solution.py:512
  128.1 0.0 copy-start.17
  128.1 1.2 broadcast_select_fusion.1
  129.3 0.2 copy-done.17
  129.5 1.1 maximum_multiply_fusion
  130.6 13.0 %all-to-all-done.2 = f16[16,144,128]{2,1,0:T(8,128)(2,1)S(1)} async-done(((f16[16,144,128]{2,1,0:T(8,128)(2,1)}), f16[16,144,128]{2,1,0:T(8,128)(2,1)S(1)}, u32[]{:S(2)}, u32[]{:S(2)}) %all-to-all-start.2) | async-done | bytes 589856 | tf_op jit(solution)/shard_map/all_to_all | solution.py:512
  143.7 0.6 copy.18
  144.3 0.5 negate_select_fusion
  144.8 0.1 copy.16
  144.9 0.3 copy.17
  145.2 1.3 copy.19
  (45 shorter events, 0.2 us)
Async XLA Ops:
  0.6 95.2 %copy-start = (f32[128,2048]{1,0:T(8,128)S(1)}, f32[128,2048]{1,0:T(8,128)}, u32[]{:S(2)}) copy-start(f32[128,2048]{1,0:T(8,128)} %param.11) | copy-start | bytes 3145732
  2.8 30.2 %copy-start.16 = (bf16[1024,256]{1,0:T(8,128)(2,1)}, bf16[1024,256]{1,0:T(8,128)(2,1)S(1)}, u32[]{:S(2)}) copy-start(bf16[1024,256]{1,0:T(8,128)(2,1)S(1)} %get-tuple-element.23.refs_0_) | copy-start | bytes 1572868
  2.8 25.4 %collective-permute-start.5 = (bf16[1024,256]{1,0:T(8,128)(2,1)S(1)}, bf16[1024,256]{1,0:T(8,128)(2,1)S(1)}, u32[]{:S(2)}, u32[]{:S(2)}) collective-permute-start(bf16[1024,256]{1,0:T(8,128)(2,1)S(1)} %get-tuple-element.23.refs_0_), channel_id=1, source_target_pairs={{0,8},{2,10},{4,12},{6,14},{8,0},{10,2},{12,4},{14,6},{16,24},{18,... | collective-permute-start | bytes 1572872 | tf_op jit(solution)/shard_map/ppermute | solution.py:263
  5.9 22.4 %collective-permute-start.6 = (bf16[1024,256]{1,0:T(8,128)(2,1)}, bf16[1024,256]{1,0:T(8,128)(2,1)S(1)}, u32[]{:S(2)}, u32[]{:S(2)}) collective-permute-start(bf16[1024,256]{1,0:T(8,128)(2,1)} %get-tuple-element.22.refs_0_), channel_id=1, source_target_pairs={{0,4},{2,6},{4,0},{6,2},{8,12},{10,14},{12,8},{14,10},{16,20},{18,... | collective-permute-start | bytes 1572872 | tf_op jit(solution)/shard_map/ppermute | solution.py:274
  7.4 25.6 %collective-permute-start.3 = (bf16[1024,256]{1,0:T(8,128)(2,1)}, bf16[1024,256]{1,0:T(8,128)(2,1)S(1)}, u32[]{:S(2)}, u32[]{:S(2)}) collective-permute-start(bf16[1024,256]{1,0:T(8,128)(2,1)} %get-tuple-element.22.refs_0_), channel_id=1, source_target_pairs={{0,16},{2,18},{4,20},{6,22},{8,24},{10,26},{12,28},{14,30},{16,0},... | collective-permute-start | bytes 1572872 | tf_op jit(solution)/shard_map/ppermute | solution.py:266
  10.0 30.8 %collective-permute-start.1 = (bf16[128,2048]{1,0:T(8,128)(2,1)}, bf16[128,2048]{1,0:T(8,128)(2,1)}, u32[]{:S(2)}, u32[]{:S(2)}) collective-permute-start(bf16[128,2048]{1,0:T(8,128)(2,1)} %refs_0_.1), channel_id=1, source_target_pairs={{0,8},{2,10},{4,12},{6,14},{8,0},{10,2},{12,4},{14,6},{16,24},{18,... | collective-permute-start | bytes 1572872 | tf_op jit(solution)/shard_map/ppermute | solution.py:263
  28.3 0.8 copy-start.21
  29.1 0.8 copy-start.18
  29.9 12.5 %copy-start.3 = (f32[128,2048]{1,0:T(8,128)S(1)}, f32[128,2048]{1,0:T(8,128)}, u32[]{:S(2)}) copy-start(f32[128,2048]{1,0:T(8,128)} %gate_ref.1) | copy-start | bytes 3145732
  29.9 16.2 %collective-permute-start.7 = (bf16[1024,256]{1,0:T(8,128)(2,1)}, bf16[1024,256]{1,0:T(8,128)(2,1)}, u32[]{:S(2)}, u32[]{:S(2)}) collective-permute-start(bf16[1024,256]{1,0:T(8,128)(2,1)} %after.5.refs_2_), channel_id=1, source_target_pairs={{0,4},{2,6},{4,0},{6,2},{8,12},{10,14},{12,8},{14,10},{16,20},{18,... | collective-permute-start | bytes 1572872 | tf_op jit(solution)/shard_map/ppermute | solution.py:274
  33.0 0.8 copy-start.19
  33.8 21.3 %collective-permute-start.4 = (bf16[1024,256]{1,0:T(8,128)(2,1)}, bf16[1024,256]{1,0:T(8,128)(2,1)}, u32[]{:S(2)}, u32[]{:S(2)}) collective-permute-start(bf16[1024,256]{1,0:T(8,128)(2,1)} %after.4), channel_id=1, source_target_pairs={{0,24},{2,26},{4,28},{6,30},{8,16},{10,18},{12,20},{14,22},{16,8},... | collective-permute-start | bytes 1572872 | tf_op jit(solution)/shard_map/ppermute | solution.py:270
  36.9 18.2 %collective-permute-start.8 = (bf16[1024,256]{1,0:T(8,128)(2,1)}, bf16[1024,256]{1,0:T(8,128)(2,1)S(1)}, u32[]{:S(2)}, u32[]{:S(2)}) collective-permute-start(bf16[1024,256]{1,0:T(8,128)(2,1)} %copy-done.19), channel_id=1, source_target_pairs={{0,4},{2,6},{4,0},{6,2},{8,12},{10,14},{12,8},{14,10},{16,20},{18,... | collective-permute-start | bytes 1572872 | tf_op jit(solution)/shard_map/ppermute | solution.py:274
  36.9 20.5 %collective-permute-start = (bf16[128,2048]{1,0:T(8,128)(2,1)}, bf16[128,2048]{1,0:T(8,128)(2,1)}, u32[]{:S(2)}, u32[]{:S(2)}) collective-permute-start(bf16[128,2048]{1,0:T(8,128)(2,1)} %refs_0_.1), channel_id=1, source_target_pairs={{0,1},{1,0},{2,3},{3,2},{4,5},{5,4},{6,7},{7,6},{8,9},{9,8},{10,11... | collective-permute-start | bytes 1572872 | tf_op jit(solution)/shard_map/ppermute | solution.py:304
  40.8 18.7 %collective-permute-start.2 = (bf16[128,2048]{1,0:T(8,128)(2,1)}, bf16[128,2048]{1,0:T(8,128)(2,1)}, u32[]{:S(2)}, u32[]{:S(2)}) collective-permute-start(bf16[128,2048]{1,0:T(8,128)(2,1)} %collective-permute-done.1.refs_2_), channel_id=1, source_target_pairs={{0,1},{1,0},{2,3},{3,2},{4,5},{5,4},{6,7},{7,6},{8,9},{9,8},{10,11... | collective-permute-start | bytes 1572872 | tf_op jit(solution)/shard_map/ppermute | solution.py:304
  46.0 19.1 %collective-permute-start.10 = (f32[128,1024]{1,0:T(8,128)}, f32[128,1024]{1,0:T(8,128)S(1)}, u32[]{:S(2)}, u32[]{:S(2)}) collective-permute-start(f32[128,1024]{1,0:T(8,128)} %constant_dynamic-slice_fusion.1), channel_id=1, source_target_pairs={{0,8},{2,10},{4,12},{6,14},{8,0},{10,2},{12,4},{14,6},{16,24},{18,... | collective-permute-start | bytes 1572872 | tf_op jit(solution)/shard_map/ppermute | solution.py:263
  55.1 0.8 copy-start.6
  55.9 6.8 %copy-start.7 = (bf16[1024,256]{1,0:T(8,128)(2,1)S(1)}, bf16[1024,256]{1,0:T(8,128)(2,1)}, u32[]{:S(2)}) copy-start(bf16[1024,256]{1,0:T(8,128)(2,1)} %copy-done.6) | copy-start | bytes 1572868
  55.9 11.9 %collective-permute-start.9 = (bf16[1024,256]{1,0:T(8,128)(2,1)}, bf16[1024,256]{1,0:T(8,128)(2,1)S(1)}, u32[]{:S(2)}, u32[]{:S(2)}) collective-permute-start(bf16[1024,256]{1,0:T(8,128)(2,1)} %after.6.refs_6_), channel_id=1, source_target_pairs={{0,4},{2,6},{4,0},{6,2},{8,12},{10,14},{12,8},{14,10},{16,20},{18,... | collective-permute-start | bytes 1572872 | tf_op jit(solution)/shard_map/ppermute | solution.py:274
  62.7 1.2 copy-start.8
  64.1 1.0 copy-start.1
  65.1 2.6 %copy-start.4 = (f32[128,1024]{1,0:T(8,128)}, f32[128,1024]{1,0:T(8,128)S(1)}, u32[]{:S(2)}) copy-start(f32[128,1024]{1,0:T(8,128)S(1)} %collective-permute-done.10.refs_2_.far_gate_ref) | copy-start | bytes 1572868
  67.7 0.8 copy-start.20
  68.6 1.3 copy-start.2
  68.6 7.0 %collective-permute-start.11 = (bf16[256,2048]{1,0:T(8,128)(2,1)}, bf16[256,2048]{1,0:T(8,128)(2,1)}, u32[]{:S(2)}, u32[]{:S(2)}) collective-permute-start(bf16[256,2048]{1,0:T(8,128)(2,1)} %after.7), channel_id=1, source_target_pairs={{0,2},{2,0},{4,6},{6,4},{8,10},{10,8},{12,14},{14,12},{16,18},{18,... | collective-permute-start | bytes 3145736 | tf_op jit(solution)/shard_map/ppermute | solution.py:260
  70.7 20.4 %all-to-all-start.1 = ((f16[16,144,128]{2,1,0:T(8,128)(2,1)}), f16[16,144,128]{2,1,0:T(8,128)(2,1)S(1)}, u32[]{:S(2)}, u32[]{:S(2)}) async-start(f16[16,144,128]{2,1,0:T(8,128)(2,1)} %convert_element_type.34), calls=%async_computation.1 | async-start | bytes 1179648 | tf_op jit(solution)/shard_map/all_to_all | solution.py:512
  75.6 9.7 %copy-start.5 = (f32[128,1024]{1,0:T(8,128)S(1)}, f32[128,1024]{1,0:T(8,128)}, u32[]{:S(2)}) copy-start(f32[128,1024]{1,0:T(8,128)} %copy-done.4) | copy-start | bytes 1572868
  82.3 3.0 %collective-permute-start.12 = (f32[256,1024]{1,0:T(8,128)}, f32[256,1024]{1,0:T(8,128)S(1)}, u32[]{:S(2)}, u32[]{:S(2)}) collective-permute-start(f32[256,1024]{1,0:T(8,128)} %get-tuple-element.13), channel_id=1, source_target_pairs={{0,2},{2,0},{4,6},{6,4},{8,10},{10,8},{12,14},{14,12},{16,18},{18,... | collective-permute-start | bytes 3145736 | tf_op jit(solution)/shard_map/ppermute | solution.py:260
  85.3 1.2 copy-start.9
  87.3 0.8 copy-start.10
  88.1 0.8 copy-start.12
  91.1 0.8 copy-start.14
  91.9 20.0 %all-to-all-start = ((f16[8,272,128]{2,1,0:T(8,128)(2,1)}), f16[8,272,128]{2,1,0:T(8,128)(2,1)S(1)}, u32[]{:S(2)}, u32[]{:S(2)}) async-start(f16[8,272,128]{2,1,0:T(8,128)(2,1)} %convert_element_type.32), calls=%async_computation | async-start | bytes 1114112 | tf_op jit(solution)/shard_map/all_to_all | solution.py:512
  96.5 7.0 %copy-start.15 = (f16[16,144,128]{2,1,0:T(8,128)(2,1)S(1)}, f16[16,144,128]{2,1,0:T(8,128)(2,1)}, u32[]{:S(2)}) copy-start(f16[16,144,128]{2,1,0:T(8,128)(2,1)} %copy-done.14) | copy-start | bytes 1769476
  104.1 3.2 %copy-start.13 = (f32[128,1024]{1,0:T(8,128)S(1)}, f32[128,1024]{1,0:T(8,128)}, u32[]{:S(2)}) copy-start(f32[128,1024]{1,0:T(8,128)} %copy-done.12) | copy-start | bytes 1572868
  107.3 20.8 %collective-permute-start.13 = (f32[128,1024]{1,0:T(8,128)S(1)}, f32[128,1024]{1,0:T(8,128)}, u32[]{:S(2)}, u32[]{:S(2)}) collective-permute-start(f32[128,1024]{1,0:T(8,128)S(1)} %copy-done.13), channel_id=1, source_target_pairs={{0,8},{2,10},{4,12},{6,14},{8,0},{10,2},{12,4},{14,6},{16,24},{18,... | collective-permute-start | bytes 1572872 | tf_op jit(solution)/shard_map/ppermute | solution.py:263
  123.6 4.5 %copy-start.11 = (f32[128,1024]{1,0:T(8,128)S(1)}, f32[128,1024]{1,0:T(8,128)}, u32[]{:S(2)}) copy-start(f32[128,1024]{1,0:T(8,128)} %copy-done.10) | copy-start | bytes 1572868
  124.5 19.1 %all-to-all-start.2 = ((f16[16,144,128]{2,1,0:T(8,128)(2,1)}), f16[16,144,128]{2,1,0:T(8,128)(2,1)S(1)}, u32[]{:S(2)}, u32[]{:S(2)}) async-start(f16[16,144,128]{2,1,0:T(8,128)(2,1)} %convert_element_type.37), calls=%async_computation.2 | async-start | bytes 1179648 | tf_op jit(solution)/shard_map/all_to_all | solution.py:512
  128.1 1.4 copy-start.17

commit v6 on v5

--- a/solution.py
+++ b/solution.py
@@ -234,6 +234,7 @@
         out_specs=ANY,
         out_shape=jax.ShapeDtypeStruct(value.shape, value.dtype),
         input_output_aliases={0: 0},
+        compiler_params=pltpu.CompilerParams(vmem_limit_bytes=1 * 1024 * 1024),
         cost_estimate=pl.CostEstimate(flops=0, bytes_accessed=0, transcendentals=0),
         name="after",
     )(value, *earlier)
@@ -309,7 +310,7 @@
         in_specs=[SMEM] + [VMEM] * (2 * parts),
         out_specs=[VMEM] * 2,
         out_shape=[whole, whole],
-        compiler_params=pltpu.CompilerParams(vmem_limit_bytes=GRANT),
+        compiler_params=pltpu.CompilerParams(vmem_limit_bytes=10 * 1024 * 1024),
         cost_estimate=pl.CostEstimate(flops=0, bytes_accessed=8 * tok * held * parts, transcendentals=0),
         name="pick_features",
     )(place.core.reshape(1), *along_ch(cotangent), *along_ch(far))
@@ -364,7 +365,7 @@
             jax.ShapeDtypeStruct((tok, half), jnp.float32),
             jax.ShapeDtypeStruct((tok, half), jnp.float32),
         ],
-        compiler_params=pltpu.CompilerParams(vmem_limit_bytes=24 * 1024 * 1024),
+        compiler_params=pltpu.CompilerParams(vmem_limit_bytes=12 * 1024 * 1024),
         cost_estimate=pl.CostEstimate(
             flops=2 * tok * channels, bytes_accessed=24 * tok * channels, transcendentals=0
         ),
@@ -490,7 +491,7 @@
         in_specs=[VMEM] + [ANY] * len(awaited),
         out_specs=VMEM,
         out_shape=jax.ShapeDtypeStruct((devices, tok + ROW_TILE, channels // devices), jnp.float32),
-        compiler_params=pltpu.CompilerParams(vmem_limit_bytes=32 * 1024 * 1024),
+        compiler_params=pltpu.CompilerParams(vmem_limit_bytes=8 * 1024 * 1024),
         cost_estimate=pl.CostEstimate(flops=4 * tok * channels, bytes_accessed=8 * tok * channels, transcendentals=0),
         name="code_input",
     )(value, *awaited)

time: 148 us -> 144 us (0.973)
  local copies, waits for them, and re-layouts: 17.4 us -> 9.9 us
  waiting for transfers between devices: 57.3 us -> 61.1 us
  Pallas kernels: 32.6 us -> 30.6 us
  other arithmetic: 6.09 us -> 7.91 us
    unnamed x45 -> x43, local copies, waits for them, and re-layouts: 12.7 us -> 6.74 us
    ppermute x4, waiting for transfers between devices: 20.3 us -> 25.8 us  [swap_pair(): lax.ppermute(v, 'ctx', [(self.index(h, p, y, c), self.index(h, 1 - p, y,...]
    pallas_call x1, Pallas kernels: 3.1 us -> 1.2 us  [gather_cotangent(): pl.pallas_call(functools.partial(pick_kernel, features, parts), in_specs=...]
    all_to_all x3, waiting for transfers between devices: 17.7 us -> 16 us  [exchange(): lax.all_to_all(blocks, 'ctx', 0, 0, tiled=True, axis_index_groups=groups)]
  transfers between devices with their start and end apart: 17 -> 17, of which waited for: 11 -> 12; matrix products, arithmetic and copies ran while one was open for 5% -> 6% of each run, Pallas kernels for 22% -> 21%
where the time goes in v6:
time: 144 us; the launch traced here: 143 us
  waiting for transfers between devices  61.1 us (42%)
  starting transfers between devices  32.6 us (23%)
  Pallas kernels  30.6 us (21%)
  local copies, waits for them, and re-layouts  9.9 us (7%)
  other arithmetic  7.91 us (5%)
    ppermute x4, waiting for transfers between devices, swap_pair(): lax.ppermute(v, 'ctx', [(self.index(h, p, y, c), self.index(h, 1 - p, y,...  25.8 us
    all_to_all x3, waiting for transfers between devices, exchange(): lax.all_to_all(blocks, 'ctx', 0, 0, tiled=True, axis_index_groups=groups)  16 us
    all_to_all x3, starting transfers between devices, exchange(): lax.all_to_all(blocks, 'ctx', 0, 0, tiled=True, axis_index_groups=groups)  12 us
    pallas_call x1, Pallas kernels, convolve(): pl.pallas_call(functools.partial(conv_kernel, scale, lag_own), grid=(grou...  11.5 us
    ppermute x1, waiting for transfers between devices, swap_half_and_pair(): return lax.ppermute(v, 'ctx', pairs)  10.1 us
    pallas_call x1, Pallas kernels, toeplitz(): pl.pallas_call(toeplitz_kernel, grid=(groups,), in_specs=[pl.BlockSpec((1...  6.97 us
    unnamed x43, local copies, waits for them, and re-layouts  6.74 us
    pallas_call x1, Pallas kernels, add_shares(): pl.pallas_call(functools.partial(share_kernel, where, place.ys, parts), g...  6.69 us
  transfers between devices with their start and end apart: 17, of which 12 were waited for; matrix products, arithmetic and copies ran while one was open for 6% of the time, Pallas kernels for 21%

profile of v6, /device:TPU:0, one launch (start us, length us, event | category | flops | bytes accessed | tf_op | source)
XLA Modules:
  0.0 143.1 jit_solution(8402412597185956104)
XLA Ops:
  0.6 0.0 copy-start
  0.7 1.4 constant_dynamic-slice_fusion.2
  2.1 3.1 %collective-permute-start.5 = (bf16[1024,256]{1,0:T(8,128)(2,1)S(1)}, bf16[1024,256]{1,0:T(8,128)(2,1)S(1)}, u32[]{:S(2)}, u32[]{:S(2)}) collective-permute-start(bf16[1024,256]{1,0:T(8,128)(2,1)S(1)} %get-tuple-element.23.refs_0_), channel_id=1, source_target_pairs={{0,8},{2,10},{4,12},{6,14},{8,0},{10,2},{12,4},{14,6},{16,24},{18,... | collective-permute-start | bytes 1572872 | tf_op jit(solution)/shard_map/ppermute | solution.py:264
  5.2 1.5 %collective-permute-start.6 = (bf16[1024,256]{1,0:T(8,128)(2,1)S(1)}, bf16[1024,256]{1,0:T(8,128)(2,1)S(1)}, u32[]{:S(2)}, u32[]{:S(2)}) collective-permute-start(bf16[1024,256]{1,0:T(8,128)(2,1)S(1)} %get-tuple-element.22.refs_0_), channel_id=1, source_target_pairs={{0,4},{2,6},{4,0},{6,2},{8,12},{10,14},{12,8},{14,10},{16,20},{18,... | collective-permute-start | bytes 1572872 | tf_op jit(solution)/shard_map/ppermute | solution.py:275
  6.7 2.6 %collective-permute-start.3 = (bf16[1024,256]{1,0:T(8,128)(2,1)S(1)}, bf16[1024,256]{1,0:T(8,128)(2,1)S(1)}, u32[]{:S(2)}, u32[]{:S(2)}) collective-permute-start(bf16[1024,256]{1,0:T(8,128)(2,1)S(1)} %get-tuple-element.22.refs_0_), channel_id=1, source_target_pairs={{0,16},{2,18},{4,20},{6,22},{8,24},{10,26},{12,28},{14,30},{16,0},... | collective-permute-start | bytes 1572872 | tf_op jit(solution)/shard_map/ppermute | solution.py:267
  9.3 0.4 collective-permute-start.1
  9.8 18.1 %collective-permute-done.5.refs_0_ = bf16[1024,256]{1,0:T(8,128)(2,1)S(1)} collective-permute-done((bf16[1024,256]{1,0:T(8,128)(2,1)S(1)}, bf16[1024,256]{1,0:T(8,128)(2,1)S(1)}, u32[]{:S(2)}, u32[]{:S(2)}) %collective-permute-start.5) | collective-permute-done | bytes 524320 | tf_op jit(solution)/shard_map/ppermute | solution.py:264
  27.8 0.0 collective-permute-done.6.refs_1_
  27.9 0.0 copy-start.1
  27.9 3.1 %collective-permute-start.7 = (bf16[1024,256]{1,0:T(8,128)(2,1)S(1)}, bf16[1024,256]{1,0:T(8,128)(2,1)S(1)}, u32[]{:S(2)}, u32[]{:S(2)}) collective-permute-start(bf16[1024,256]{1,0:T(8,128)(2,1)S(1)} %after.5.refs_2_), channel_id=1, source_target_pairs={{0,4},{2,6},{4,0},{6,2},{8,12},{10,14},{12,8},{14,10},{16,20},{18,... | collective-permute-start | bytes 1572872 | tf_op jit(solution)/shard_map/ppermute | solution.py:275
  31.0 1.2 collective-permute-done.3.refs_1_.refs_4_
  32.1 3.3 %collective-permute-start.4 = (bf16[1024,256]{1,0:T(8,128)(2,1)S(1)}, bf16[1024,256]{1,0:T(8,128)(2,1)S(1)}, u32[]{:S(2)}, u32[]{:S(2)}) collective-permute-start(bf16[1024,256]{1,0:T(8,128)(2,1)S(1)} %after.4), channel_id=1, source_target_pairs={{0,24},{2,26},{4,28},{6,30},{8,16},{10,18},{12,20},{14,22},{16,8},... | collective-permute-start | bytes 1572872 | tf_op jit(solution)/shard_map/ppermute | solution.py:271
  35.4 0.0 collective-permute-start.8
  35.4 1.5 %collective-permute-start = (bf16[128,2048]{1,0:T(8,128)(2,1)S(1)}, bf16[128,2048]{1,0:T(8,128)(2,1)S(1)}, u32[]{:S(2)}, u32[]{:S(2)}) collective-permute-start(bf16[128,2048]{1,0:T(8,128)(2,1)S(1)} %copy-done.7), channel_id=1, source_target_pairs={{0,1},{1,0},{2,3},{3,2},{4,5},{5,4},{6,7},{7,6},{8,9},{9,8},{10,11... | collective-permute-start | bytes 1572872 | tf_op jit(solution)/shard_map/ppermute | solution.py:305
  36.9 3.2 %collective-permute-done.1.refs_2_ = bf16[128,2048]{1,0:T(8,128)(2,1)S(1)} collective-permute-done((bf16[128,2048]{1,0:T(8,128)(2,1)S(1)}, bf16[128,2048]{1,0:T(8,128)(2,1)S(1)}, u32[]{:S(2)}, u32[]{:S(2)}) %collective-permute-start.1) | collective-permute-done | bytes 524320 | tf_op jit(solution)/shard_map/ppermute | solution.py:264
  40.1 1.5 %collective-permute-start.2 = (bf16[128,2048]{1,0:T(8,128)(2,1)S(1)}, bf16[128,2048]{1,0:T(8,128)(2,1)S(1)}, u32[]{:S(2)}, u32[]{:S(2)}) collective-permute-start(bf16[128,2048]{1,0:T(8,128)(2,1)S(1)} %collective-permute-done.1.refs_2_), channel_id=1, source_target_pairs={{0,1},{1,0},{2,3},{3,2},{4,5},{5,4},{6,7},{7,6},{8,9},{9,8},{10,11... | collective-permute-start | bytes 1572872 | tf_op jit(solution)/shard_map/ppermute | solution.py:305
  41.6 2.2 %collective-permute-done.7.refs_1_.refs_3_ = bf16[1024,256]{1,0:T(8,128)(2,1)S(1)} collective-permute-done((bf16[1024,256]{1,0:T(8,128)(2,1)S(1)}, bf16[1024,256]{1,0:T(8,128)(2,1)S(1)}, u32[]{:S(2)}, u32[]{:S(2)}) %collective-permute-start.7) | collective-permute-done | bytes 524320 | tf_op jit(solution)/shard_map/ppermute | solution.py:275
  43.8 0.4 collective-permute-start.10
  44.2 10.1 %collective-permute-done.4.refs_0_ = bf16[1024,256]{1,0:T(8,128)(2,1)S(1)} collective-permute-done((bf16[1024,256]{1,0:T(8,128)(2,1)S(1)}, bf16[1024,256]{1,0:T(8,128)(2,1)S(1)}, u32[]{:S(2)}, u32[]{:S(2)}) %collective-permute-start.4) | collective-permute-done | bytes 524320 | tf_op jit(solution)/shard_map/ppermute | solution.py:271
  54.3 0.9 copy-done.14
  55.1 1.5 %collective-permute-start.9 = (bf16[1024,256]{1,0:T(8,128)(2,1)S(1)}, bf16[1024,256]{1,0:T(8,128)(2,1)S(1)}, u32[]{:S(2)}, u32[]{:S(2)}) collective-permute-start(bf16[1024,256]{1,0:T(8,128)(2,1)S(1)} %after.6.refs_6_), channel_id=1, source_target_pairs={{0,4},{2,6},{4,0},{6,2},{8,12},{10,14},{12,8},{14,10},{16,20},{18,... | collective-permute-start | bytes 1572872 | tf_op jit(solution)/shard_map/ppermute | solution.py:275
  56.7 0.0 collective-permute-done.refs_1_
  56.7 0.7 collective-permute-done.2.refs_3_
  57.4 1.2 pick_features.1
  58.6 0.2 code_input.1.refs_3_
  58.8 0.7 copy-done.16
  59.6 4.6 %collective-permute-done.10.refs_2_.far_gate_ref = f32[128,1024]{1,0:T(8,128)S(1)} collective-permute-done((f32[128,1024]{1,0:T(8,128)S(1)}, f32[128,1024]{1,0:T(8,128)S(1)}, u32[]{:S(2)}, u32[]{:S(2)}) %collective-permute-start.10) | collective-permute-done | bytes 524320 | tf_op jit(solution)/shard_map/ppermute | solution.py:264
  64.2 2.6 %collective-permute-done.9.refs_1_.refs_7_ = bf16[1024,256]{1,0:T(8,128)(2,1)S(1)} collective-permute-done((bf16[1024,256]{1,0:T(8,128)(2,1)S(1)}, bf16[1024,256]{1,0:T(8,128)(2,1)S(1)}, u32[]{:S(2)}, u32[]{:S(2)}) %collective-permute-start.9) | collective-permute-done | bytes 524320 | tf_op jit(solution)/shard_map/ppermute | solution.py:275
  66.8 0.8 copy-done.12
  67.6 0.0 collective-permute-start.11
  67.6 0.9 convert_element_type.34
  68.5 4.3 %all-to-all-start.1 = ((f16[16,144,128]{2,1,0:T(8,128)(2,1)}), f16[16,144,128]{2,1,0:T(8,128)(2,1)}, u32[]{:S(2)}, u32[]{:S(2)}) async-start(f16[16,144,128]{2,1,0:T(8,128)(2,1)} %convert_element_type.34), calls=%async_computation.1 | async-start | bytes 1179648 | tf_op jit(solution)/shard_map/all_to_all | solution.py:513
  72.8 6.7 %add_shares.1 = (f32[256,1024]{1,0:T(8,128)}, f32[256,1024]{1,0:T(8,128)}) custom-call(s32[1]{0:T(128)} %bitcast.1.ctx_ref, s32[1]{0:T(128)} %bitcast.2.ch_ref, bf16[256,2048]{1,0:T(8,128)(2,1)} %copy-done.16, bf16[256,2048]{1,0:T(8,128)(2,1)} %collective-permute-done.11.theirs_ref, bf16[1024,256]{1,0:T(8,128)(2,1)} %copy-done.20, ...), custom_call_target="tpu_custom_call" | custom-call | flops 2147483648 | bytes 10485760 | tf_op jit(solution)/shard_map/add_shares/pallas_call | solution.py:427
  79.5 0.5 collective-permute-start.12
  79.9 2.5 %collective-permute-done.12.arrived_ref = f32[256,1024]{1,0:T(8,128)S(1)} collective-permute-done((f32[256,1024]{1,0:T(8,128)}, f32[256,1024]{1,0:T(8,128)S(1)}, u32[]{:S(2)}, u32[]{:S(2)}) %collective-permute-start.12) | collective-permute-done | bytes 1048608 | tf_op jit(solution)/shard_map/ppermute | solution.py:261
  82.4 1.2 copy-done.6
  83.7 0.8 seq_grad.1
  84.5 0.8 copy-done.8
  85.3 0.8 copy-done.17
  86.1 0.9 convert_element_type.32
  87.0 1.3 all-to-all-done.1
  88.3 3.8 %all-to-all-start = ((f16[8,272,128]{2,1,0:T(8,128)(2,1)}), f16[8,272,128]{2,1,0:T(8,128)(2,1)S(1)}, u32[]{:S(2)}, u32[]{:S(2)}) async-start(f16[8,272,128]{2,1,0:T(8,128)(2,1)} %convert_element_type.32), calls=%async_computation | async-start | bytes 1114112 | tf_op jit(solution)/shard_map/all_to_all | solution.py:513
  92.2 0.7 broadcast_in_dim.3.filter_ref
  92.8 7.0 %toeplitz.1.t_ref = bf16[8,256,2176]{2,1,0:T(8,128)(2,1)} custom-call(f32[8,1,2176]{2,1,0:T(1,128)} %broadcast_in_dim.3.filter_ref), custom_call_target="tpu_custom_call" | custom-call | flops 8912896 | bytes 8982528 | tf_op jit(solution)/shard_map/toeplitz/pallas_call | solution.py:38
  99.8 0.8 fusion.14
  100.6 1.5 %negate_select_fusion.1.x_ref = f32[16,128,128]{2,1,0:T(8,128)S(1)} fusion(f16[16,144,128]{2,1,0:T(8,128)(2,1)} %all-to-all-done.1, f32[16,128]{1,0:T(8,128)S(1)} %bitcast.23), kind=kLoop, calls=%fused_computation.1 | loop fusion | flops 1835008 | bytes 1581056 | tf_op jit(solution)/shard_map/jit(_where)/select_n | solution.py:99
  102.1 0.0 copy-start.18
  102.1 3.2 %stack_input.1.left_ref = bf16[8,256,256]{2,1,0:T(8,128)(2,1)S(1)} custom-call(f32[16,128,128]{2,1,0:T(8,128)S(1)} %negate_select_fusion.1.x_ref), custom_call_target="tpu_custom_call" | custom-call | flops 2097152 | bytes 2097152 | tf_op jit(solution)/shard_map/stack_input/pallas_call | solution.py:76
  105.4 1.3 collective-permute-start.13
  106.6 1.5 %all-to-all-done = f16[8,272,128]{2,1,0:T(8,128)(2,1)S(1)} async-done(((f16[8,272,128]{2,1,0:T(8,128)(2,1)}), f16[8,272,128]{2,1,0:T(8,128)(2,1)S(1)}, u32[]{:S(2)}, u32[]{:S(2)}) %all-to-all-start) | async-done | bytes 557088 | tf_op jit(solution)/shard_map/all_to_all | solution.py:513
  108.2 0.1 convert_element_type.33.s_ref
  108.3 11.5 %convolve.1 = f32[16,144,128]{2,1,0:T(8,128)S(1)} custom-call(f32[8,272,128]{2,1,0:T(8,128)S(1)} %convert_element_type.33.s_ref, bf16[8,256,256]{2,1,0:T(8,128)(2,1)S(1)} %stack_input.1.left_ref, bf16[8,256,2176]{2,1,0:T(8,128)(2,1)} %toeplitz.1.t_ref), custom_call_target="tpu_custom_call" | custom-call | flops 7985954816 | bytes 12058624 | tf_op jit(solution)/shard_map/convolve/pallas_call | solution.py:200
  119.8 0.9 convert_element_type.37
  120.7 3.9 %all-to-all-start.2 = ((f16[16,144,128]{2,1,0:T(8,128)(2,1)}), f16[16,144,128]{2,1,0:T(8,128)(2,1)S(1)}, u32[]{:S(2)}, u32[]{:S(2)}) async-start(f16[16,144,128]{2,1,0:T(8,128)(2,1)} %convert_element_type.37), calls=%async_computation.2 | async-start | bytes 1179648 | tf_op jit(solution)/shard_map/all_to_all | solution.py:513
  124.7 0.0 copy-start.19
  124.7 1.2 broadcast_select_fusion.1
  125.9 0.1 copy-done.19
  126.0 1.1 maximum_multiply_fusion
  127.2 13.1 %all-to-all-done.2 = f16[16,144,128]{2,1,0:T(8,128)(2,1)S(1)} async-done(((f16[16,144,128]{2,1,0:T(8,128)(2,1)}), f16[16,144,128]{2,1,0:T(8,128)(2,1)S(1)}, u32[]{:S(2)}, u32[]{:S(2)}) %all-to-all-start.2) | async-done | bytes 589856 | tf_op jit(solution)/shard_map/all_to_all | solution.py:513
  140.3 0.6 copy.18
  140.9 0.5 negate_select_fusion
  141.4 0.1 copy.16
  141.5 0.3 copy.17
  141.8 1.3 copy.19
  (43 shorter events, 0.2 us)
Async XLA Ops:
  0.6 91.5 %copy-start = (f32[128,2048]{1,0:T(8,128)S(1)}, f32[128,2048]{1,0:T(8,128)}, u32[]{:S(2)}) copy-start(f32[128,2048]{1,0:T(8,128)} %param.11) | copy-start | bytes 3145732
  0.6 8.7 %copy-start.7 = (bf16[128,2048]{1,0:T(8,128)(2,1)S(1)}, bf16[128,2048]{1,0:T(8,128)(2,1)}, u32[]{:S(2)}) copy-start(bf16[128,2048]{1,0:T(8,128)(2,1)} %refs_0_.1) | copy-start | bytes 1572868
  2.1 30.0 %copy-start.20 = (bf16[1024,256]{1,0:T(8,128)(2,1)}, bf16[1024,256]{1,0:T(8,128)(2,1)S(1)}, u32[]{:S(2)}) copy-start(bf16[1024,256]{1,0:T(8,128)(2,1)S(1)} %get-tuple-element.22.refs_0_) | copy-start | bytes 1572868
  2.1 25.7 %collective-permute-start.5 = (bf16[1024,256]{1,0:T(8,128)(2,1)S(1)}, bf16[1024,256]{1,0:T(8,128)(2,1)S(1)}, u32[]{:S(2)}, u32[]{:S(2)}) collective-permute-start(bf16[1024,256]{1,0:T(8,128)(2,1)S(1)} %get-tuple-element.23.refs_0_), channel_id=1, source_target_pairs={{0,8},{2,10},{4,12},{6,14},{8,0},{10,2},{12,4},{14,6},{16,24},{18,... | collective-permute-start | bytes 1572872 | tf_op jit(solution)/shard_map/ppermute | solution.py:264
  5.2 22.6 %collective-permute-start.6 = (bf16[1024,256]{1,0:T(8,128)(2,1)S(1)}, bf16[1024,256]{1,0:T(8,128)(2,1)S(1)}, u32[]{:S(2)}, u32[]{:S(2)}) collective-permute-start(bf16[1024,256]{1,0:T(8,128)(2,1)S(1)} %get-tuple-element.22.refs_0_), channel_id=1, source_target_pairs={{0,4},{2,6},{4,0},{6,2},{8,12},{10,14},{12,8},{14,10},{16,20},{18,... | collective-permute-start | bytes 1572872 | tf_op jit(solution)/shard_map/ppermute | solution.py:275
  6.7 25.4 %collective-permute-start.3 = (bf16[1024,256]{1,0:T(8,128)(2,1)S(1)}, bf16[1024,256]{1,0:T(8,128)(2,1)S(1)}, u32[]{:S(2)}, u32[]{:S(2)}) collective-permute-start(bf16[1024,256]{1,0:T(8,128)(2,1)S(1)} %get-tuple-element.22.refs_0_), channel_id=1, source_target_pairs={{0,16},{2,18},{4,20},{6,22},{8,24},{10,26},{12,28},{14,30},{16,0},... | collective-permute-start | bytes 1572872 | tf_op jit(solution)/shard_map/ppermute | solution.py:267
  9.3 30.7 %collective-permute-start.1 = (bf16[128,2048]{1,0:T(8,128)(2,1)S(1)}, bf16[128,2048]{1,0:T(8,128)(2,1)S(1)}, u32[]{:S(2)}, u32[]{:S(2)}) collective-permute-start(bf16[128,2048]{1,0:T(8,128)(2,1)S(1)} %copy-done.7), channel_id=1, source_target_pairs={{0,8},{2,10},{4,12},{6,14},{8,0},{10,2},{12,4},{14,6},{16,24},{18,... | collective-permute-start | bytes 1572872 | tf_op jit(solution)/shard_map/ppermute | solution.py:264
  27.8 4.3 %copy-start.10 = (bf16[1024,256]{1,0:T(8,128)(2,1)}, bf16[1024,256]{1,0:T(8,128)(2,1)S(1)}, u32[]{:S(2)}) copy-start(bf16[1024,256]{1,0:T(8,128)(2,1)S(1)} %collective-permute-done.6.refs_1_) | copy-start | bytes 1572868
  27.9 13.7 %copy-start.13 = (bf16[1024,256]{1,0:T(8,128)(2,1)}, bf16[1024,256]{1,0:T(8,128)(2,1)S(1)}, u32[]{:S(2)}) copy-start(bf16[1024,256]{1,0:T(8,128)(2,1)S(1)} %after.5.refs_2_) | copy-start | bytes 1572868
  27.9 13.7 %copy-start.1 = (f32[128,2048]{1,0:T(8,128)S(1)}, f32[128,2048]{1,0:T(8,128)}, u32[]{:S(2)}) copy-start(f32[128,2048]{1,0:T(8,128)} %gate_ref.1) | copy-start | bytes 3145732
  27.9 15.9 %collective-permute-start.7 = (bf16[1024,256]{1,0:T(8,128)(2,1)S(1)}, bf16[1024,256]{1,0:T(8,128)(2,1)S(1)}, u32[]{:S(2)}, u32[]{:S(2)}) collective-permute-start(bf16[1024,256]{1,0:T(8,128)(2,1)S(1)} %after.5.refs_2_), channel_id=1, source_target_pairs={{0,4},{2,6},{4,0},{6,2},{8,12},{10,14},{12,8},{14,10},{16,20},{18,... | collective-permute-start | bytes 1572872 | tf_op jit(solution)/shard_map/ppermute | solution.py:275
  32.1 9.5 %copy-start.11 = (bf16[1024,256]{1,0:T(8,128)(2,1)}, bf16[1024,256]{1,0:T(8,128)(2,1)S(1)}, u32[]{:S(2)}) copy-start(bf16[1024,256]{1,0:T(8,128)(2,1)S(1)} %collective-permute-done.3.refs_1_.refs_4_) | copy-start | bytes 1572868
  32.1 22.1 %collective-permute-start.4 = (bf16[1024,256]{1,0:T(8,128)(2,1)S(1)}, bf16[1024,256]{1,0:T(8,128)(2,1)S(1)}, u32[]{:S(2)}, u32[]{:S(2)}) collective-permute-start(bf16[1024,256]{1,0:T(8,128)(2,1)S(1)} %after.4), channel_id=1, source_target_pairs={{0,24},{2,26},{4,28},{6,30},{8,16},{10,18},{12,20},{14,22},{16,8},... | collective-permute-start | bytes 1572872 | tf_op jit(solution)/shard_map/ppermute | solution.py:271
  35.4 18.9 %collective-permute-start.8 = (bf16[1024,256]{1,0:T(8,128)(2,1)S(1)}, bf16[1024,256]{1,0:T(8,128)(2,1)S(1)}, u32[]{:S(2)}, u32[]{:S(2)}) collective-permute-start(bf16[1024,256]{1,0:T(8,128)(2,1)S(1)} %collective-permute-done.3.refs_1_.refs_4_), channel_id=1, source_target_pairs={{0,4},{2,6},{4,0},{6,2},{8,12},{10,14},{12,8},{14,10},{16,20},{18,... | collective-permute-start | bytes 1572872 | tf_op jit(solution)/shard_map/ppermute | solution.py:275
  35.4 21.3 %collective-permute-start = (bf16[128,2048]{1,0:T(8,128)(2,1)S(1)}, bf16[128,2048]{1,0:T(8,128)(2,1)S(1)}, u32[]{:S(2)}, u32[]{:S(2)}) collective-permute-start(bf16[128,2048]{1,0:T(8,128)(2,1)S(1)} %copy-done.7), channel_id=1, source_target_pairs={{0,1},{1,0},{2,3},{3,2},{4,5},{5,4},{6,7},{7,6},{8,9},{9,8},{10,11... | collective-permute-start | bytes 1572872 | tf_op jit(solution)/shard_map/ppermute | solution.py:305
  40.1 17.3 %collective-permute-start.2 = (bf16[128,2048]{1,0:T(8,128)(2,1)S(1)}, bf16[128,2048]{1,0:T(8,128)(2,1)S(1)}, u32[]{:S(2)}, u32[]{:S(2)}) collective-permute-start(bf16[128,2048]{1,0:T(8,128)(2,1)S(1)} %collective-permute-done.1.refs_2_), channel_id=1, source_target_pairs={{0,1},{1,0},{2,3},{3,2},{4,5},{5,4},{6,7},{7,6},{8,9},{9,8},{10,11... | collective-permute-start | bytes 1572872 | tf_op jit(solution)/shard_map/ppermute | solution.py:305
  43.8 20.4 %collective-permute-start.10 = (f32[128,1024]{1,0:T(8,128)S(1)}, f32[128,1024]{1,0:T(8,128)S(1)}, u32[]{:S(2)}, u32[]{:S(2)}) collective-permute-start(f32[128,1024]{1,0:T(8,128)S(1)} %constant_dynamic-slice_fusion.1), channel_id=1, source_target_pairs={{0,8},{2,10},{4,12},{6,14},{8,0},{10,2},{12,4},{14,6},{16,24},{18,... | collective-permute-start | bytes 1572872 | tf_op jit(solution)/shard_map/ppermute | solution.py:264
  54.3 4.3 %copy-start.4 = (bf16[1024,256]{1,0:T(8,128)(2,1)}, bf16[1024,256]{1,0:T(8,128)(2,1)S(1)}, u32[]{:S(2)}) copy-start(bf16[1024,256]{1,0:T(8,128)(2,1)S(1)} %collective-permute-done.8.refs_2_.refs_0_.refs_5_) | copy-start | bytes 1572868
  54.3 0.9 copy-start.14
  55.1 3.7 %copy-start.15 = (bf16[1024,256]{1,0:T(8,128)(2,1)}, bf16[1024,256]{1,0:T(8,128)(2,1)S(1)}, u32[]{:S(2)}) copy-start(bf16[1024,256]{1,0:T(8,128)(2,1)S(1)} %after.6.refs_6_) | copy-start | bytes 1572868
  55.1 3.5 %copy-start.5 = (f32[128,2048]{1,0:T(8,128)S(1)}, f32[128,2048]{1,0:T(8,128)}, u32[]{:S(2)}) copy-start(f32[128,2048]{1,0:T(8,128)} %x_ref.1) | copy-start | bytes 3145732
  55.1 11.6 %collective-permute-start.9 = (bf16[1024,256]{1,0:T(8,128)(2,1)S(1)}, bf16[1024,256]{1,0:T(8,128)(2,1)S(1)}, u32[]{:S(2)}, u32[]{:S(2)}) collective-permute-start(bf16[1024,256]{1,0:T(8,128)(2,1)S(1)} %after.6.refs_6_), channel_id=1, source_target_pairs={{0,4},{2,6},{4,0},{6,2},{8,12},{10,14},{12,8},{14,10},{16,20},{18,... | collective-permute-start | bytes 1572872 | tf_op jit(solution)/shard_map/ppermute | solution.py:275
  58.6 1.0 copy-start.16
  64.2 2.6 %copy-start.2 = (f32[128,1024]{1,0:T(8,128)}, f32[128,1024]{1,0:T(8,128)S(1)}, u32[]{:S(2)}) copy-start(f32[128,1024]{1,0:T(8,128)S(1)} %collective-permute-done.10.refs_2_.far_gate_ref) | copy-start | bytes 1572868
  66.8 0.8 copy-start.12
  67.6 5.2 %collective-permute-start.11 = (bf16[256,2048]{1,0:T(8,128)(2,1)}, bf16[256,2048]{1,0:T(8,128)(2,1)}, u32[]{:S(2)}, u32[]{:S(2)}) collective-permute-start(bf16[256,2048]{1,0:T(8,128)(2,1)} %after.7), channel_id=1, source_target_pairs={{0,2},{2,0},{4,6},{6,4},{8,10},{10,8},{12,14},{14,12},{16,18},{18,... | collective-permute-start | bytes 3145736 | tf_op jit(solution)/shard_map/ppermute | solution.py:261
  68.5 19.8 %all-to-all-start.1 = ((f16[16,144,128]{2,1,0:T(8,128)(2,1)}), f16[16,144,128]{2,1,0:T(8,128)(2,1)}, u32[]{:S(2)}, u32[]{:S(2)}) async-start(f16[16,144,128]{2,1,0:T(8,128)(2,1)} %convert_element_type.34), calls=%async_computation.1 | async-start | bytes 1179648 | tf_op jit(solution)/shard_map/all_to_all | solution.py:513
  72.8 9.7 %copy-start.3 = (f32[128,1024]{1,0:T(8,128)S(1)}, f32[128,1024]{1,0:T(8,128)}, u32[]{:S(2)}) copy-start(f32[128,1024]{1,0:T(8,128)} %copy-done.2) | copy-start | bytes 1572868
  79.5 3.0 %collective-permute-start.12 = (f32[256,1024]{1,0:T(8,128)}, f32[256,1024]{1,0:T(8,128)S(1)}, u32[]{:S(2)}, u32[]{:S(2)}) collective-permute-start(f32[256,1024]{1,0:T(8,128)} %get-tuple-element.13), channel_id=1, source_target_pairs={{0,2},{2,0},{4,6},{6,4},{8,10},{10,8},{12,14},{14,12},{16,18},{18,... | collective-permute-start | bytes 3145736 | tf_op jit(solution)/shard_map/ppermute | solution.py:261
  82.4 1.2 copy-start.6
  84.5 0.8 copy-start.8
  85.3 0.8 copy-start.17
  88.3 19.9 %all-to-all-start = ((f16[8,272,128]{2,1,0:T(8,128)(2,1)}), f16[8,272,128]{2,1,0:T(8,128)(2,1)S(1)}, u32[]{:S(2)}, u32[]{:S(2)}) async-start(f16[8,272,128]{2,1,0:T(8,128)(2,1)} %convert_element_type.32), calls=%async_computation | async-start | bytes 1114112 | tf_op jit(solution)/shard_map/all_to_all | solution.py:513
  102.1 3.2 %copy-start.18 = (f32[128,1024]{1,0:T(8,128)S(1)}, f32[128,1024]{1,0:T(8,128)}, u32[]{:S(2)}) copy-start(f32[128,1024]{1,0:T(8,128)} %copy-done.17) | copy-start | bytes 1572868
  105.4 19.3 %collective-permute-start.13 = (f32[128,1024]{1,0:T(8,128)S(1)}, f32[128,1024]{1,0:T(8,128)}, u32[]{:S(2)}, u32[]{:S(2)}) collective-permute-start(f32[128,1024]{1,0:T(8,128)S(1)} %copy-done.18), channel_id=1, source_target_pairs={{0,8},{2,10},{4,12},{6,14},{8,0},{10,2},{12,4},{14,6},{16,24},{18,... | collective-permute-start | bytes 1572872 | tf_op jit(solution)/shard_map/ppermute | solution.py:264
  119.8 4.9 %copy-start.9 = (f32[128,1024]{1,0:T(8,128)S(1)}, f32[128,1024]{1,0:T(8,128)}, u32[]{:S(2)}) copy-start(f32[128,1024]{1,0:T(8,128)} %copy-done.8) | copy-start | bytes 1572868
  120.7 19.5 %all-to-all-start.2 = ((f16[16,144,128]{2,1,0:T(8,128)(2,1)}), f16[16,144,128]{2,1,0:T(8,128)(2,1)S(1)}, u32[]{:S(2)}, u32[]{:S(2)}) async-start(f16[16,144,128]{2,1,0:T(8,128)(2,1)} %convert_element_type.37), calls=%async_computation.2 | async-start | bytes 1179648 | tf_op jit(solution)/shard_map/all_to_all | solution.py:513
  124.7 1.4 copy-start.19

commit v7 on v6

--- a/solution.py
+++ b/solution.py
@@ -41,6 +41,7 @@
         in_specs=[pl.BlockSpec((1, 1, width), lambda g: (g, 0, 0))],
         out_specs=pl.BlockSpec((1, 2 * tok, width), lambda g: (g, 0, 0)),
         out_shape=jax.ShapeDtypeStruct((groups, 2 * tok, width), jnp.bfloat16),
+        compiler_params=pltpu.CompilerParams(vmem_limit_bytes=8 * 1024 * 1024),
         cost_estimate=pl.CostEstimate(
             flops=groups * tok * width * 4, bytes_accessed=groups * width * (4 + 4 * tok), transcendentals=0
         ),
@@ -79,7 +80,7 @@
         out_specs=VMEM,
         out_shape=jax.ShapeDtypeStruct((groups, 2 * tok, rows), jnp.bfloat16),
         scratch_shapes=[pltpu.VMEM((groups, rows, tok), jnp.bfloat16)] * 2,
-        compiler_params=pltpu.CompilerParams(vmem_limit_bytes=32 * 1024 * 1024),
+        compiler_params=pltpu.CompilerParams(vmem_limit_bytes=12 * 1024 * 1024),
         cost_estimate=pl.CostEstimate(
             flops=blocks * tok * lanes * 8, bytes_accessed=blocks * tok * lanes * 8, transcendentals=0
         ),
@@ -362,8 +363,8 @@
         ),
         out_shape=[
             jax.ShapeDtypeStruct((blocks, 2 * tok + ROW_TILE, own), jnp.float32),
-            jax.ShapeDtypeStruct((tok, half), jnp.float32),
-            jax.ShapeDtypeStruct((tok, half), jnp.float32),
+            pltpu.HBM((tok, half), jnp.float32),
+            pltpu.HBM((tok, half), jnp.float32),
         ],
         compiler_params=pltpu.CompilerParams(vmem_limit_bytes=12 * 1024 * 1024),
         cost_estimate=pl.CostEstimate(
@@ -421,7 +422,7 @@
             ]
             sums = [a + b for a, b in zip(sums, terms)] if sums else terms
         return sums
-    tile = min(256, half)
+    tile = min(512, half)
     whole = jax.ShapeDtypeStruct((rows, half), jnp.float32)
     tiles = pl.BlockSpec((rows, tile), lambda n: (0, n))
     return pl.pallas_call(
@@ -459,8 +460,8 @@
     held.append(along_y(after(paired, *held[0][1:])))
     held.append(along_y(far))
     held.append(along_y(after(far_paired, *held[1][1:], *held[2][1:])))
-    made = between(held[2][-1])
-    mine, theirs = gather_cotangent(cotangent, features, place, [*held[3][1:], waited, made])
+    made, sign = between(held[2][-1])
+    mine, theirs = gather_cotangent(cotangent, features, place, [*held[3][1:], waited, sign])
     shares = [
         ((other // 2, other % 2, shift), held[other][shift]) for other in range(4) for shift in range(place.ys)
     ]
@@ -516,10 +517,13 @@
         return blocks.reshape((2, 2, devices // 4) + blocks.shape[1:]).swapaxes(0, 1).reshape(blocks.shape)
 
     far_gate = place.swap_pair(lax.dynamic_slice_in_dim(gate_value, (1 - place.p) * half, half, 1))
-    total, arrived, code = project(
-        cotangent, out_weight, place, far_gate, lambda earlier: code_blocks(conv_input, devices, earlier)
-    )
-    code = exchange(code.astype(jnp.float16))
+
+    def code_input(earlier):
+        code = lax.optimization_barrier(code_blocks(conv_input, devices, earlier).astype(jnp.float16))
+        return code, code[0, :8].astype(jnp.float32)
+
+    total, arrived, code = project(cotangent, out_weight, place, far_gate, code_input)
+    code = exchange(code)
     input_blocks = decoded(code[:, :tok], code[:, tok : tok + 1])
     first_group = (place.p * half + place.block * own) // per_group
     moved = toeplitz(lax.dynamic_slice_in_dim(filters, first_group, groups, 0), tok)

time: 144 us -> 141 us (0.979)
  Pallas kernels: 30.6 us -> 28.1 us
    all_to_all x3, waiting for transfers between devices: 16 us -> 20.3 us  [exchange(): lax.all_to_all(blocks, 'ctx', 0, 0, tiled=True, axis_index_groups=groups)]
    pallas_call x1, Pallas kernels: 6.97 us -> 2.96 us  [toeplitz(): pl.pallas_call(toeplitz_kernel, grid=(groups,), in_specs=[pl.BlockSpec((1...]
    ppermute x4, waiting for transfers between devices: 25.8 us -> 24 us  [swap_pair(): lax.ppermute(v, 'ctx', [(self.index(h, p, y, c), self.index(h, 1 - p, y,...]
    unnamed x43 -> x33, local copies, waits for them, and re-layouts: 6.74 us -> 7.94 us
  transfers between devices with their start and end apart: 17 -> 17, of which waited for: 12 -> 12; matrix products, arithmetic and copies ran while one was open for 6% -> 5% of each run, Pallas kernels for 21% -> 20%
where the time goes in v7:
time: 141 us
  waiting for transfers between devices  62.5 us (44%)
  starting transfers between devices  31.9 us (23%)
  Pallas kernels  28.1 us (20%)
  local copies, waits for them, and re-layouts  10.4 us (7%)
  other arithmetic  6.8 us (5%)
    ppermute x4, waiting for transfers between devices, swap_pair(): lax.ppermute(v, 'ctx', [(self.index(h, p, y, c), self.index(h, 1 - p, y,...  24 us
    all_to_all x3, waiting for transfers between devices, exchange(): lax.all_to_all(blocks, 'ctx', 0, 0, tiled=True, axis_index_groups=groups)  20.3 us
    pallas_call x1, Pallas kernels, convolve(): pl.pallas_call(functools.partial(conv_kernel, scale, lag_own), grid=(grou...  11.6 us
    all_to_all x3, starting transfers between devices, exchange(): lax.all_to_all(blocks, 'ctx', 0, 0, tiled=True, axis_index_groups=groups)  11.2 us
    ppermute x1, waiting for transfers between devices, swap_half_and_pair(): return lax.ppermute(v, 'ctx', pairs)  10.1 us
    unnamed x33, local copies, waits for them, and re-layouts  7.94 us
    ppermute x4, starting transfers between devices, along_y(): lax.ppermute(v, 'ctx', [(self.index(h, p, y, c), self.index(h, p, (y + sh...  6.18 us
    pallas_call x1, Pallas kernels, add_shares(): pl.pallas_call(functools.partial(share_kernel, where, place.ys, parts), g...  5.99 us
  transfers between devices with their start and end apart: 17, of which 12 were waited for; matrix products, arithmetic and copies ran while one was open for 5% of the time, Pallas kernels for 20%

profile of v7, /device:TPU:0, one launch (start us, length us, event | category | flops | bytes accessed | tf_op | source)
XLA Modules:
  0.0 140.7 jit_solution(4216888308749624464)
XLA Ops:
  0.6 0.0 copy-start
  0.7 1.3 constant_dynamic-slice_fusion.2
  2.1 3.1 %collective-permute-start.5 = (bf16[1024,256]{1,0:T(8,128)(2,1)S(1)}, bf16[1024,256]{1,0:T(8,128)(2,1)S(1)}, u32[]{:S(2)}, u32[]{:S(2)}) collective-permute-start(bf16[1024,256]{1,0:T(8,128)(2,1)S(1)} %get-tuple-element.23.refs_0_), channel_id=1, source_target_pairs={{0,8},{2,10},{4,12},{6,14},{8,0},{10,2},{12,4},{14,6},{16,24},{18,... | collective-permute-start | bytes 1572872 | tf_op jit(solution)/shard_map/ppermute | solution.py:265
  5.2 1.5 %collective-permute-start.6 = (bf16[1024,256]{1,0:T(8,128)(2,1)S(1)}, bf16[1024,256]{1,0:T(8,128)(2,1)S(1)}, u32[]{:S(2)}, u32[]{:S(2)}) collective-permute-start(bf16[1024,256]{1,0:T(8,128)(2,1)S(1)} %get-tuple-element.22.refs_0_), channel_id=1, source_target_pairs={{0,4},{2,6},{4,0},{6,2},{8,12},{10,14},{12,8},{14,10},{16,20},{18,... | collective-permute-start | bytes 1572872 | tf_op jit(solution)/shard_map/ppermute | solution.py:276
  6.7 2.6 %collective-permute-start.3 = (bf16[1024,256]{1,0:T(8,128)(2,1)S(1)}, bf16[1024,256]{1,0:T(8,128)(2,1)S(1)}, u32[]{:S(2)}, u32[]{:S(2)}) collective-permute-start(bf16[1024,256]{1,0:T(8,128)(2,1)S(1)} %get-tuple-element.22.refs_0_), channel_id=1, source_target_pairs={{0,16},{2,18},{4,20},{6,22},{8,24},{10,26},{12,28},{14,30},{16,0},... | collective-permute-start | bytes 1572872 | tf_op jit(solution)/shard_map/ppermute | solution.py:268
  9.3 0.4 collective-permute-start.1
  9.7 18.1 %collective-permute-done.5.refs_0_ = bf16[1024,256]{1,0:T(8,128)(2,1)S(1)} collective-permute-done((bf16[1024,256]{1,0:T(8,128)(2,1)S(1)}, bf16[1024,256]{1,0:T(8,128)(2,1)S(1)}, u32[]{:S(2)}, u32[]{:S(2)}) %collective-permute-start.5) | collective-permute-done | bytes 524320 | tf_op jit(solution)/shard_map/ppermute | solution.py:265
  27.8 0.0 collective-permute-done.6.refs_1_
  27.8 0.0 copy-start.2
  27.8 3.1 %collective-permute-start.7 = (bf16[1024,256]{1,0:T(8,128)(2,1)S(1)}, bf16[1024,256]{1,0:T(8,128)(2,1)S(1)}, u32[]{:S(2)}, u32[]{:S(2)}) collective-permute-start(bf16[1024,256]{1,0:T(8,128)(2,1)S(1)} %after.5.refs_2_), channel_id=1, source_target_pairs={{0,4},{2,6},{4,0},{6,2},{8,12},{10,14},{12,8},{14,10},{16,20},{18,... | collective-permute-start | bytes 1572872 | tf_op jit(solution)/shard_map/ppermute | solution.py:276
  30.9 1.2 collective-permute-done.3.refs_1_.refs_4_
  32.1 3.3 %collective-permute-start.4 = (bf16[1024,256]{1,0:T(8,128)(2,1)S(1)}, bf16[1024,256]{1,0:T(8,128)(2,1)S(1)}, u32[]{:S(2)}, u32[]{:S(2)}) collective-permute-start(bf16[1024,256]{1,0:T(8,128)(2,1)S(1)} %after.4), channel_id=1, source_target_pairs={{0,24},{2,26},{4,28},{6,30},{8,16},{10,18},{12,20},{14,22},{16,8},... | collective-permute-start | bytes 1572872 | tf_op jit(solution)/shard_map/ppermute | solution.py:272
  35.3 0.0 collective-permute-start.8
  35.3 1.5 %collective-permute-start = (bf16[128,2048]{1,0:T(8,128)(2,1)}, bf16[128,2048]{1,0:T(8,128)(2,1)S(1)}, u32[]{:S(2)}, u32[]{:S(2)}) collective-permute-start(bf16[128,2048]{1,0:T(8,128)(2,1)} %refs_0_.1), channel_id=1, source_target_pairs={{0,1},{1,0},{2,3},{3,2},{4,5},{5,4},{6,7},{7,6},{8,9},{9,8},{10,11... | collective-permute-start | bytes 1572872 | tf_op jit(solution)/shard_map/ppermute | solution.py:306
  36.8 3.3 %collective-permute-done.1.refs_2_ = bf16[128,2048]{1,0:T(8,128)(2,1)S(1)} collective-permute-done((bf16[128,2048]{1,0:T(8,128)(2,1)}, bf16[128,2048]{1,0:T(8,128)(2,1)S(1)}, u32[]{:S(2)}, u32[]{:S(2)}) %collective-permute-start.1) | collective-permute-done | bytes 524320 | tf_op jit(solution)/shard_map/ppermute | solution.py:265
  40.1 1.5 %collective-permute-start.2 = (bf16[128,2048]{1,0:T(8,128)(2,1)S(1)}, bf16[128,2048]{1,0:T(8,128)(2,1)S(1)}, u32[]{:S(2)}, u32[]{:S(2)}) collective-permute-start(bf16[128,2048]{1,0:T(8,128)(2,1)S(1)} %collective-permute-done.1.refs_2_), channel_id=1, source_target_pairs={{0,1},{1,0},{2,3},{3,2},{4,5},{5,4},{6,7},{7,6},{8,9},{9,8},{10,11... | collective-permute-start | bytes 1572872 | tf_op jit(solution)/shard_map/ppermute | solution.py:306
  41.7 0.0 copy-start.4
  41.7 2.1 %collective-permute-done.7.refs_1_.refs_3_ = bf16[1024,256]{1,0:T(8,128)(2,1)S(1)} collective-permute-done((bf16[1024,256]{1,0:T(8,128)(2,1)S(1)}, bf16[1024,256]{1,0:T(8,128)(2,1)S(1)}, u32[]{:S(2)}, u32[]{:S(2)}) %collective-permute-start.7) | collective-permute-done | bytes 524320 | tf_op jit(solution)/shard_map/ppermute | solution.py:276
  43.7 0.4 collective-permute-start.10
  44.1 10.1 %collective-permute-done.4.refs_0_ = bf16[1024,256]{1,0:T(8,128)(2,1)S(1)} collective-permute-done((bf16[1024,256]{1,0:T(8,128)(2,1)S(1)}, bf16[1024,256]{1,0:T(8,128)(2,1)S(1)}, u32[]{:S(2)}, u32[]{:S(2)}) %collective-permute-start.4) | collective-permute-done | bytes 524320 | tf_op jit(solution)/shard_map/ppermute | solution.py:272
  54.2 0.0 collective-permute-done.8.refs_2_.refs_0_.refs_5_
  54.2 1.6 %collective-permute-start.9 = (bf16[1024,256]{1,0:T(8,128)(2,1)S(1)}, bf16[1024,256]{1,0:T(8,128)(2,1)S(1)}, u32[]{:S(2)}, u32[]{:S(2)}) collective-permute-start(bf16[1024,256]{1,0:T(8,128)(2,1)S(1)} %after.6.refs_6_), channel_id=1, source_target_pairs={{0,4},{2,6},{4,0},{6,2},{8,12},{10,14},{12,8},{14,10},{16,20},{18,... | collective-permute-start | bytes 1572872 | tf_op jit(solution)/shard_map/ppermute | solution.py:276
  55.8 0.2 code_input.1
  56.1 0.9 convert_element_type.37
  57.0 0.0 collective-permute-done.refs_1_
  57.0 0.6 collective-permute-done.2.refs_3_
  57.6 2.3 %pick_features.1 = (bf16[256,2048]{1,0:T(8,128)(2,1)S(1)}, bf16[256,2048]{1,0:T(8,128)(2,1)}) custom-call(s32[1]{0:T(128)} %bitcast.3.core_ref, bf16[128,2048]{1,0:T(8,128)(2,1)} %refs_0_.1, bf16[128,2048]{1,0:T(8,128)(2,1)S(1)} %collective-permute-done.refs_1_, bf16[128,2048]{1,0:T(8,128)(2,1)S(1)} %collective-permute-done.1.refs_2_, ...), custom_call_target="tpu_custom_call" | custom-call | bytes 4194304 | tf_op jit(solution)/shard_map/pick_features/pallas_call | solution.py:309
  59.8 1.0 copy-done.12
  60.8 0.7 fusion.15.refs_3_
  61.5 2.6 %collective-permute-done.10.refs_2_.far_gate_ref = f32[128,1024]{1,0:T(8,128)S(1)} collective-permute-done((f32[128,1024]{1,0:T(8,128)S(1)}, f32[128,1024]{1,0:T(8,128)S(1)}, u32[]{:S(2)}, u32[]{:S(2)}) %collective-permute-start.10) | collective-permute-done | bytes 524320 | tf_op jit(solution)/shard_map/ppermute | solution.py:265
  64.1 1.8 %collective-permute-done.9.refs_1_.refs_7_ = bf16[1024,256]{1,0:T(8,128)(2,1)S(1)} collective-permute-done((bf16[1024,256]{1,0:T(8,128)(2,1)S(1)}, bf16[1024,256]{1,0:T(8,128)(2,1)S(1)}, u32[]{:S(2)}, u32[]{:S(2)}) %collective-permute-start.9) | collective-permute-done | bytes 524320 | tf_op jit(solution)/shard_map/ppermute | solution.py:276
  66.0 0.8 copy-done.10
  66.7 0.0 collective-permute-start.11
  66.7 3.8 %all-to-all-start.1 = ((f16[16,144,128]{2,1,0:T(8,128)(2,1)}), f16[16,144,128]{2,1,0:T(8,128)(2,1)S(1)}, u32[]{:S(2)}, u32[]{:S(2)}) async-start(f16[16,144,128]{2,1,0:T(8,128)(2,1)} %convert_element_type.37), calls=%async_computation.1 | async-start | bytes 1179648 | tf_op jit(solution)/shard_map/all_to_all | solution.py:514
  70.5 0.0 collective-permute-done.11.theirs_ref
  70.5 6.0 %add_shares.1 = (f32[256,1024]{1,0:T(8,128)}, f32[256,1024]{1,0:T(8,128)}) custom-call(s32[1]{0:T(128)} %bitcast.1.ctx_ref, s32[1]{0:T(128)} %bitcast.2.ch_ref, bf16[256,2048]{1,0:T(8,128)(2,1)} %copy-done.12, bf16[256,2048]{1,0:T(8,128)(2,1)} %collective-permute-done.11.theirs_ref, bf16[1024,256]{1,0:T(8,128)(2,1)} %copy-done.15, ...), custom_call_target="tpu_custom_call" | custom-call | flops 2147483648 | bytes 10485760 | tf_op jit(solution)/shard_map/add_shares/pallas_call | solution.py:428
  76.5 0.5 collective-permute-start.12
  77.0 2.5 %collective-permute-done.12.arrived_ref = f32[256,1024]{1,0:T(8,128)S(1)} collective-permute-done((f32[256,1024]{1,0:T(8,128)}, f32[256,1024]{1,0:T(8,128)S(1)}, u32[]{:S(2)}, u32[]{:S(2)}) %collective-permute-start.12) | collective-permute-done | bytes 1048608 | tf_op jit(solution)/shard_map/ppermute | solution.py:262
  79.5 1.2 copy-done.5
  80.7 1.9 %seq_grad.1 = (f32[8,272,128]{2,1,0:T(8,128)S(1)}, f32[128,1024]{1,0:T(8,128)}, f32[128,1024]{1,0:T(8,128)}) custom-call(s32[1]{0:T(128)} %bitcast.p_ref, f32[256,1024]{1,0:T(8,128)S(1)} %copy-done.5, f32[256,1024]{1,0:T(8,128)S(1)} %collective-permute-done.12.arrived_ref, f32[128,2048]{1,0:T(8,128)S(1)} %copy-done.2, ...), custom_call_target="tpu_custom_call" | custom-call | flops 524288 | bytes 6291456 | tf_op jit(solution)/shard_map/seq_grad/pallas_call | solution.py:346
  82.6 0.9 convert_element_type.40
  83.5 2.6 %all-to-all-done.1 = f16[16,144,128]{2,1,0:T(8,128)(2,1)S(1)} async-done(((f16[16,144,128]{2,1,0:T(8,128)(2,1)}), f16[16,144,128]{2,1,0:T(8,128)(2,1)S(1)}, u32[]{:S(2)}, u32[]{:S(2)}) %all-to-all-start.1) | async-done | bytes 589856 | tf_op jit(solution)/shard_map/all_to_all | solution.py:514
  86.1 3.9 %all-to-all-start = ((f16[8,272,128]{2,1,0:T(8,128)(2,1)}), f16[8,272,128]{2,1,0:T(8,128)(2,1)S(1)}, u32[]{:S(2)}, u32[]{:S(2)}) async-start(f16[8,272,128]{2,1,0:T(8,128)(2,1)} %convert_element_type.40), calls=%async_computation | async-start | bytes 1114112 | tf_op jit(solution)/shard_map/all_to_all | solution.py:514
  90.0 3.0 %toeplitz.1.t_ref = bf16[8,256,2176]{2,1,0:T(8,128)(2,1)S(1)} custom-call(f32[8,1,2176]{2,1,0:T(1,128)S(1)} %broadcast_in_dim.3.filter_ref), custom_call_target="tpu_custom_call" | custom-call | flops 8912896 | bytes 8982528 | tf_op jit(solution)/shard_map/toeplitz/pallas_call | solution.py:38
  93.0 3.5 %copy-done.1 = bf16[8,256,2176]{2,1,0:T(8,128)(2,1)} copy-done((bf16[8,256,2176]{2,1,0:T(8,128)(2,1)}, bf16[8,256,2176]{2,1,0:T(8,128)(2,1)S(1)}, u32[]{:S(2)}) %copy-start.1) | copy-done | bytes 8912920
  96.5 0.5 negate_select_fusion.1.x_ref
  97.0 3.2 %stack_input.1.left_ref = bf16[8,256,256]{2,1,0:T(8,128)(2,1)S(1)} custom-call(f32[16,128,128]{2,1,0:T(8,128)S(1)} %negate_select_fusion.1.x_ref), custom_call_target="tpu_custom_call" | custom-call | flops 2097152 | bytes 2097152 | tf_op jit(solution)/shard_map/stack_input/pallas_call | solution.py:77
  100.2 1.2 collective-permute-start.13
  101.4 4.7 %all-to-all-done = f16[8,272,128]{2,1,0:T(8,128)(2,1)S(1)} async-done(((f16[8,272,128]{2,1,0:T(8,128)(2,1)}), f16[8,272,128]{2,1,0:T(8,128)(2,1)S(1)}, u32[]{:S(2)}, u32[]{:S(2)}) %all-to-all-start) | async-done | bytes 557088 | tf_op jit(solution)/shard_map/all_to_all | solution.py:514
  106.1 0.1 convert_element_type.41.s_ref
  106.2 11.6 %convolve.1 = f32[16,144,128]{2,1,0:T(8,128)S(1)} custom-call(f32[8,272,128]{2,1,0:T(8,128)S(1)} %convert_element_type.41.s_ref, bf16[8,256,256]{2,1,0:T(8,128)(2,1)S(1)} %stack_input.1.left_ref, bf16[8,256,2176]{2,1,0:T(8,128)(2,1)} %copy-done.1), custom_call_target="tpu_custom_call" | custom-call | flops 7985954816 | bytes 12058624 | tf_op jit(solution)/shard_map/convolve/pallas_call | solution.py:201
  117.8 0.9 convert_element_type.44
  118.7 3.6 %all-to-all-start.2 = ((f16[16,144,128]{2,1,0:T(8,128)(2,1)}), f16[16,144,128]{2,1,0:T(8,128)(2,1)S(1)}, u32[]{:S(2)}, u32[]{:S(2)}) async-start(f16[16,144,128]{2,1,0:T(8,128)(2,1)} %convert_element_type.44), calls=%async_computation.2 | async-start | bytes 1179648 | tf_op jit(solution)/shard_map/all_to_all | solution.py:514
  122.3 0.0 copy-start.13
  122.3 0.0 collective-permute-done.13
  122.3 1.2 broadcast_select_fusion.1
  123.5 0.1 copy-done.13
  123.6 1.1 maximum_multiply_fusion
  124.8 13.0 %all-to-all-done.2 = f16[16,144,128]{2,1,0:T(8,128)(2,1)S(1)} async-done(((f16[16,144,128]{2,1,0:T(8,128)(2,1)}), f16[16,144,128]{2,1,0:T(8,128)(2,1)S(1)}, u32[]{:S(2)}, u32[]{:S(2)}) %all-to-all-start.2) | async-done | bytes 589856 | tf_op jit(solution)/shard_map/all_to_all | solution.py:514
  137.8 0.6 copy.18
  138.5 0.5 negate_select_fusion
  139.0 0.1 copy.16
  139.0 0.3 copy.17
  139.4 1.3 copy.19
  (34 shorter events, 0.2 us)
Async XLA Ops:
  0.6 89.3 %copy-start = (f32[128,2048]{1,0:T(8,128)S(1)}, f32[128,2048]{1,0:T(8,128)}, u32[]{:S(2)}) copy-start(f32[128,2048]{1,0:T(8,128)} %param.11) | copy-start | bytes 3145732
  2.1 30.0 %copy-start.15 = (bf16[1024,256]{1,0:T(8,128)(2,1)}, bf16[1024,256]{1,0:T(8,128)(2,1)S(1)}, u32[]{:S(2)}) copy-start(bf16[1024,256]{1,0:T(8,128)(2,1)S(1)} %get-tuple-element.22.refs_0_) | copy-start | bytes 1572868
  2.1 25.7 %collective-permute-start.5 = (bf16[1024,256]{1,0:T(8,128)(2,1)S(1)}, bf16[1024,256]{1,0:T(8,128)(2,1)S(1)}, u32[]{:S(2)}, u32[]{:S(2)}) collective-permute-start(bf16[1024,256]{1,0:T(8,128)(2,1)S(1)} %get-tuple-element.23.refs_0_), channel_id=1, source_target_pairs={{0,8},{2,10},{4,12},{6,14},{8,0},{10,2},{12,4},{14,6},{16,24},{18,... | collective-permute-start | bytes 1572872 | tf_op jit(solution)/shard_map/ppermute | solution.py:265
  5.2 22.6 %collective-permute-start.6 = (bf16[1024,256]{1,0:T(8,128)(2,1)S(1)}, bf16[1024,256]{1,0:T(8,128)(2,1)S(1)}, u32[]{:S(2)}, u32[]{:S(2)}) collective-permute-start(bf16[1024,256]{1,0:T(8,128)(2,1)S(1)} %get-tuple-element.22.refs_0_), channel_id=1, source_target_pairs={{0,4},{2,6},{4,0},{6,2},{8,12},{10,14},{12,8},{14,10},{16,20},{18,... | collective-permute-start | bytes 1572872 | tf_op jit(solution)/shard_map/ppermute | solution.py:276
  6.7 25.4 %collective-permute-start.3 = (bf16[1024,256]{1,0:T(8,128)(2,1)S(1)}, bf16[1024,256]{1,0:T(8,128)(2,1)S(1)}, u32[]{:S(2)}, u32[]{:S(2)}) collective-permute-start(bf16[1024,256]{1,0:T(8,128)(2,1)S(1)} %get-tuple-element.22.refs_0_), channel_id=1, source_target_pairs={{0,16},{2,18},{4,20},{6,22},{8,24},{10,26},{12,28},{14,30},{16,0},... | collective-permute-start | bytes 1572872 | tf_op jit(solution)/shard_map/ppermute | solution.py:268
  9.3 30.8 %collective-permute-start.1 = (bf16[128,2048]{1,0:T(8,128)(2,1)}, bf16[128,2048]{1,0:T(8,128)(2,1)S(1)}, u32[]{:S(2)}, u32[]{:S(2)}) collective-permute-start(bf16[128,2048]{1,0:T(8,128)(2,1)} %refs_0_.1), channel_id=1, source_target_pairs={{0,8},{2,10},{4,12},{6,14},{8,0},{10,2},{12,4},{14,6},{16,24},{18,... | collective-permute-start | bytes 1572872 | tf_op jit(solution)/shard_map/ppermute | solution.py:265
  27.8 4.3 %copy-start.6 = (bf16[1024,256]{1,0:T(8,128)(2,1)}, bf16[1024,256]{1,0:T(8,128)(2,1)S(1)}, u32[]{:S(2)}) copy-start(bf16[1024,256]{1,0:T(8,128)(2,1)S(1)} %collective-permute-done.6.refs_1_) | copy-start | bytes 1572868
  27.8 13.9 %copy-start.8 = (bf16[1024,256]{1,0:T(8,128)(2,1)}, bf16[1024,256]{1,0:T(8,128)(2,1)S(1)}, u32[]{:S(2)}) copy-start(bf16[1024,256]{1,0:T(8,128)(2,1)S(1)} %after.5.refs_2_) | copy-start | bytes 1572868
  27.8 13.8 %copy-start.2 = (f32[128,2048]{1,0:T(8,128)S(1)}, f32[128,2048]{1,0:T(8,128)}, u32[]{:S(2)}) copy-start(f32[128,2048]{1,0:T(8,128)} %gate_ref.1) | copy-start | bytes 3145732
  27.8 15.9 %collective-permute-start.7 = (bf16[1024,256]{1,0:T(8,128)(2,1)S(1)}, bf16[1024,256]{1,0:T(8,128)(2,1)S(1)}, u32[]{:S(2)}, u32[]{:S(2)}) collective-permute-start(bf16[1024,256]{1,0:T(8,128)(2,1)S(1)} %after.5.refs_2_), channel_id=1, source_target_pairs={{0,4},{2,6},{4,0},{6,2},{8,12},{10,14},{12,8},{14,10},{16,20},{18,... | collective-permute-start | bytes 1572872 | tf_op jit(solution)/shard_map/ppermute | solution.py:276
  32.1 9.6 %copy-start.7 = (bf16[1024,256]{1,0:T(8,128)(2,1)}, bf16[1024,256]{1,0:T(8,128)(2,1)S(1)}, u32[]{:S(2)}) copy-start(bf16[1024,256]{1,0:T(8,128)(2,1)S(1)} %collective-permute-done.3.refs_1_.refs_4_) | copy-start | bytes 1572868
  32.1 22.1 %collective-permute-start.4 = (bf16[1024,256]{1,0:T(8,128)(2,1)S(1)}, bf16[1024,256]{1,0:T(8,128)(2,1)S(1)}, u32[]{:S(2)}, u32[]{:S(2)}) collective-permute-start(bf16[1024,256]{1,0:T(8,128)(2,1)S(1)} %after.4), channel_id=1, source_target_pairs={{0,24},{2,26},{4,28},{6,30},{8,16},{10,18},{12,20},{14,22},{16,8},... | collective-permute-start | bytes 1572872 | tf_op jit(solution)/shard_map/ppermute | solution.py:272
  35.3 18.9 %collective-permute-start.8 = (bf16[1024,256]{1,0:T(8,128)(2,1)S(1)}, bf16[1024,256]{1,0:T(8,128)(2,1)S(1)}, u32[]{:S(2)}, u32[]{:S(2)}) collective-permute-start(bf16[1024,256]{1,0:T(8,128)(2,1)S(1)} %collective-permute-done.3.refs_1_.refs_4_), channel_id=1, source_target_pairs={{0,4},{2,6},{4,0},{6,2},{8,12},{10,14},{12,8},{14,10},{16,20},{18,... | collective-permute-start | bytes 1572872 | tf_op jit(solution)/shard_map/ppermute | solution.py:276
  35.3 21.6 %collective-permute-start = (bf16[128,2048]{1,0:T(8,128)(2,1)}, bf16[128,2048]{1,0:T(8,128)(2,1)S(1)}, u32[]{:S(2)}, u32[]{:S(2)}) collective-permute-start(bf16[128,2048]{1,0:T(8,128)(2,1)} %refs_0_.1), channel_id=1, source_target_pairs={{0,1},{1,0},{2,3},{3,2},{4,5},{5,4},{6,7},{7,6},{8,9},{9,8},{10,11... | collective-permute-start | bytes 1572872 | tf_op jit(solution)/shard_map/ppermute | solution.py:306
  40.1 17.5 %collective-permute-start.2 = (bf16[128,2048]{1,0:T(8,128)(2,1)S(1)}, bf16[128,2048]{1,0:T(8,128)(2,1)S(1)}, u32[]{:S(2)}, u32[]{:S(2)}) collective-permute-start(bf16[128,2048]{1,0:T(8,128)(2,1)S(1)} %collective-permute-done.1.refs_2_), channel_id=1, source_target_pairs={{0,1},{1,0},{2,3},{3,2},{4,5},{5,4},{6,7},{7,6},{8,9},{9,8},{10,11... | collective-permute-start | bytes 1572872 | tf_op jit(solution)/shard_map/ppermute | solution.py:306
  41.7 14.2 %copy-start.4 = (f32[128,2048]{1,0:T(8,128)S(1)}, f32[128,2048]{1,0:T(8,128)}, u32[]{:S(2)}) copy-start(f32[128,2048]{1,0:T(8,128)} %x_ref.1) | copy-start | bytes 3145732
  43.7 10.5 %copy-start.9 = (bf16[1024,256]{1,0:T(8,128)(2,1)}, bf16[1024,256]{1,0:T(8,128)(2,1)S(1)}, u32[]{:S(2)}) copy-start(bf16[1024,256]{1,0:T(8,128)(2,1)S(1)} %collective-permute-done.7.refs_1_.refs_3_) | copy-start | bytes 1572868
  43.7 20.4 %collective-permute-start.10 = (f32[128,1024]{1,0:T(8,128)S(1)}, f32[128,1024]{1,0:T(8,128)S(1)}, u32[]{:S(2)}, u32[]{:S(2)}) collective-permute-start(f32[128,1024]{1,0:T(8,128)S(1)} %constant_dynamic-slice_fusion.1), channel_id=1, source_target_pairs={{0,8},{2,10},{4,12},{6,14},{8,0},{10,2},{12,4},{14,6},{16,24},{18,... | collective-permute-start | bytes 1572872 | tf_op jit(solution)/shard_map/ppermute | solution.py:265
  54.2 1.8 %copy-start.3 = (bf16[1024,256]{1,0:T(8,128)(2,1)}, bf16[1024,256]{1,0:T(8,128)(2,1)S(1)}, u32[]{:S(2)}) copy-start(bf16[1024,256]{1,0:T(8,128)(2,1)S(1)} %collective-permute-done.8.refs_2_.refs_0_.refs_5_) | copy-start | bytes 1572868
  54.2 1.8 %copy-start.11 = (bf16[1024,256]{1,0:T(8,128)(2,1)}, bf16[1024,256]{1,0:T(8,128)(2,1)S(1)}, u32[]{:S(2)}) copy-start(bf16[1024,256]{1,0:T(8,128)(2,1)S(1)} %after.6.refs_6_) | copy-start | bytes 1572868
  54.2 11.7 %collective-permute-start.9 = (bf16[1024,256]{1,0:T(8,128)(2,1)S(1)}, bf16[1024,256]{1,0:T(8,128)(2,1)S(1)}, u32[]{:S(2)}, u32[]{:S(2)}) collective-permute-start(bf16[1024,256]{1,0:T(8,128)(2,1)S(1)} %after.6.refs_6_), channel_id=1, source_target_pairs={{0,4},{2,6},{4,0},{6,2},{8,12},{10,14},{12,8},{14,10},{16,20},{18,... | collective-permute-start | bytes 1572872 | tf_op jit(solution)/shard_map/ppermute | solution.py:276
  59.8 1.0 copy-start.12
  65.9 0.8 copy-start.10
  66.7 3.8 %collective-permute-start.11 = (bf16[256,2048]{1,0:T(8,128)(2,1)}, bf16[256,2048]{1,0:T(8,128)(2,1)}, u32[]{:S(2)}, u32[]{:S(2)}) collective-permute-start(bf16[256,2048]{1,0:T(8,128)(2,1)} %after.7), channel_id=1, source_target_pairs={{0,2},{2,0},{4,6},{6,4},{8,10},{10,8},{12,14},{14,12},{16,18},{18,... | collective-permute-start | bytes 3145736 | tf_op jit(solution)/shard_map/ppermute | solution.py:262
  66.7 19.4 %all-to-all-start.1 = ((f16[16,144,128]{2,1,0:T(8,128)(2,1)}), f16[16,144,128]{2,1,0:T(8,128)(2,1)S(1)}, u32[]{:S(2)}, u32[]{:S(2)}) async-start(f16[16,144,128]{2,1,0:T(8,128)(2,1)} %convert_element_type.37), calls=%async_computation.1 | async-start | bytes 1179648 | tf_op jit(solution)/shard_map/all_to_all | solution.py:514
  76.5 3.0 %collective-permute-start.12 = (f32[256,1024]{1,0:T(8,128)}, f32[256,1024]{1,0:T(8,128)S(1)}, u32[]{:S(2)}, u32[]{:S(2)}) collective-permute-start(f32[256,1024]{1,0:T(8,128)} %get-tuple-element.13), channel_id=1, source_target_pairs={{0,2},{2,0},{4,6},{6,4},{8,10},{10,8},{12,14},{14,12},{16,18},{18,... | collective-permute-start | bytes 3145736 | tf_op jit(solution)/shard_map/ppermute | solution.py:262
  79.5 1.2 copy-start.5
  86.1 20.0 %all-to-all-start = ((f16[8,272,128]{2,1,0:T(8,128)(2,1)}), f16[8,272,128]{2,1,0:T(8,128)(2,1)S(1)}, u32[]{:S(2)}, u32[]{:S(2)}) async-start(f16[8,272,128]{2,1,0:T(8,128)(2,1)} %convert_element_type.40), calls=%async_computation | async-start | bytes 1114112 | tf_op jit(solution)/shard_map/all_to_all | solution.py:514
  93.0 3.5 %copy-start.1 = (bf16[8,256,2176]{2,1,0:T(8,128)(2,1)}, bf16[8,256,2176]{2,1,0:T(8,128)(2,1)S(1)}, u32[]{:S(2)}) copy-start(bf16[8,256,2176]{2,1,0:T(8,128)(2,1)S(1)} %toeplitz.1.t_ref) | copy-start | bytes 26738692
  100.2 22.0 %collective-permute-start.13 = (f32[128,1024]{1,0:T(8,128)}, f32[128,1024]{1,0:T(8,128)}, u32[]{:S(2)}, u32[]{:S(2)}) collective-permute-start(f32[128,1024]{1,0:T(8,128)} %get-tuple-element.16), channel_id=1, source_target_pairs={{0,8},{2,10},{4,12},{6,14},{8,0},{10,2},{12,4},{14,6},{16,24},{18,... | collective-permute-start | bytes 1572872 | tf_op jit(solution)/shard_map/ppermute | solution.py:265
  117.8 4.5 %copy-start.14 = (f32[128,1024]{1,0:T(8,128)S(1)}, f32[128,1024]{1,0:T(8,128)}, u32[]{:S(2)}) copy-start(f32[128,1024]{1,0:T(8,128)} %get-tuple-element.15) | copy-start | bytes 1572868
  118.7 19.1 %all-to-all-start.2 = ((f16[16,144,128]{2,1,0:T(8,128)(2,1)}), f16[16,144,128]{2,1,0:T(8,128)(2,1)S(1)}, u32[]{:S(2)}, u32[]{:S(2)}) async-start(f16[16,144,128]{2,1,0:T(8,128)(2,1)} %convert_element_type.44), calls=%async_computation.2 | async-start | bytes 1179648 | tf_op jit(solution)/shard_map/all_to_all | solution.py:514
  122.3 1.4 copy-start.13

commit v8 on v7

--- a/solution.py
+++ b/solution.py
@@ -96,8 +96,8 @@
 
 def decoded(code, exponent):
     code = code.astype(jnp.float32)
-    value = jnp.sqrt(jnp.abs(code) * (1.0 / CODE_UNIT)) * jnp.exp2(exponent.astype(jnp.float32))
-    return jnp.where(code < 0, -value, value)
+    scale = jnp.exp2(exponent.astype(jnp.float32)) * (CODE_UNIT**-0.5)
+    return code * lax.rsqrt(jnp.maximum(jnp.abs(code), SMALLEST)) * scale
 
 
 def largest(value):

time: 141 us -> 141 us (level)
  transfers between devices with their start and end apart: 17 -> 17, of which waited for: 12 -> 12; matrix products, arithmetic and copies ran while one was open for 5% -> 4% of each run, Pallas kernels for 20% -> 20%
where the time goes in v8:
time: 141 us; the launch traced here: 140 us
  waiting for transfers between devices  62.7 us (44%)
  starting transfers between devices  31.9 us (23%)
  Pallas kernels  27.9 us (20%)
  local copies, waits for them, and re-layouts  10.4 us (7%)
  other arithmetic  6.27 us (4%)
    ppermute x4, waiting for transfers between devices, swap_pair(): lax.ppermute(v, 'ctx', [(self.index(h, p, y, c), self.index(h, 1 - p, y,...  24 us
    all_to_all x3, waiting for transfers between devices, exchange(): lax.all_to_all(blocks, 'ctx', 0, 0, tiled=True, axis_index_groups=groups)  20.5 us
    pallas_call x1, Pallas kernels, convolve(): pl.pallas_call(functools.partial(conv_kernel, scale, lag_own), grid=(grou...  11.3 us
    all_to_all x3, starting transfers between devices, exchange(): lax.all_to_all(blocks, 'ctx', 0, 0, tiled=True, axis_index_groups=groups)  11.2 us
    ppermute x1, waiting for transfers between devices, swap_half_and_pair(): return lax.ppermute(v, 'ctx', pairs)  10.1 us
    unnamed x33, local copies, waits for them, and re-layouts  7.94 us
    ppermute x4, starting transfers between devices, along_y(): lax.ppermute(v, 'ctx', [(self.index(h, p, y, c), self.index(h, p, (y + sh...  6.18 us
    pallas_call x1, Pallas kernels, add_shares(): pl.pallas_call(functools.partial(share_kernel, where, place.ys, parts), g...  5.99 us
  transfers between devices with their start and end apart: 17, of which 12 were waited for; matrix products, arithmetic and copies ran while one was open for 4% of the time, Pallas kernels for 20%

profile of v8, /device:TPU:0, one launch (start us, length us, event | category | flops | bytes accessed | tf_op | source)
XLA Modules:
  0.0 140.2 jit_solution(1096739611209100983)
XLA Ops:
  0.6 0.0 copy-start
  0.7 1.3 constant_dynamic-slice_fusion.2
  2.1 3.1 %collective-permute-start.5 = (bf16[1024,256]{1,0:T(8,128)(2,1)S(1)}, bf16[1024,256]{1,0:T(8,128)(2,1)S(1)}, u32[]{:S(2)}, u32[]{:S(2)}) collective-permute-start(bf16[1024,256]{1,0:T(8,128)(2,1)S(1)} %get-tuple-element.26.refs_0_), channel_id=1, source_target_pairs={{0,8},{2,10},{4,12},{6,14},{8,0},{10,2},{12,4},{14,6},{16,24},{18,... | collective-permute-start | bytes 1572872 | tf_op jit(solution)/shard_map/ppermute | solution.py:265
  5.2 1.5 %collective-permute-start.6 = (bf16[1024,256]{1,0:T(8,128)(2,1)S(1)}, bf16[1024,256]{1,0:T(8,128)(2,1)S(1)}, u32[]{:S(2)}, u32[]{:S(2)}) collective-permute-start(bf16[1024,256]{1,0:T(8,128)(2,1)S(1)} %get-tuple-element.25.refs_0_), channel_id=1, source_target_pairs={{0,4},{2,6},{4,0},{6,2},{8,12},{10,14},{12,8},{14,10},{16,20},{18,... | collective-permute-start | bytes 1572872 | tf_op jit(solution)/shard_map/ppermute | solution.py:276
  6.7 2.6 %collective-permute-start.3 = (bf16[1024,256]{1,0:T(8,128)(2,1)S(1)}, bf16[1024,256]{1,0:T(8,128)(2,1)S(1)}, u32[]{:S(2)}, u32[]{:S(2)}) collective-permute-start(bf16[1024,256]{1,0:T(8,128)(2,1)S(1)} %get-tuple-element.25.refs_0_), channel_id=1, source_target_pairs={{0,16},{2,18},{4,20},{6,22},{8,24},{10,26},{12,28},{14,30},{16,0},... | collective-permute-start | bytes 1572872 | tf_op jit(solution)/shard_map/ppermute | solution.py:268
  9.3 0.4 collective-permute-start.1
  9.7 18.1 %collective-permute-done.5.refs_0_ = bf16[1024,256]{1,0:T(8,128)(2,1)S(1)} collective-permute-done((bf16[1024,256]{1,0:T(8,128)(2,1)S(1)}, bf16[1024,256]{1,0:T(8,128)(2,1)S(1)}, u32[]{:S(2)}, u32[]{:S(2)}) %collective-permute-start.5) | collective-permute-done | bytes 524320 | tf_op jit(solution)/shard_map/ppermute | solution.py:265
  27.8 0.0 collective-permute-done.6.refs_1_
  27.8 0.0 copy-start.2
  27.8 3.1 %collective-permute-start.7 = (bf16[1024,256]{1,0:T(8,128)(2,1)S(1)}, bf16[1024,256]{1,0:T(8,128)(2,1)S(1)}, u32[]{:S(2)}, u32[]{:S(2)}) collective-permute-start(bf16[1024,256]{1,0:T(8,128)(2,1)S(1)} %after.5.refs_2_), channel_id=1, source_target_pairs={{0,4},{2,6},{4,0},{6,2},{8,12},{10,14},{12,8},{14,10},{16,20},{18,... | collective-permute-start | bytes 1572872 | tf_op jit(solution)/shard_map/ppermute | solution.py:276
  30.9 1.2 collective-permute-done.3.refs_1_.refs_4_
  32.1 3.3 %collective-permute-start.4 = (bf16[1024,256]{1,0:T(8,128)(2,1)S(1)}, bf16[1024,256]{1,0:T(8,128)(2,1)S(1)}, u32[]{:S(2)}, u32[]{:S(2)}) collective-permute-start(bf16[1024,256]{1,0:T(8,128)(2,1)S(1)} %after.4), channel_id=1, source_target_pairs={{0,24},{2,26},{4,28},{6,30},{8,16},{10,18},{12,20},{14,22},{16,8},... | collective-permute-start | bytes 1572872 | tf_op jit(solution)/shard_map/ppermute | solution.py:272
  35.3 0.0 collective-permute-start.8
  35.3 1.5 %collective-permute-start = (bf16[128,2048]{1,0:T(8,128)(2,1)}, bf16[128,2048]{1,0:T(8,128)(2,1)S(1)}, u32[]{:S(2)}, u32[]{:S(2)}) collective-permute-start(bf16[128,2048]{1,0:T(8,128)(2,1)} %refs_0_.1), channel_id=1, source_target_pairs={{0,1},{1,0},{2,3},{3,2},{4,5},{5,4},{6,7},{7,6},{8,9},{9,8},{10,11... | collective-permute-start | bytes 1572872 | tf_op jit(solution)/shard_map/ppermute | solution.py:306
  36.8 3.3 %collective-permute-done.1.refs_2_ = bf16[128,2048]{1,0:T(8,128)(2,1)S(1)} collective-permute-done((bf16[128,2048]{1,0:T(8,128)(2,1)}, bf16[128,2048]{1,0:T(8,128)(2,1)S(1)}, u32[]{:S(2)}, u32[]{:S(2)}) %collective-permute-start.1) | collective-permute-done | bytes 524320 | tf_op jit(solution)/shard_map/ppermute | solution.py:265
  40.1 1.5 %collective-permute-start.2 = (bf16[128,2048]{1,0:T(8,128)(2,1)S(1)}, bf16[128,2048]{1,0:T(8,128)(2,1)S(1)}, u32[]{:S(2)}, u32[]{:S(2)}) collective-permute-start(bf16[128,2048]{1,0:T(8,128)(2,1)S(1)} %collective-permute-done.1.refs_2_), channel_id=1, source_target_pairs={{0,1},{1,0},{2,3},{3,2},{4,5},{5,4},{6,7},{7,6},{8,9},{9,8},{10,11... | collective-permute-start | bytes 1572872 | tf_op jit(solution)/shard_map/ppermute | solution.py:306
  41.7 0.0 copy-start.4
  41.7 2.1 %collective-permute-done.7.refs_1_.refs_3_ = bf16[1024,256]{1,0:T(8,128)(2,1)S(1)} collective-permute-done((bf16[1024,256]{1,0:T(8,128)(2,1)S(1)}, bf16[1024,256]{1,0:T(8,128)(2,1)S(1)}, u32[]{:S(2)}, u32[]{:S(2)}) %collective-permute-start.7) | collective-permute-done | bytes 524320 | tf_op jit(solution)/shard_map/ppermute | solution.py:276
  43.7 0.4 collective-permute-start.10
  44.1 10.1 %collective-permute-done.4.refs_0_ = bf16[1024,256]{1,0:T(8,128)(2,1)S(1)} collective-permute-done((bf16[1024,256]{1,0:T(8,128)(2,1)S(1)}, bf16[1024,256]{1,0:T(8,128)(2,1)S(1)}, u32[]{:S(2)}, u32[]{:S(2)}) %collective-permute-start.4) | collective-permute-done | bytes 524320 | tf_op jit(solution)/shard_map/ppermute | solution.py:272
  54.2 0.0 collective-permute-done.8.refs_2_.refs_0_.refs_5_
  54.2 1.6 %collective-permute-start.9 = (bf16[1024,256]{1,0:T(8,128)(2,1)S(1)}, bf16[1024,256]{1,0:T(8,128)(2,1)S(1)}, u32[]{:S(2)}, u32[]{:S(2)}) collective-permute-start(bf16[1024,256]{1,0:T(8,128)(2,1)S(1)} %after.6.refs_6_), channel_id=1, source_target_pairs={{0,4},{2,6},{4,0},{6,2},{8,12},{10,14},{12,8},{14,10},{16,20},{18,... | collective-permute-start | bytes 1572872 | tf_op jit(solution)/shard_map/ppermute | solution.py:276
  55.8 0.2 code_input.1
  56.1 0.9 convert_element_type.37
  57.0 0.0 collective-permute-done.refs_1_
  57.0 0.6 collective-permute-done.2.refs_3_
  57.6 2.3 %pick_features.1 = (bf16[256,2048]{1,0:T(8,128)(2,1)S(1)}, bf16[256,2048]{1,0:T(8,128)(2,1)}) custom-call(s32[1]{0:T(128)} %bitcast.3.core_ref, bf16[128,2048]{1,0:T(8,128)(2,1)} %refs_0_.1, bf16[128,2048]{1,0:T(8,128)(2,1)S(1)} %collective-permute-done.refs_1_, bf16[128,2048]{1,0:T(8,128)(2,1)S(1)} %collective-permute-done.1.refs_2_, ...), custom_call_target="tpu_custom_call" | custom-call | bytes 4194304 | tf_op jit(solution)/shard_map/pick_features/pallas_call | solution.py:309
  59.8 1.0 copy-done.12
  60.8 0.7 fusion.18.refs_3_
  61.5 2.6 %collective-permute-done.10.refs_2_.far_gate_ref = f32[128,1024]{1,0:T(8,128)S(1)} collective-permute-done((f32[128,1024]{1,0:T(8,128)S(1)}, f32[128,1024]{1,0:T(8,128)S(1)}, u32[]{:S(2)}, u32[]{:S(2)}) %collective-permute-start.10) | collective-permute-done | bytes 524320 | tf_op jit(solution)/shard_map/ppermute | solution.py:265
  64.1 1.8 %collective-permute-done.9.refs_1_.refs_7_ = bf16[1024,256]{1,0:T(8,128)(2,1)S(1)} collective-permute-done((bf16[1024,256]{1,0:T(8,128)(2,1)S(1)}, bf16[1024,256]{1,0:T(8,128)(2,1)S(1)}, u32[]{:S(2)}, u32[]{:S(2)}) %collective-permute-start.9) | collective-permute-done | bytes 524320 | tf_op jit(solution)/shard_map/ppermute | solution.py:276
  66.0 0.8 copy-done.10
  66.7 0.0 collective-permute-start.11
  66.7 3.8 %all-to-all-start.1 = ((f16[16,144,128]{2,1,0:T(8,128)(2,1)}), f16[16,144,128]{2,1,0:T(8,128)(2,1)S(1)}, u32[]{:S(2)}, u32[]{:S(2)}) async-start(f16[16,144,128]{2,1,0:T(8,128)(2,1)} %convert_element_type.37), calls=%async_computation.1 | async-start | bytes 1179648 | tf_op jit(solution)/shard_map/all_to_all | solution.py:514
  70.5 0.0 collective-permute-done.11.theirs_ref
  70.5 6.0 %add_shares.1 = (f32[256,1024]{1,0:T(8,128)}, f32[256,1024]{1,0:T(8,128)}) custom-call(s32[1]{0:T(128)} %bitcast.1.ctx_ref, s32[1]{0:T(128)} %bitcast.2.ch_ref, bf16[256,2048]{1,0:T(8,128)(2,1)} %copy-done.12, bf16[256,2048]{1,0:T(8,128)(2,1)} %collective-permute-done.11.theirs_ref, bf16[1024,256]{1,0:T(8,128)(2,1)} %copy-done.15, ...), custom_call_target="tpu_custom_call" | custom-call | flops 2147483648 | bytes 10485760 | tf_op jit(solution)/shard_map/add_shares/pallas_call | solution.py:428
  76.5 0.5 collective-permute-start.12
  77.0 2.5 %collective-permute-done.12.arrived_ref = f32[256,1024]{1,0:T(8,128)S(1)} collective-permute-done((f32[256,1024]{1,0:T(8,128)}, f32[256,1024]{1,0:T(8,128)S(1)}, u32[]{:S(2)}, u32[]{:S(2)}) %collective-permute-start.12) | collective-permute-done | bytes 1048608 | tf_op jit(solution)/shard_map/ppermute | solution.py:262
  79.5 1.2 copy-done.5
  80.7 1.9 %seq_grad.1 = (f32[8,272,128]{2,1,0:T(8,128)S(1)}, f32[128,1024]{1,0:T(8,128)}, f32[128,1024]{1,0:T(8,128)}) custom-call(s32[1]{0:T(128)} %bitcast.p_ref, f32[256,1024]{1,0:T(8,128)S(1)} %copy-done.5, f32[256,1024]{1,0:T(8,128)S(1)} %collective-permute-done.12.arrived_ref, f32[128,2048]{1,0:T(8,128)S(1)} %copy-done.2, ...), custom_call_target="tpu_custom_call" | custom-call | flops 524288 | bytes 6291456 | tf_op jit(solution)/shard_map/seq_grad/pallas_call | solution.py:346
  82.6 0.9 convert_element_type.40
  83.5 2.6 %all-to-all-done.1 = f16[16,144,128]{2,1,0:T(8,128)(2,1)S(1)} async-done(((f16[16,144,128]{2,1,0:T(8,128)(2,1)}), f16[16,144,128]{2,1,0:T(8,128)(2,1)S(1)}, u32[]{:S(2)}, u32[]{:S(2)}) %all-to-all-start.1) | async-done | bytes 589856 | tf_op jit(solution)/shard_map/all_to_all | solution.py:514
  86.1 3.9 %all-to-all-start = ((f16[8,272,128]{2,1,0:T(8,128)(2,1)}), f16[8,272,128]{2,1,0:T(8,128)(2,1)S(1)}, u32[]{:S(2)}, u32[]{:S(2)}) async-start(f16[8,272,128]{2,1,0:T(8,128)(2,1)} %convert_element_type.40), calls=%async_computation | async-start | bytes 1114112 | tf_op jit(solution)/shard_map/all_to_all | solution.py:514
  90.0 3.0 %toeplitz.1.t_ref = bf16[8,256,2176]{2,1,0:T(8,128)(2,1)S(1)} custom-call(f32[8,1,2176]{2,1,0:T(1,128)S(1)} %broadcast_in_dim.3.filter_ref), custom_call_target="tpu_custom_call" | custom-call | flops 8912896 | bytes 8982528 | tf_op jit(solution)/shard_map/toeplitz/pallas_call | solution.py:38
  93.0 3.5 %copy-done.1 = bf16[8,256,2176]{2,1,0:T(8,128)(2,1)} copy-done((bf16[8,256,2176]{2,1,0:T(8,128)(2,1)}, bf16[8,256,2176]{2,1,0:T(8,128)(2,1)S(1)}, u32[]{:S(2)}) %copy-start.1) | copy-done | bytes 8912920
  96.5 0.2 fusion.2.x_ref
  96.7 3.2 %stack_input.1.left_ref = bf16[8,256,256]{2,1,0:T(8,128)(2,1)S(1)} custom-call(f32[16,128,128]{2,1,0:T(8,128)S(1)} %fusion.2.x_ref), custom_call_target="tpu_custom_call" | custom-call | flops 2097152 | bytes 2097152 | tf_op jit(solution)/shard_map/stack_input/pallas_call | solution.py:77
  100.0 1.2 collective-permute-start.13
  101.2 5.0 %all-to-all-done = f16[8,272,128]{2,1,0:T(8,128)(2,1)S(1)} async-done(((f16[8,272,128]{2,1,0:T(8,128)(2,1)}), f16[8,272,128]{2,1,0:T(8,128)(2,1)S(1)}, u32[]{:S(2)}, u32[]{:S(2)}) %all-to-all-start) | async-done | bytes 557088 | tf_op jit(solution)/shard_map/all_to_all | solution.py:514
  106.1 0.1 convert_element_type.41.s_ref
  106.2 11.3 %convolve.1 = f32[16,144,128]{2,1,0:T(8,128)S(1)} custom-call(f32[8,272,128]{2,1,0:T(8,128)S(1)} %convert_element_type.41.s_ref, bf16[8,256,256]{2,1,0:T(8,128)(2,1)S(1)} %stack_input.1.left_ref, bf16[8,256,2176]{2,1,0:T(8,128)(2,1)} %copy-done.1), custom_call_target="tpu_custom_call" | custom-call | flops 7985954816 | bytes 12058624 | tf_op jit(solution)/shard_map/convolve/pallas_call | solution.py:201
  117.5 0.9 convert_element_type.44
  118.4 3.6 %all-to-all-start.2 = ((f16[16,144,128]{2,1,0:T(8,128)(2,1)}), f16[16,144,128]{2,1,0:T(8,128)(2,1)S(1)}, u32[]{:S(2)}, u32[]{:S(2)}) async-start(f16[16,144,128]{2,1,0:T(8,128)(2,1)} %convert_element_type.44), calls=%async_computation.2 | async-start | bytes 1179648 | tf_op jit(solution)/shard_map/all_to_all | solution.py:514
  122.0 0.0 copy-start.13
  122.0 0.0 collective-permute-done.13
  122.0 1.2 broadcast_select_fusion.1
  123.3 0.1 copy-done.13
  123.4 1.1 maximum_multiply_fusion
  124.5 13.0 %all-to-all-done.2 = f16[16,144,128]{2,1,0:T(8,128)(2,1)S(1)} async-done(((f16[16,144,128]{2,1,0:T(8,128)(2,1)}), f16[16,144,128]{2,1,0:T(8,128)(2,1)S(1)}, u32[]{:S(2)}, u32[]{:S(2)}) %all-to-all-start.2) | async-done | bytes 589856 | tf_op jit(solution)/shard_map/all_to_all | solution.py:514
  137.6 0.6 copy.22
  138.2 0.2 fusion.5
  138.4 0.1 copy.20
  138.5 0.3 copy.21
  138.9 1.3 copy.23
  (34 shorter events, 0.2 us)
Async XLA Ops:
  0.6 89.3 %copy-start = (f32[128,2048]{1,0:T(8,128)S(1)}, f32[128,2048]{1,0:T(8,128)}, u32[]{:S(2)}) copy-start(f32[128,2048]{1,0:T(8,128)} %param.11) | copy-start | bytes 3145732
  2.1 30.0 %copy-start.15 = (bf16[1024,256]{1,0:T(8,128)(2,1)}, bf16[1024,256]{1,0:T(8,128)(2,1)S(1)}, u32[]{:S(2)}) copy-start(bf16[1024,256]{1,0:T(8,128)(2,1)S(1)} %get-tuple-element.25.refs_0_) | copy-start | bytes 1572868
  2.1 25.7 %collective-permute-start.5 = (bf16[1024,256]{1,0:T(8,128)(2,1)S(1)}, bf16[1024,256]{1,0:T(8,128)(2,1)S(1)}, u32[]{:S(2)}, u32[]{:S(2)}) collective-permute-start(bf16[1024,256]{1,0:T(8,128)(2,1)S(1)} %get-tuple-element.26.refs_0_), channel_id=1, source_target_pairs={{0,8},{2,10},{4,12},{6,14},{8,0},{10,2},{12,4},{14,6},{16,24},{18,... | collective-permute-start | bytes 1572872 | tf_op jit(solution)/shard_map/ppermute | solution.py:265
  5.2 22.6 %collective-permute-start.6 = (bf16[1024,256]{1,0:T(8,128)(2,1)S(1)}, bf16[1024,256]{1,0:T(8,128)(2,1)S(1)}, u32[]{:S(2)}, u32[]{:S(2)}) collective-permute-start(bf16[1024,256]{1,0:T(8,128)(2,1)S(1)} %get-tuple-element.25.refs_0_), channel_id=1, source_target_pairs={{0,4},{2,6},{4,0},{6,2},{8,12},{10,14},{12,8},{14,10},{16,20},{18,... | collective-permute-start | bytes 1572872 | tf_op jit(solution)/shard_map/ppermute | solution.py:276
  6.7 25.4 %collective-permute-start.3 = (bf16[1024,256]{1,0:T(8,128)(2,1)S(1)}, bf16[1024,256]{1,0:T(8,128)(2,1)S(1)}, u32[]{:S(2)}, u32[]{:S(2)}) collective-permute-start(bf16[1024,256]{1,0:T(8,128)(2,1)S(1)} %get-tuple-element.25.refs_0_), channel_id=1, source_target_pairs={{0,16},{2,18},{4,20},{6,22},{8,24},{10,26},{12,28},{14,30},{16,0},... | collective-permute-start | bytes 1572872 | tf_op jit(solution)/shard_map/ppermute | solution.py:268
  9.3 30.8 %collective-permute-start.1 = (bf16[128,2048]{1,0:T(8,128)(2,1)}, bf16[128,2048]{1,0:T(8,128)(2,1)S(1)}, u32[]{:S(2)}, u32[]{:S(2)}) collective-permute-start(bf16[128,2048]{1,0:T(8,128)(2,1)} %refs_0_.1), channel_id=1, source_target_pairs={{0,8},{2,10},{4,12},{6,14},{8,0},{10,2},{12,4},{14,6},{16,24},{18,... | collective-permute-start | bytes 1572872 | tf_op jit(solution)/shard_map/ppermute | solution.py:265
  27.8 4.3 %copy-start.6 = (bf16[1024,256]{1,0:T(8,128)(2,1)}, bf16[1024,256]{1,0:T(8,128)(2,1)S(1)}, u32[]{:S(2)}) copy-start(bf16[1024,256]{1,0:T(8,128)(2,1)S(1)} %collective-permute-done.6.refs_1_) | copy-start | bytes 1572868
  27.8 13.9 %copy-start.8 = (bf16[1024,256]{1,0:T(8,128)(2,1)}, bf16[1024,256]{1,0:T(8,128)(2,1)S(1)}, u32[]{:S(2)}) copy-start(bf16[1024,256]{1,0:T(8,128)(2,1)S(1)} %after.5.refs_2_) | copy-start | bytes 1572868
  27.8 13.8 %copy-start.2 = (f32[128,2048]{1,0:T(8,128)S(1)}, f32[128,2048]{1,0:T(8,128)}, u32[]{:S(2)}) copy-start(f32[128,2048]{1,0:T(8,128)} %gate_ref.1) | copy-start | bytes 3145732
  27.8 15.9 %collective-permute-start.7 = (bf16[1024,256]{1,0:T(8,128)(2,1)S(1)}, bf16[1024,256]{1,0:T(8,128)(2,1)S(1)}, u32[]{:S(2)}, u32[]{:S(2)}) collective-permute-start(bf16[1024,256]{1,0:T(8,128)(2,1)S(1)} %after.5.refs_2_), channel_id=1, source_target_pairs={{0,4},{2,6},{4,0},{6,2},{8,12},{10,14},{12,8},{14,10},{16,20},{18,... | collective-permute-start | bytes 1572872 | tf_op jit(solution)/shard_map/ppermute | solution.py:276
  32.1 9.6 %copy-start.7 = (bf16[1024,256]{1,0:T(8,128)(2,1)}, bf16[1024,256]{1,0:T(8,128)(2,1)S(1)}, u32[]{:S(2)}) copy-start(bf16[1024,256]{1,0:T(8,128)(2,1)S(1)} %collective-permute-done.3.refs_1_.refs_4_) | copy-start | bytes 1572868
  32.1 22.1 %collective-permute-start.4 = (bf16[1024,256]{1,0:T(8,128)(2,1)S(1)}, bf16[1024,256]{1,0:T(8,128)(2,1)S(1)}, u32[]{:S(2)}, u32[]{:S(2)}) collective-permute-start(bf16[1024,256]{1,0:T(8,128)(2,1)S(1)} %after.4), channel_id=1, source_target_pairs={{0,24},{2,26},{4,28},{6,30},{8,16},{10,18},{12,20},{14,22},{16,8},... | collective-permute-start | bytes 1572872 | tf_op jit(solution)/shard_map/ppermute | solution.py:272
  35.3 18.9 %collective-permute-start.8 = (bf16[1024,256]{1,0:T(8,128)(2,1)S(1)}, bf16[1024,256]{1,0:T(8,128)(2,1)S(1)}, u32[]{:S(2)}, u32[]{:S(2)}) collective-permute-start(bf16[1024,256]{1,0:T(8,128)(2,1)S(1)} %collective-permute-done.3.refs_1_.refs_4_), channel_id=1, source_target_pairs={{0,4},{2,6},{4,0},{6,2},{8,12},{10,14},{12,8},{14,10},{16,20},{18,... | collective-permute-start | bytes 1572872 | tf_op jit(solution)/shard_map/ppermute | solution.py:276
  35.3 21.6 %collective-permute-start = (bf16[128,2048]{1,0:T(8,128)(2,1)}, bf16[128,2048]{1,0:T(8,128)(2,1)S(1)}, u32[]{:S(2)}, u32[]{:S(2)}) collective-permute-start(bf16[128,2048]{1,0:T(8,128)(2,1)} %refs_0_.1), channel_id=1, source_target_pairs={{0,1},{1,0},{2,3},{3,2},{4,5},{5,4},{6,7},{7,6},{8,9},{9,8},{10,11... | collective-permute-start | bytes 1572872 | tf_op jit(solution)/shard_map/ppermute | solution.py:306
  40.1 17.5 %collective-permute-start.2 = (bf16[128,2048]{1,0:T(8,128)(2,1)S(1)}, bf16[128,2048]{1,0:T(8,128)(2,1)S(1)}, u32[]{:S(2)}, u32[]{:S(2)}) collective-permute-start(bf16[128,2048]{1,0:T(8,128)(2,1)S(1)} %collective-permute-done.1.refs_2_), channel_id=1, source_target_pairs={{0,1},{1,0},{2,3},{3,2},{4,5},{5,4},{6,7},{7,6},{8,9},{9,8},{10,11... | collective-permute-start | bytes 1572872 | tf_op jit(solution)/shard_map/ppermute | solution.py:306
  41.7 14.2 %copy-start.4 = (f32[128,2048]{1,0:T(8,128)S(1)}, f32[128,2048]{1,0:T(8,128)}, u32[]{:S(2)}) copy-start(f32[128,2048]{1,0:T(8,128)} %x_ref.1) | copy-start | bytes 3145732
  43.7 10.5 %copy-start.9 = (bf16[1024,256]{1,0:T(8,128)(2,1)}, bf16[1024,256]{1,0:T(8,128)(2,1)S(1)}, u32[]{:S(2)}) copy-start(bf16[1024,256]{1,0:T(8,128)(2,1)S(1)} %collective-permute-done.7.refs_1_.refs_3_) | copy-start | bytes 1572868
  43.7 20.4 %collective-permute-start.10 = (f32[128,1024]{1,0:T(8,128)S(1)}, f32[128,1024]{1,0:T(8,128)S(1)}, u32[]{:S(2)}, u32[]{:S(2)}) collective-permute-start(f32[128,1024]{1,0:T(8,128)S(1)} %constant_dynamic-slice_fusion.1), channel_id=1, source_target_pairs={{0,8},{2,10},{4,12},{6,14},{8,0},{10,2},{12,4},{14,6},{16,24},{18,... | collective-permute-start | bytes 1572872 | tf_op jit(solution)/shard_map/ppermute | solution.py:265
  54.2 1.8 %copy-start.3 = (bf16[1024,256]{1,0:T(8,128)(2,1)}, bf16[1024,256]{1,0:T(8,128)(2,1)S(1)}, u32[]{:S(2)}) copy-start(bf16[1024,256]{1,0:T(8,128)(2,1)S(1)} %collective-permute-done.8.refs_2_.refs_0_.refs_5_) | copy-start | bytes 1572868
  54.2 1.8 %copy-start.11 = (bf16[1024,256]{1,0:T(8,128)(2,1)}, bf16[1024,256]{1,0:T(8,128)(2,1)S(1)}, u32[]{:S(2)}) copy-start(bf16[1024,256]{1,0:T(8,128)(2,1)S(1)} %after.6.refs_6_) | copy-start | bytes 1572868
  54.2 11.7 %collective-permute-start.9 = (bf16[1024,256]{1,0:T(8,128)(2,1)S(1)}, bf16[1024,256]{1,0:T(8,128)(2,1)S(1)}, u32[]{:S(2)}, u32[]{:S(2)}) collective-permute-start(bf16[1024,256]{1,0:T(8,128)(2,1)S(1)} %after.6.refs_6_), channel_id=1, source_target_pairs={{0,4},{2,6},{4,0},{6,2},{8,12},{10,14},{12,8},{14,10},{16,20},{18,... | collective-permute-start | bytes 1572872 | tf_op jit(solution)/shard_map/ppermute | solution.py:276
  59.8 1.0 copy-start.12
  65.9 0.8 copy-start.10
  66.7 3.8 %collective-permute-start.11 = (bf16[256,2048]{1,0:T(8,128)(2,1)}, bf16[256,2048]{1,0:T(8,128)(2,1)}, u32[]{:S(2)}, u32[]{:S(2)}) collective-permute-start(bf16[256,2048]{1,0:T(8,128)(2,1)} %after.7), channel_id=1, source_target_pairs={{0,2},{2,0},{4,6},{6,4},{8,10},{10,8},{12,14},{14,12},{16,18},{18,... | collective-permute-start | bytes 3145736 | tf_op jit(solution)/shard_map/ppermute | solution.py:262
  66.7 19.4 %all-to-all-start.1 = ((f16[16,144,128]{2,1,0:T(8,128)(2,1)}), f16[16,144,128]{2,1,0:T(8,128)(2,1)S(1)}, u32[]{:S(2)}, u32[]{:S(2)}) async-start(f16[16,144,128]{2,1,0:T(8,128)(2,1)} %convert_element_type.37), calls=%async_computation.1 | async-start | bytes 1179648 | tf_op jit(solution)/shard_map/all_to_all | solution.py:514
  76.5 3.0 %collective-permute-start.12 = (f32[256,1024]{1,0:T(8,128)}, f32[256,1024]{1,0:T(8,128)S(1)}, u32[]{:S(2)}, u32[]{:S(2)}) collective-permute-start(f32[256,1024]{1,0:T(8,128)} %get-tuple-element.13), channel_id=1, source_target_pairs={{0,2},{2,0},{4,6},{6,4},{8,10},{10,8},{12,14},{14,12},{16,18},{18,... | collective-permute-start | bytes 3145736 | tf_op jit(solution)/shard_map/ppermute | solution.py:262
  79.5 1.2 copy-start.5
  86.1 20.0 %all-to-all-start = ((f16[8,272,128]{2,1,0:T(8,128)(2,1)}), f16[8,272,128]{2,1,0:T(8,128)(2,1)S(1)}, u32[]{:S(2)}, u32[]{:S(2)}) async-start(f16[8,272,128]{2,1,0:T(8,128)(2,1)} %convert_element_type.40), calls=%async_computation | async-start | bytes 1114112 | tf_op jit(solution)/shard_map/all_to_all | solution.py:514
  93.0 3.5 %copy-start.1 = (bf16[8,256,2176]{2,1,0:T(8,128)(2,1)}, bf16[8,256,2176]{2,1,0:T(8,128)(2,1)S(1)}, u32[]{:S(2)}) copy-start(bf16[8,256,2176]{2,1,0:T(8,128)(2,1)S(1)} %toeplitz.1.t_ref) | copy-start | bytes 26738692
  100.0 22.1 %collective-permute-start.13 = (f32[128,1024]{1,0:T(8,128)}, f32[128,1024]{1,0:T(8,128)}, u32[]{:S(2)}, u32[]{:S(2)}) collective-permute-start(f32[128,1024]{1,0:T(8,128)} %get-tuple-element.16), channel_id=1, source_target_pairs={{0,8},{2,10},{4,12},{6,14},{8,0},{10,2},{12,4},{14,6},{16,24},{18,... | collective-permute-start | bytes 1572872 | tf_op jit(solution)/shard_map/ppermute | solution.py:265
  117.5 4.5 %copy-start.14 = (f32[128,1024]{1,0:T(8,128)S(1)}, f32[128,1024]{1,0:T(8,128)}, u32[]{:S(2)}) copy-start(f32[128,1024]{1,0:T(8,128)} %get-tuple-element.15) | copy-start | bytes 1572868
  118.4 19.1 %all-to-all-start.2 = ((f16[16,144,128]{2,1,0:T(8,128)(2,1)}), f16[16,144,128]{2,1,0:T(8,128)(2,1)S(1)}, u32[]{:S(2)}, u32[]{:S(2)}) async-start(f16[16,144,128]{2,1,0:T(8,128)(2,1)} %convert_element_type.44), calls=%async_computation.2 | async-start | bytes 1179648 | tf_op jit(solution)/shard_map/all_to_all | solution.py:514
  122.0 1.4 copy-start.13
